TPU v7x, 256 devices: a whole 4x4x8 slice. The times are simulated.
256 devices in a mesh: img: 16 (over z_lo, y), tile: 16 (over x, z_hi, core).
Axes of the slice: x: 4, y: 4, z: 8 (z_hi: 2, z_lo: 4; z = z_hi * 4 + z_lo), core: 2. Of those that a mesh axis runs over, the one named last changes fastest.
Arguments:
- feature_map: bfloat16 [16, 256, 256, 256], P('img', 'tile'), may hold values from -0.0234375 to 0.0234375
- cotangent: bfloat16 [16, 256, 256, 256], P('img', 'tile'), may hold values from -6 to 6
- style: float32 [16, 256], P('img'), may hold values from 0.3 to 3
- bank: bfloat16 [8, 256, 9, 256], P(None, 'tile'), may hold values from -0.125 to 0.125
- selection: int32 [16, 3], P('img'), may hold values from 0 to 7, all different within a row
Outputs:
- input_grad: bfloat16 [16, 256, 256, 256], P('img', 'tile')
- style_grad: float32 [16, 256], P('img')
- bank_grad: float32 [8, 256, 9, 256], P(None, 'tile')
Inputs may be any that keep to these rules, and one draw needn't show every extreme that they name: `selection`: each row names 3 different banks, and every bank is named by some image.
All inputs are finite; a program needn't handle non-finite values.
Results may differ from a plain program's by a relative error of at most 0.012.
Values may be sent and summed in bfloat16 or wider, within the bound.
No kernel may reach another device: no remote copies, remote signals or barrier semaphores. Data moves between devices by JAX's collectives and lax.ppermute only.
A program may use at most 128 MiB of HBM per device.

v0:
```python
import jax
import jax.numpy as jnp
from jax import lax
from jax.sharding import PartitionSpec as P

epsilon = 1e-06


def padded_2(block, sides, width):
    for axis, dim in sides:
        count = lax.axis_size(axis)
        forward = [(i, i + 1) for i in range(count - 1)]
        backward = [(target, source) for source, target in forward]
        low = lax.ppermute(
            lax.slice_in_dim(block, block.shape[dim] - width, None, axis=dim), axis, forward
        )
        high = lax.ppermute(lax.slice_in_dim(block, 0, width, axis=dim), axis, backward)
        block = jnp.concatenate([low, block, high], axis=dim)
    return block


def bank_mixing(selection, bank_count):
    pick_count = selection.shape[1]
    ranks = jnp.arange(pick_count).astype(jnp.float32)
    weights = (pick_count - ranks) / (pick_count * (pick_count + 1) / 2.0)
    onehot = (
        selection[:, :, None] == jnp.arange(bank_count, dtype=jnp.int32)[None, None, :]
    ).astype(jnp.float32)
    return jnp.sum(weights[None, :, None] * onehot, axis=1)


def local(feature_map, cotangent, style, bank, selection):
    batch_size, row_count, col_count, channels = feature_map.shape
    mixing = bank_mixing(selection, bank.shape[0])
    kernel = jnp.einsum("bk,kotc->botc", mixing, bank.astype(jnp.float32))
    modded = kernel * style[:, None, None, :]
    demod_scale = lax.rsqrt(jnp.sum(modded * modded, axis=(2, 3)) + epsilon)
    final_kernel = (modded * demod_scale[:, :, None, None]).astype(jnp.bfloat16)
    padded = padded_2(cotangent, (("tile", 1),), 1)
    padded = jnp.pad(padded, ((0, 0), (0, 0), (1, 1), (0, 0)))
    pieces = []
    for shift_row in (-1, 0, 1):
        for shift_col in (-1, 0, 1):
            moved = padded[
                :,
                1 - shift_row : 1 - shift_row + row_count,
                1 - shift_col : 1 - shift_col + col_count,
                :,
            ]
            pieces.append(moved.reshape(batch_size, row_count * col_count, channels))
    shifted = jnp.stack(pieces, axis=0)
    flat_in = feature_map.reshape(batch_size, row_count * col_count, channels)
    gathered = lax.all_gather(final_kernel, "tile", axis=1, tiled=True)
    data_grad = jnp.einsum("tbpo,boti->bpi", shifted, gathered, preferred_element_type=jnp.float32)
    input_grad = data_grad.astype(jnp.bfloat16).reshape(batch_size, row_count, col_count, channels)
    summed = lax.psum_scatter(
        jnp.einsum("tbpo,bpi->obti", shifted, flat_in, preferred_element_type=jnp.float32),
        "tile",
        scatter_dimension=0,
        tiled=True,
    )
    grad = jnp.moveaxis(summed, 0, 1)
    curvature = jnp.sum(grad * modded, axis=(2, 3))
    modded_grad = (
        demod_scale[:, :, None, None] * grad
        - (demod_scale**3)[:, :, None, None] * modded * curvature[:, :, None, None]
    )
    style_part = jnp.sum(modded_grad * kernel, axis=(1, 2))
    style_grad = lax.psum(style_part, "tile")
    kernel_grad = modded_grad * style[:, None, None, :]
    bank_part = jnp.einsum("bk,botc->kotc", mixing, kernel_grad)
    bank_grad = lax.psum(bank_part, "img")
    return (input_grad, style_grad, bank_grad)


def solution(mesh):
    in_specs = (
        P("img", "tile", None, None),
        P("img", "tile", None, None),
        P("img", None),
        P(None, "tile", None, None),
        P("img", None),
    )
    out_specs = (P("img", "tile", None, None), P("img", None), P(None, "tile", None, None))
    return jax.shard_map(local, mesh=mesh, in_specs=in_specs, out_specs=out_specs, check_vma=False)
```

profile of v0, /device:TPU:8, one launch (start us, length us, event | category | flops | bytes accessed | tf_op | source)
XLA Modules:
  0.0 375.4 jit_solution(10214314733803263802)
XLA Ops:
  7.2 1.1 fusion.29
  8.4 1.7 collective-permute-start
  10.1 1.3 collective-permute-start.1
  11.4 8.9 %collective-permute-done.1 = bf16[1,1,256,256]{3,2,1,0:T(8,128)(2,1)S(1)} collective-permute-done((bf16[1,1,256,256]{3,2,1,0:T(8,128)(2,1)S(1)}, bf16[1,1,256,256]{3,2,1,0:T(8,128)(2,1)S(1)}, u32[]{:S(2)}, u32[]{:S(2)}) %collective-permute-start.1) | collective-permute-done | bytes 131104 | tf_op jit(solution)/shard_map/ppermute | solution.py:17
  20.3 2.1 fusion.15
  22.4 4.3 %fusion.28 = (bf16[1,16,256,256]{3,2,1,0:T(8,128)(2,1)S(1)}, bf16[1,16,256,256]{3,2,1,0:T(8,128)(2,1)S(1)}, bf16[1,16,256,256]{3,2,1,0:T(8,128)(2,1)S(1)}, bf16[...) fusion(bf16[1,18,258,256]{3,2,1,0:T(8,128)(2,1)S(1)} %fusion.15), kind=kLoop, calls=%fused_computation.45 | loop fusion | bytes 25165824 | tf_op jit(solution)/shard_map/slice | solution.py:44
  26.7 1.5 constant_dynamic-update-slice_fusion.8
  28.2 0.9 copy-done.1
  29.1 0.4 pad_maximum_fusion
  29.4 1.4 constant_dynamic-update-slice_fusion.7
  30.9 1.5 constant_dynamic-update-slice_fusion.6
  32.3 1.5 constant_dynamic-update-slice_fusion.5
  33.8 1.5 constant_dynamic-update-slice_fusion.4
  35.3 1.4 constant_dynamic-update-slice_fusion.3
  36.7 1.5 constant_dynamic-update-slice_fusion.2
  38.2 1.5 constant_dynamic-update-slice_fusion.1
  39.7 1.5 constant_dynamic-update-slice_fusion
  41.2 10.4 %fusion.16 = f32[256,1,9,256]{3,0,2,1:T(8,128)} fusion(bf16[4096,256,1]{1,0,2:T(8,128)(2,1)S(1)} %bitcast.81, bf16[9,1,4096,256]{3,2,0,1:T(8,128)(2,1)} %constant_dynamic-update-slice_fusion), kind=kOutput, calls=%fused_computation.16 | convolution fusion | flops 4831838208 | bytes 23330816 | tf_op jit(solution)/shard_map/tbpo,bpi->obti/dot_general | solution.py:57
  51.7 0.6 copy-done.4
  52.2 0.1 fusion.25
  52.3 0.3 copy-done.2
  52.7 0.3 fusion.19
  53.0 94.5 %reduce-scatter.2.cloned.1.call-done = f32[16,1,9,256]{3,0,2,1:T(8,128)} async-done(((f32[256,1,9,256]{3,0,2,1:T(8,128)}), f32[16,1,9,256]{3,0,2,1:T(8,128)}) %reduce-scatter.2.cloned.1.call-update) | async-done | bytes 147472 | tf_op jit(solution)/shard_map/reduce_scatter | solution.py:56
  147.4 1.0 fusion.22
  148.5 1.7 fusion.24
  150.2 0.0 all-reduce.3.cloned.1.call-start
  150.2 46.4 %psum.14 = f32[1,256]{1,0:T(1,128)} all-reduce(f32[1,256]{1,0:T(1,128)S(1)} %bitcast.93), channel_id=1, replica_groups=mesh['img'=16,'tile'=16] {'tile'}, use_global_device_ids=true, to_apply=%region_5.6 | all-reduce | flops 256 | bytes 2048 | tf_op jit(solution)/shard_map/psum | solution.py:69
  196.6 1.2 broadcast_multiply_fusion
  197.8 5.6 %all-gather.3.cloned.1.call-done = bf16[256,9,256]{2,0,1:T(8,128)(2,1)} async-done(((bf16[16,9,256]{2,0,1:T(8,128)(2,1)}), bf16[256,9,256]{2,0,1:T(8,128)(2,1)}) %all-gather.3.cloned.1.call-update) | async-done | bytes 1179664 | tf_op jit(solution)/shard_map/all_gather | solution.py:53
  203.5 10.3 %fusion.7 = bf16[4096,256]{1,0:T(8,128)(2,1)} fusion(bf16[256,9,256]{2,0,1:T(8,128)(2,1)} %all-gather.3.cloned.1.call-done, bf16[9,1,4096,256]{3,2,0,1:T(8,128)(2,1)} %constant_dynamic-update-slice_fusion), kind=kOutput, calls=%fused_computation.7 | convolution fusion | flops 4832886784 | bytes 22151168 | tf_op jit(solution)/shard_map/tbpo,boti->bpi/dot_general | solution.py:54
  213.8 152.7 %all-reduce.3.cloned.1.call-done = f32[8,16,9,256]{3,1,2,0:T(8,128)} async-done(((f32[8,16,9,256]{3,1,2,0:T(8,128)}), f32[8,16,9,256]{3,1,2,0:T(8,128)}) %all-reduce.3.cloned.1.call-update) | async-done | bytes 1179664 | tf_op jit(solution)/shard_map/psum | solution.py:72
  366.5 2.4 copy.39
  (15 shorter events, 0.2 us)
Async XLA Ops:
  7.2 34.0 %copy-start = (bf16[1,16,256,256]{3,2,1,0:T(8,128)(2,1)S(1)}, bf16[1,16,256,256]{3,2,1,0:T(8,128)(2,1)}, u32[]{:S(2)}) copy-start(bf16[1,16,256,256]{3,2,1,0:T(8,128)(2,1)} %param.5) | copy-start | bytes 6291460
  7.2 140.3 %reduce-scatter.2.cloned.1.call-start = ((), (), s32[]{:S(2)}) async-start(), calls=%async_computation.1 | async-start | bytes 2506752 | tf_op jit(solution)/shard_map/reduce_scatter | solution.py:56
  8.4 3.1 collective-permute-start
  10.1 10.2 %collective-permute-start.1 = (bf16[1,1,256,256]{3,2,1,0:T(8,128)(2,1)S(1)}, bf16[1,1,256,256]{3,2,1,0:T(8,128)(2,1)S(1)}, u32[]{:S(2)}, u32[]{:S(2)}) collective-permute-start(bf16[1,1,256,256]{3,2,1,0:T(8,128)(2,1)S(1)} %get-tuple-element.14), channel_id=1, source_target_pairs={{1,0},{2,1},{3,2},{4,3},{5,4},{6,5},{7,6},{8,7},{9,8},{10,9},{11,1... | collective-permute-start | bytes 393224 | tf_op jit(solution)/shard_map/ppermute | solution.py:17
  26.7 2.4 copy-start.1
  51.6 0.7 copy-start.4
  51.6 1.1 copy-start.2
  51.6 95.8 %copy-start.3 = (f32[1,256]{1,0:T(1,128)S(1)}, f32[1,256]{1,0:T(1,128)}, u32[]{:S(2)}) copy-start(f32[1,256]{1,0:T(1,128)} %param.7) | copy-start | bytes 3076
  51.6 151.8 %all-gather.3.cloned.1.call-start = ((), (), s32[]{:S(2)}) async-start(), calls=%async_computation.3 | async-start | bytes 1253376 | tf_op jit(solution)/shard_map/all_gather | solution.py:53
  150.2 216.3 %all-reduce.3.cloned.1.call-start = ((), (), s32[]{:S(2)}) async-start(), calls=%async_computation.2 | async-start | bytes 2359296 | tf_op jit(solution)/shard_map/psum | solution.py:72
Sparse Core Ops, SparseCore 0:
  51.7 95.6 reduce-scatter.1
  150.6 52.8 all-gather.2
  206.7 159.7 all-reduce.2
where the time goes:
time: 376 us; the launch traced here: 375 us
  waiting for transfers between devices  262 us (70%)
  blocking collectives  46.4 us (12%)
  local copies, waits for them, and re-layouts  22.8 us (6%)
  matrix products  21 us (6%)
  between operations  13.8 us (4%)
  other arithmetic  6.48 us (2%)
    psum x1, waiting for transfers between devices, local(): bank_grad = lax.psum(bank_part, 'img')  153 us
    reduce_scatter x1, waiting for transfers between devices, local(): lax.psum_scatter(jnp.einsum('tbpo,bpi->obti', shifted, flat_in, preferred...  94.5 us
    psum x1, blocking collectives, local(): style_grad = lax.psum(style_part, 'tile')  46.4 us
    unnamed x19, local copies, waits for them, and re-layouts  15.9 us
    dot_general x1, matrix products, local(): jnp.einsum('tbpo,bpi->obti', shifted, flat_in, preferred_element_type=jnp...  10.4 us
    dot_general x1, matrix products, local(): jnp.einsum('tbpo,boti->bpi', shifted, gathered, preferred_element_type=jn...  10.3 us
    ppermute x1, waiting for transfers between devices, padded_2(): lax.ppermute(lax.slice_in_dim(block, 0, width, axis=dim), axis, backward)  8.9 us
  transfers between devices with their start and end apart: 5, of which 4 were waited for; matrix products, arithmetic and copies ran while one was open for 3% of the time, Pallas kernels for 0%

commit v1 on v0

v1 whole, which is shorter than its diff:
```python
import functools

import jax
import jax.numpy as jnp
from jax import lax
from jax.experimental import pallas as pl
from jax.experimental.pallas import tpu as pltpu
from jax.sharding import PartitionSpec as P

epsilon = 1e-06
F32 = jnp.float32
BF16 = jnp.bfloat16
VMEM = pl.BlockSpec(memory_space=pltpu.VMEM)
SMEM = pl.BlockSpec(memory_space=pltpu.SMEM)
ANY = pl.BlockSpec(memory_space=pl.ANY)

NX, NZ, NC = 4, 2, 2
NL, NY = 4, 4


def tile_perm(move):
    place = lambda x, z, c: (x * NZ + z) * NC + c
    return [
        (place(x, z, c), place(*move(x, z, c)))
        for x in range(NX)
        for z in range(NZ)
        for c in range(NC)
    ]


def img_perm(move):
    place = lambda l, y: l * NY + y
    return [(place(l, y), place(*move(l, y))) for l in range(NL) for y in range(NY)]


def swap_core(a):
    return lax.ppermute(a, "tile", tile_perm(lambda x, z, c: (x, z, 1 - c)))


def swap_z(a):
    return lax.ppermute(a, "tile", tile_perm(lambda x, z, c: (x, 1 - z, c)))


def shift_x(a, k):
    return lax.ppermute(a, "tile", tile_perm(lambda x, z, c: ((x + k) % NX, z, c)))


def flip_x(a, k):
    return lax.ppermute(a, "tile", tile_perm(lambda x, z, c: (x ^ k, z, c)))


def flip_l(a, k):
    return lax.ppermute(a, "img", img_perm(lambda l, y: (l ^ k, y)))


def shift_y(a, k):
    return lax.ppermute(a, "img", img_perm(lambda l, y: (l, (y + k) % NY)))


def call(body, outs, in_specs, scratch=(), flops=0, nbytes=0, vmem=48 << 20, name=None):
    return pl.pallas_call(
        body,
        out_shape=outs,
        in_specs=in_specs,
        out_specs=jax.tree.map(lambda _: VMEM, outs),
        scratch_shapes=list(scratch),
        compiler_params=pltpu.CompilerParams(vmem_limit_bytes=vmem),
        cost_estimate=pl.CostEstimate(flops=flops, bytes_accessed=nbytes, transcendentals=0),
        name=name,
    )


def shape(s, dtype):
    return jax.ShapeDtypeStruct(s, dtype)


def demod_of(kernel, style):
    total = None
    for t in range(kernel.shape[0]):
        modded = kernel[t] * style
        total = modded * modded if total is None else total + modded * modded
    return lax.rsqrt(jnp.sum(total, axis=1, keepdims=True) + epsilon)


def mix_body(sel, style, bank, kernel, final):
    banks, taps = bank.shape[:2]
    top = sel.shape[1]
    weights = []
    for k in range(banks):
        w = F32(0)
        for j in range(top):
            w = w + jnp.where(sel[0, j] == k, F32((top - j) / (top * (top + 1) / 2)), F32(0))
        weights.append(w)
    for t in range(taps):
        mixed = None
        for k in range(banks):
            term = weights[k] * bank[k, t].astype(F32)
            mixed = term if mixed is None else mixed + term
        kernel[t] = mixed
    demod = demod_of(kernel, style[...])
    for t in range(taps):
        final[t] = (kernel[t] * style[...] * demod).astype(BF16)


def moved_columns(row):
    width = row.shape[0]
    column = lax.broadcasted_iota(jnp.int32, row.shape, 0)
    before = jnp.where(column == 0, F32(0), pltpu.roll(row, 1, 0))
    after = jnp.where(column == width - 1, F32(0), pltpu.roll(row, width - 1, 0))
    return before, after


def turned(row, core, out, at):
    width, channels = row.shape
    groups = channels // (16 * NC)
    flat = jnp.transpose(row)
    for g in range(groups):
        for c in range(NC):
            start = (g * NC + c) * 16
            out[c ^ core, g, :, at] = flat[start : start + 16]


def grad_body(place, cot, fm, grad, cot_t, fm_v):
    rows, width, channels = cot.shape
    groups = channels // (16 * NC)
    core = place[2]
    pad = jnp.zeros((width, channels), BF16)
    for v in range(3):
        fm_v[v, pl.ds(0, width)] = pad
        fm_v[v, pl.ds((rows + 1) * width, width)] = pad

    @pl.loop(0, rows)
    def _(r):
        row = fm[r]
        before, after = moved_columns(row.astype(F32))
        here = pl.ds(pl.multiple_of((r + 1) * width, width), width)
        fm_v[0, here] = before.astype(BF16)
        fm_v[1, here] = row
        fm_v[2, here] = after.astype(BF16)
        turned(cot[r], core, cot_t, pl.ds(pl.multiple_of(r * width, width), width))

    @pl.loop(0, 9)
    def _(t):
        u, v = t // 3, t % 3
        left = cot_t[...].reshape(channels, rows * width)
        right = fm_v[v, pl.ds(pl.multiple_of(u * width, width), rows * width)]
        out = jnp.dot(left, right, preferred_element_type=F32)
        grad[t] = out.reshape(NC, groups, 16, channels)


def edge_body(place, grad, low, high, first, last, mine, theirs, turn_low, turn_high):
    taps, _, groups, _, channels = grad.shape
    width = low.shape[0]
    core = place[2]
    turned(low[...], core, turn_low, pl.ds(0, width))
    turned(high[...], core, turn_high, pl.ds(0, width))

    def put(t, value):
        for g in range(groups):
            mine[g, t] = value[0, g]
            theirs[g, t] = value[1, g].astype(BF16)

    for turn, row, tap in ((turn_high, last, 0), (turn_low, first, 6)):
        whole = row[...].reshape(width, channels)
        before, after = moved_columns(whole.astype(F32))
        left = turn[...].reshape(channels, width)
        for v, right in enumerate((before.astype(BF16), whole, after.astype(BF16))):
            out = jnp.dot(left, right, preferred_element_type=F32)
            put(tap + v, grad[tap + v] + out.reshape(NC, groups, 16, channels))
    for t in (3, 4, 5):
        put(t, grad[t])


def split_x_body(place, mine, got, own, one, two, three):
    x = place[0]
    for k, out in ((0, own), (1, one), (2, two), (3, three)):
        base = lax.rem(x + k, NX) * NZ
        for z in range(NZ):
            out[z] = (mine[base + z] + got[base + z].astype(F32)).astype(out.dtype)


def split_z_body(place, mine, one, two, three, own, other):
    z = place[1]
    for k, out in ((0, own), (1, other)):
        at = z ^ k
        total = mine[at] + one[at].astype(F32) + two[at].astype(F32) + three[at].astype(F32)
        out[...] = total.astype(out.dtype)


def owner_body(sel, style, kernel, mine, got, message, style_part):
    taps, outs, channels = kernel.shape
    top = sel.shape[1]
    s = style[...]
    demod = demod_of(kernel, s)
    total = None
    for t in range(taps):
        grad = mine[t] + got[t].astype(F32)
        term = grad * (kernel[t] * s)
        total = term if total is None else total + term
    curvature = jnp.sum(total, axis=1, keepdims=True)
    slope = demod * demod * demod * curvature
    part = None
    for t in range(taps):
        grad = mine[t] + got[t].astype(F32)
        modded_grad = demod * grad - slope * (kernel[t] * s)
        term = modded_grad * kernel[t]
        part = term if part is None else part + term
        message[t] = (modded_grad * s).astype(BF16)
    style_part[...] = jnp.broadcast_to(jnp.sum(part, axis=0, keepdims=True), style_part.shape)
    bank = lax.broadcasted_iota(jnp.int32, (outs, channels), 0)
    rank = jnp.zeros((outs, channels), F32)
    for j in range(top):
        rank = rank + jnp.where(bank == sel[0, j], F32(top - j), F32(0))
    message[taps] = rank.astype(BF16)


def banks_body(*refs):
    out = refs[-1]
    banks, taps = out.shape[:2]
    pieces = []
    for ref in refs[:-1]:
        if len(ref.shape) == 3:
            pieces.append(ref)
        else:
            pieces.extend(ref.at[n] for n in range(ref.shape[0]))
    weights = [piece[taps].astype(F32) / F32(6) for piece in pieces]

    @pl.loop(0, taps)
    def _(t):
        values = [piece[t].astype(F32) for piece in pieces]
        for k in range(banks):
            total = None
            for weight, value in zip(weights, values):
                term = weight[k : k + 1] * value
                total = term if total is None else total + term
            out[k, t] = total


def input_body(place, near, far, low, high, cot, out, final, padded, sem):
    rows, width, channels = out.shape
    copy = pltpu.make_async_copy(cot, padded.at[pl.ds(1, rows)], sem)
    copy.start()
    padded[0] = low[...]
    padded[rows + 1] = high[...]
    x, z, core = place[0], place[1], place[2]
    for n in range(NX * NZ):
        at = lax.rem(x + NX - n // NZ, NX) * NZ + (z ^ (n % NZ))
        for pieces, c in ((near, core), (far, 1 - core)):
            for t in range(9):
                u, v = t // 3, t % 3
                final[u, pl.ds(pl.multiple_of((at * NC + c) * 16, 16), 16), v * channels : (v + 1) * channels] = pieces[n, t]
    copy.wait()
    step = 2

    @pl.loop(0, rows // step)
    def _(q):
        r = q * step
        left = jnp.concatenate(
            [padded[pl.ds(r + 2 - u, step)].reshape(step * width, channels) for u in range(3)], axis=1
        )
        right = final[...].reshape(3 * channels, 3 * channels)
        sums = jnp.dot(left, right, preferred_element_type=F32)
        for n in range(step):
            part = sums[n * width : (n + 1) * width]
            _, after = moved_columns(part[:, :channels])
            before, _ = moved_columns(part[:, 2 * channels :])
            out[r + n] = (part[:, channels : 2 * channels] + after + before).astype(BF16)


def local(feature_map, cotangent, style, bank, selection):
    _, rows, width, channels = feature_map.shape
    fm = feature_map.reshape(rows, width, channels)
    cot = cotangent.reshape(rows, width, channels)
    banks, own_out, taps, _ = bank.shape
    groups = NX * NZ
    tile = lax.axis_index("tile")
    place = jnp.stack([tile // (NZ * NC), (tile // NC) % NZ, tile % NC]).astype(jnp.int32)

    count = lax.axis_size("tile")
    low = lax.ppermute(cot[rows - 1], "tile", [(i, i + 1) for i in range(count - 1)])
    high = lax.ppermute(cot[0], "tile", [(i + 1, i) for i in range(count - 1)])

    piece = (taps, own_out, channels)
    kernel, final = call(
        mix_body, (shape(piece, F32), shape(piece, BF16)), [SMEM, VMEM, VMEM], flops=10**6, nbytes=10**6, name="mix"
    )(selection, style, jnp.transpose(bank, (0, 2, 1, 3)))

    final_z = swap_z(final)
    near = [final, final_z]
    for k in range(1, NX):
        near += [shift_x(final, k), shift_x(final_z, k)]
    near = jnp.stack(near)
    far = swap_core(near)

    grad = call(
        grad_body,
        shape((taps, NC, groups, 16, channels), F32),
        [SMEM, VMEM, VMEM],
        [
            pltpu.VMEM((NC, groups, 16, rows * width), BF16),
            pltpu.VMEM((3, (rows + 2) * width, channels), BF16),
        ],
        flops=2 * 9 * rows * width * channels * channels,
        nbytes=4 * rows * width * channels,
        name="grad",
    )(place, cot, fm)
    mine, theirs = call(
        edge_body,
        (shape((groups,) + piece, F32), shape((groups,) + piece, BF16)),
        [SMEM] + [VMEM] * 5,
        [pltpu.VMEM((NC, groups, 16, width), BF16)] * 2,
        flops=2 * 6 * width * channels * channels,
        nbytes=4 * 10**6,
        name="edge",
    )(place, grad, low, high, fm[0], fm[rows - 1])

    pair = (NZ,) + piece
    own_x, one, two, three = call(
        split_x_body,
        (shape(pair, F32),) + (shape(pair, BF16),) * 3,
        [SMEM, VMEM, VMEM],
        flops=10**6,
        nbytes=3 * 10**6,
        name="split_x",
    )(place, mine, swap_core(theirs))
    own_z, other = call(
        split_z_body,
        (shape(piece, F32), shape(piece, BF16)),
        [SMEM] + [VMEM] * 4,
        flops=10**6,
        nbytes=10**6,
        name="split_z",
    )(place, own_x, shift_x(one, 1), shift_x(two, 2), shift_x(three, 3))
    message, style_part = call(
        owner_body,
        (shape((taps + 1, own_out, channels), BF16), shape((8, channels), F32)),
        [SMEM] + [VMEM] * 4,
        flops=10**6,
        nbytes=10**6,
        name="owner",
    )(selection, style, kernel, own_z, swap_z(other))

    over_l = [flip_l(message, k) for k in range(1, NL)]
    over_y = [shift_y(message, k) for k in range(1, NY)]
    ahead = jnp.stack(over_l)
    rest = [shift_y(ahead, k) for k in range(1, NY)]

    style_sum = style_part + swap_core(style_part)
    style_sum = style_sum + flip_x(style_sum, 1)
    style_sum = style_sum + flip_x(style_sum, 2)
    style_sum = style_sum + swap_z(style_sum)

    bank_grad = call(
        banks_body,
        shape((banks,) + piece, F32),
        [VMEM] * 10,
        flops=10**7,
        nbytes=3 * 10**6,
        name="banks",
    )(message, *over_l, *over_y, *rest)

    input_grad = call(
        input_body,
        shape((rows, width, channels), BF16),
        [SMEM] + [VMEM] * 4 + [ANY],
        [
            pltpu.VMEM((3, channels, 3 * channels), BF16),
            pltpu.VMEM((rows + 2, width, channels), BF16),
            pltpu.SemaphoreType.DMA,
        ],
        flops=2 * 9 * rows * width * channels * channels,
        nbytes=4 * rows * width * channels,
        name="input",
    )(place, near, far, low, high, cot)

    return (
        input_grad.reshape(feature_map.shape),
        style_sum[:1],
        jnp.transpose(bank_grad, (0, 2, 1, 3)),
    )


def solution(mesh):
    in_specs = (
        P("img", "tile", None, None),
        P("img", "tile", None, None),
        P("img", None),
        P(None, "tile", None, None),
        P("img", None),
    )
    out_specs = (P("img", "tile", None, None), P("img", None), P(None, "tile", None, None))
    return jax.shard_map(local, mesh=mesh, in_specs=in_specs, out_specs=out_specs, check_vma=False)
```

time: 376 us -> 119 us (0.32)
  waiting for transfers between devices: 262 us -> 18.3 us
  starting transfers between devices: 3.16 us -> 62.1 us
  blocking collectives: 46.4 us -> 0 us
  Pallas kernels: 0 us -> 25.4 us
  matrix products: 21 us -> 0 us
  local copies, waits for them, and re-layouts: 22.8 us -> 9.29 us
  between operations: 13.8 us -> 0.92 us
  other arithmetic: 6.48 us -> 0.68 us
    psum x1 -> x0, waiting for transfers between devices: 153 us -> none  [local(): bank_grad = lax.psum(bank_part, 'img')]
    reduce_scatter x1 -> x0, waiting for transfers between devices: 94.5 us -> none  [local(): lax.psum_scatter(jnp.einsum('tbpo,bpi->obti', shifted, flat_in, preferred...]
    ppermute x2 -> x28, starting transfers between devices: 3.04 us -> 62.1 us  [the longest x9 22.1 us: shift_x(): lax.ppermute(a, 'tile', tile_perm(lambda x, z, c: ((x + k) % NX, z, c)))]
    psum x1 -> x0, blocking collectives: 46.4 us -> none  [local(): style_grad = lax.psum(style_part, 'tile')]
    pallas_call x0 -> x8, Pallas kernels: none -> 25.4 us  [the longest x1 10.3 us: local(): call(grad_body, shape((taps, NC, groups, 16, channels), F32), [SMEM, VMEM...]
    dot_general x3 -> x0, matrix products: 21 us -> none  [the longest x1 10.4 us: local(): jnp.einsum('tbpo,bpi->obti', shifted, flat_in, preferred_element_type=jnp...]
    ppermute x2 -> x28, waiting for transfers between devices: 8.9 us -> 18.3 us  [the longest x9 6.04 us: shift_x(): lax.ppermute(a, 'tile', tile_perm(lambda x, z, c: ((x + k) % NX, z, c)))]
    unnamed x19 -> x25, local copies, waits for them, and re-layouts: 15.9 us -> 7.3 us
  transfers between devices with their start and end apart: 5 -> 28, of which waited for: 4 -> 10; matrix products, arithmetic and copies ran while one was open for 3% -> 2% of each run, Pallas kernels for 0% -> 19%
where the time goes in v1:
time: 119 us; the launch traced here: 117 us
  starting transfers between devices  62.1 us (52%)
  Pallas kernels  25.4 us (21%)
  waiting for transfers between devices  18.3 us (15%)
  local copies, waits for them, and re-layouts  9.29 us (8%)
    ppermute x9, starting transfers between devices, shift_x(): lax.ppermute(a, 'tile', tile_perm(lambda x, z, c: ((x + k) % NX, z, c)))  22.1 us
    ppermute x3, starting transfers between devices, swap_z(): return lax.ppermute(a, 'tile', tile_perm(lambda x, z, c: (x, 1 - z, c)))  18.8 us
    pallas_call x1, Pallas kernels, local(): call(grad_body, shape((taps, NC, groups, 16, channels), F32), [SMEM, VMEM...  10.3 us
    pallas_call x1, Pallas kernels, local(): call(input_body, shape((rows, width, channels), BF16), [SMEM] + [VMEM] *...  8.4 us
    ppermute x6, starting transfers between devices, shift_y(): return lax.ppermute(a, 'img', img_perm(lambda l, y: (l, (y + k) % NY)))  8.36 us
    unnamed x25, local copies, waits for them, and re-layouts  7.3 us
    ppermute x9, waiting for transfers between devices, shift_x(): lax.ppermute(a, 'tile', tile_perm(lambda x, z, c: ((x + k) % NX, z, c)))  6.04 us
    ppermute x2, starting transfers between devices, flip_x(): return lax.ppermute(a, 'tile', tile_perm(lambda x, z, c: (x ^ k, z, c)))  4.98 us
  transfers between devices with their start and end apart: 28, of which 10 were waited for; matrix products, arithmetic and copies ran while one was open for 2% of the time, Pallas kernels for 19%

profile of v1, /device:TPU:8, one launch (start us, length us, event | category | flops | bytes accessed | tf_op | source)
XLA Modules:
  0.0 116.6 jit_solution(12558362171671197785)
XLA Ops:
  3.8 7.3 %collective-permute-start = (bf16[9,16,256]{2,1,0:T(8,128)(2,1)S(1)}, bf16[9,16,256]{2,1,0:T(8,128)(2,1)S(1)}, u32[]{:S(2)}, u32[]{:S(2)}) collective-permute-start(bf16[9,16,256]{2,1,0:T(8,128)(2,1)S(1)} %get-tuple-element.15), channel_id=1, source_target_pairs={{0,2},{1,3},{2,0},{3,1},{4,6},{5,7},{6,4},{7,5},{8,10},{9,11},{10,... | collective-permute-start | bytes 221192 | tf_op jit(solution)/shard_map/ppermute | solution.py:41
  11.0 1.5 %collective-permute-start.1 = (bf16[9,16,256]{2,1,0:T(8,128)(2,1)S(1)}, bf16[9,16,256]{2,1,0:T(8,128)(2,1)S(1)}, u32[]{:S(2)}, u32[]{:S(2)}) collective-permute-start(bf16[9,16,256]{2,1,0:T(8,128)(2,1)S(1)} %get-tuple-element.15), channel_id=1, source_target_pairs={{0,4},{1,5},{2,6},{3,7},{4,8},{5,9},{6,10},{7,11},{8,12},{9,13},{1... | collective-permute-start | bytes 221192 | tf_op jit(solution)/shard_map/ppermute | solution.py:45
  12.5 2.7 %collective-permute-start.3 = (bf16[9,16,256]{2,1,0:T(8,128)(2,1)S(1)}, bf16[9,16,256]{2,1,0:T(8,128)(2,1)S(1)}, u32[]{:S(2)}, u32[]{:S(2)}) collective-permute-start(bf16[9,16,256]{2,1,0:T(8,128)(2,1)S(1)} %get-tuple-element.15), channel_id=1, source_target_pairs={{0,8},{1,9},{2,10},{3,11},{4,12},{5,13},{6,14},{7,15},{8,0},{9,1},... | collective-permute-start | bytes 221192 | tf_op jit(solution)/shard_map/ppermute | solution.py:45
  15.3 1.4 %collective-permute-start.5 = (bf16[9,16,256]{2,1,0:T(8,128)(2,1)S(1)}, bf16[9,16,256]{2,1,0:T(8,128)(2,1)S(1)}, u32[]{:S(2)}, u32[]{:S(2)}) collective-permute-start(bf16[9,16,256]{2,1,0:T(8,128)(2,1)S(1)} %get-tuple-element.15), channel_id=1, source_target_pairs={{0,12},{1,13},{2,14},{3,15},{4,0},{5,1},{6,2},{7,3},{8,4},{9,5},{1... | collective-permute-start | bytes 221192 | tf_op jit(solution)/shard_map/ppermute | solution.py:45
  17.7 1.3 %collective-permute-start.8 = (bf16[256,256]{1,0:T(8,128)(2,1)S(1)}, bf16[256,256]{1,0:T(8,128)(2,1)S(1)}, u32[]{:S(2)}, u32[]{:S(2)}) collective-permute-start(bf16[256,256]{1,0:T(8,128)(2,1)S(1)} %get-tuple-element.30), channel_id=1, source_target_pairs={{0,1},{1,2},{2,3},{3,4},{4,5},{5,6},{6,7},{7,8},{8,9},{9,10},{10,1... | collective-permute-start | bytes 393224 | tf_op jit(solution)/shard_map/ppermute | solution.py:280
  20.1 1.6 %copy-done.2 = bf16[1,16,256,256]{3,2,1,0:T(8,128)(2,1)S(1)} copy-done((bf16[1,16,256,256]{3,2,1,0:T(8,128)(2,1)S(1)}, bf16[1,16,256,256]{3,2,1,0:T(8,128)(2,1)}, u32[]{:S(2)}) %copy-start.2) | copy-done | bytes 2097176
  21.7 1.6 %copy-done.3 = bf16[1,16,256,256]{3,2,1,0:T(8,128)(2,1)S(1)} copy-done((bf16[1,16,256,256]{3,2,1,0:T(8,128)(2,1)S(1)}, bf16[1,16,256,256]{3,2,1,0:T(8,128)(2,1)}, u32[]{:S(2)}) %copy-start.3) | copy-done | bytes 2097176
  23.3 10.3 %grad.1 = f32[9,2,8,16,256]{4,3,2,1,0:T(8,128)} custom-call(s32[3]{0:T(128)S(1)} %pad_add_fusion.place, bf16[16,256,256]{2,1,0:T(8,128)(2,1)S(1)} %bitcast.40, bf16[16,256,256]{2,1,0:T(8,128)(2,1)S(1)} %bitcast.39), custom_call_target="tpu_custom_call" | custom-call | flops 4831838208 | bytes 4194304 | tf_op jit(solution)/shard_map/grad/pallas_call | solution.py:295
  33.6 1.3 %collective-permute-start.9 = (bf16[256,256]{1,0:T(8,128)(2,1)S(1)}, bf16[256,256]{1,0:T(8,128)(2,1)S(1)}, u32[]{:S(2)}, u32[]{:S(2)}) collective-permute-start(bf16[256,256]{1,0:T(8,128)(2,1)S(1)} %get-tuple-element.29), channel_id=1, source_target_pairs={{1,0},{2,1},{3,2},{4,3},{5,4},{6,5},{7,6},{8,7},{9,8},{10,9},{11,1... | collective-permute-start | bytes 393224 | tf_op jit(solution)/shard_map/ppermute | solution.py:281
  34.9 8.4 %collective-permute-start.2 = (bf16[9,16,256]{2,1,0:T(8,128)(2,1)S(1)}, bf16[9,16,256]{2,1,0:T(8,128)(2,1)S(1)}, u32[]{:S(2)}, u32[]{:S(2)}) collective-permute-start(bf16[9,16,256]{2,1,0:T(8,128)(2,1)S(1)} %collective-permute-done), channel_id=1, source_target_pairs={{0,4},{1,5},{2,6},{3,7},{4,8},{5,9},{6,10},{7,11},{8,12},{9,13},{1... | collective-permute-start | bytes 221192 | tf_op jit(solution)/shard_map/ppermute | solution.py:45
  44.3 1.8 %collective-permute-start.6 = (bf16[9,16,256]{2,1,0:T(8,128)(2,1)S(1)}, bf16[9,16,256]{2,1,0:T(8,128)(2,1)S(1)}, u32[]{:S(2)}, u32[]{:S(2)}) collective-permute-start(bf16[9,16,256]{2,1,0:T(8,128)(2,1)S(1)} %collective-permute-done), channel_id=1, source_target_pairs={{0,12},{1,13},{2,14},{3,15},{4,0},{5,1},{6,2},{7,3},{8,4},{9,5},{1... | collective-permute-start | bytes 221192 | tf_op jit(solution)/shard_map/ppermute | solution.py:45
  46.2 1.7 %copy-done = f32[9,2,8,16,256]{4,3,2,1,0:T(8,128)S(1)} copy-done((f32[9,2,8,16,256]{4,3,2,1,0:T(8,128)S(1)}, f32[9,2,8,16,256]{4,3,2,1,0:T(8,128)}, u32[]{:S(2)}) %copy-start) | copy-done | bytes 2359320
  49.7 1.3 %collective-permute-done.10.got = bf16[8,9,16,256]{3,2,1,0:T(8,128)(2,1)S(1)} collective-permute-done((bf16[8,9,16,256]{3,2,1,0:T(8,128)(2,1)S(1)}, bf16[8,9,16,256]{3,2,1,0:T(8,128)(2,1)S(1)}, u32[]{:S(2)}, u32[]{:S(2)}) %collective-permute-start.10) | collective-permute-done | bytes 589856 | tf_op jit(solution)/shard_map/ppermute | solution.py:37
  52.1 2.4 %collective-permute-start.12 = (bf16[2,9,16,256]{3,2,1,0:T(8,128)(2,1)S(1)}, bf16[2,9,16,256]{3,2,1,0:T(8,128)(2,1)S(1)}, u32[]{:S(2)}, u32[]{:S(2)}) collective-permute-start(bf16[2,9,16,256]{3,2,1,0:T(8,128)(2,1)S(1)} %get-tuple-element.21), channel_id=1, source_target_pairs={{0,8},{1,9},{2,10},{3,11},{4,12},{5,13},{6,14},{7,15},{8,0},{9,1},... | collective-permute-start | bytes 442376 | tf_op jit(solution)/shard_map/ppermute | solution.py:45
  54.5 2.3 %collective-permute-start.13 = (bf16[2,9,16,256]{3,2,1,0:T(8,128)(2,1)S(1)}, bf16[2,9,16,256]{3,2,1,0:T(8,128)(2,1)S(1)}, u32[]{:S(2)}, u32[]{:S(2)}) collective-permute-start(bf16[2,9,16,256]{3,2,1,0:T(8,128)(2,1)S(1)} %get-tuple-element.22), channel_id=1, source_target_pairs={{0,12},{1,13},{2,14},{3,15},{4,0},{5,1},{6,2},{7,3},{8,4},{9,5},{1... | collective-permute-start | bytes 442376 | tf_op jit(solution)/shard_map/ppermute | solution.py:45
  56.8 5.1 %collective-permute-done.11.one = bf16[2,9,16,256]{3,2,1,0:T(8,128)(2,1)S(1)} collective-permute-done((bf16[2,9,16,256]{3,2,1,0:T(8,128)(2,1)S(1)}, bf16[2,9,16,256]{3,2,1,0:T(8,128)(2,1)S(1)}, u32[]{:S(2)}, u32[]{:S(2)}) %collective-permute-start.11) | collective-permute-done | bytes 147488 | tf_op jit(solution)/shard_map/ppermute | solution.py:45
  63.1 6.0 %collective-permute-start.14 = (bf16[9,16,256]{2,1,0:T(8,128)(2,1)S(1)}, bf16[9,16,256]{2,1,0:T(8,128)(2,1)S(1)}, u32[]{:S(2)}, u32[]{:S(2)}) collective-permute-start(bf16[9,16,256]{2,1,0:T(8,128)(2,1)S(1)} %get-tuple-element.24), channel_id=1, source_target_pairs={{0,2},{1,3},{2,0},{3,1},{4,6},{5,7},{6,4},{7,5},{8,10},{9,11},{10,... | collective-permute-start | bytes 221192 | tf_op jit(solution)/shard_map/ppermute | solution.py:41
  69.2 2.4 %collective-permute-done.14.got = bf16[9,16,256]{2,1,0:T(8,128)(2,1)S(1)} collective-permute-done((bf16[9,16,256]{2,1,0:T(8,128)(2,1)S(1)}, bf16[9,16,256]{2,1,0:T(8,128)(2,1)S(1)}, u32[]{:S(2)}, u32[]{:S(2)}) %collective-permute-start.14) | collective-permute-done | bytes 73760 | tf_op jit(solution)/shard_map/ppermute | solution.py:41
  72.3 2.4 %collective-permute-start.19 = (bf16[10,16,256]{2,1,0:T(8,128)(2,1)S(1)}, bf16[10,16,256]{2,1,0:T(8,128)(2,1)S(1)}, u32[]{:S(2)}, u32[]{:S(2)}) collective-permute-start(bf16[10,16,256]{2,1,0:T(8,128)(2,1)S(1)} %get-tuple-element.26.refs_0_), channel_id=1, source_target_pairs={{0,64},{16,80},{32,96},{48,112},{64,0},{80,16},{96,32},{112,48},{1... | collective-permute-start | bytes 245768 | tf_op jit(solution)/shard_map/ppermute | solution.py:53
  75.0 2.2 %collective-permute-start.21 = (bf16[10,16,256]{2,1,0:T(8,128)(2,1)S(1)}, bf16[10,16,256]{2,1,0:T(8,128)(2,1)S(1)}, u32[]{:S(2)}, u32[]{:S(2)}) collective-permute-start(bf16[10,16,256]{2,1,0:T(8,128)(2,1)S(1)} %get-tuple-element.26.refs_0_), channel_id=1, source_target_pairs={{0,192},{16,208},{32,224},{48,240},{64,128},{80,144},{96,160},{112... | collective-permute-start | bytes 245768 | tf_op jit(solution)/shard_map/ppermute | solution.py:53
  78.3 2.3 %collective-permute-start.16 = (f32[8,256]{1,0:T(8,128)S(1)}, f32[8,256]{1,0:T(8,128)S(1)}, u32[]{:S(2)}, u32[]{:S(2)}) collective-permute-start(f32[8,256]{1,0:T(8,128)S(1)} %add.23), channel_id=1, source_target_pairs={{0,4},{1,5},{2,6},{3,7},{4,0},{5,1},{6,2},{7,3},{8,12},{9,13},{10,... | collective-permute-start | bytes 24584 | tf_op jit(solution)/shard_map/ppermute | solution.py:49
  80.7 1.6 %collective-permute-done.16 = f32[8,256]{1,0:T(8,128)S(1)} collective-permute-done((f32[8,256]{1,0:T(8,128)S(1)}, f32[8,256]{1,0:T(8,128)S(1)}, u32[]{:S(2)}, u32[]{:S(2)}) %collective-permute-start.16) | collective-permute-done | bytes 8224 | tf_op jit(solution)/shard_map/ppermute | solution.py:49
  82.3 2.6 %collective-permute-start.17 = (f32[8,256]{1,0:T(8,128)S(1)}, f32[8,256]{1,0:T(8,128)S(1)}, u32[]{:S(2)}, u32[]{:S(2)}) collective-permute-start(f32[8,256]{1,0:T(8,128)S(1)} %add.24), channel_id=1, source_target_pairs={{0,8},{1,9},{2,10},{3,11},{4,12},{5,13},{6,14},{7,15},{8,0},{9,1},... | collective-permute-start | bytes 24584 | tf_op jit(solution)/shard_map/ppermute | solution.py:49
  85.0 2.5 %collective-permute-done.17 = f32[8,256]{1,0:T(8,128)S(1)} collective-permute-done((f32[8,256]{1,0:T(8,128)S(1)}, f32[8,256]{1,0:T(8,128)S(1)}, u32[]{:S(2)}, u32[]{:S(2)}) %collective-permute-start.17) | collective-permute-done | bytes 8224 | tf_op jit(solution)/shard_map/ppermute | solution.py:49
  87.5 1.6 %collective-permute-start.22 = (bf16[10,16,256]{2,1,0:T(8,128)(2,1)S(1)}, bf16[10,16,256]{2,1,0:T(8,128)(2,1)S(1)}, u32[]{:S(2)}, u32[]{:S(2)}) collective-permute-start(bf16[10,16,256]{2,1,0:T(8,128)(2,1)S(1)} %get-tuple-element.26.refs_0_), channel_id=1, source_target_pairs={{0,16},{16,32},{32,48},{48,0},{64,80},{80,96},{96,112},{112,64},{1... | collective-permute-start | bytes 245768 | tf_op jit(solution)/shard_map/ppermute | solution.py:57
  89.0 5.5 %collective-permute-start.18 = (f32[8,256]{1,0:T(8,128)S(1)}, f32[8,256]{1,0:T(8,128)S(1)}, u32[]{:S(2)}, u32[]{:S(2)}) collective-permute-start(f32[8,256]{1,0:T(8,128)S(1)} %add.25), channel_id=1, source_target_pairs={{0,2},{1,3},{2,0},{3,1},{4,6},{5,7},{6,4},{7,5},{8,10},{9,11},{10,... | collective-permute-start | bytes 24584 | tf_op jit(solution)/shard_map/ppermute | solution.py:41
  94.6 1.4 %collective-permute-start.25 = (bf16[3,10,16,256]{3,2,1,0:T(8,128)(2,1)S(1)}, bf16[3,10,16,256]{3,2,1,0:T(8,128)(2,1)S(1)}, u32[]{:S(2)}, u32[]{:S(2)}) collective-permute-start(bf16[3,10,16,256]{3,2,1,0:T(8,128)(2,1)S(1)} %pad_maximum_fusion), channel_id=1, source_target_pairs={{0,16},{16,32},{32,48},{48,0},{64,80},{80,96},{96,112},{112,64},{1... | collective-permute-start | bytes 737288 | tf_op jit(solution)/shard_map/ppermute | solution.py:57
  98.3 8.4 %input.1 = bf16[16,256,256]{2,1,0:T(8,128)(2,1)} custom-call(s32[3]{0:T(128)S(1)} %pad_add_fusion.place, bf16[8,9,16,256]{3,2,1,0:T(8,128)(2,1)S(1)} %bitcast_dynamic-update-slice_fusion.near, bf16[8,9,16,256]{3,2,1,0:T(8,128)(2,1)S(1)} %collective-permute-done.7.far, bf16[256,256]{1,0:T(8,128)(2,1)S(1)} %collective-permute-done.8.low, ...), custom_call_target="tpu_custom_call" | custom-call | flops 4831838208 | bytes 4194304 | tf_op jit(solution)/shard_map/input/pallas_call | solution.py:362
  106.7 1.5 %collective-permute-start.23 = (bf16[10,16,256]{2,1,0:T(8,128)(2,1)S(1)}, bf16[10,16,256]{2,1,0:T(8,128)(2,1)S(1)}, u32[]{:S(2)}, u32[]{:S(2)}) collective-permute-start(bf16[10,16,256]{2,1,0:T(8,128)(2,1)S(1)} %get-tuple-element.26.refs_0_), channel_id=1, source_target_pairs={{0,32},{16,48},{32,0},{48,16},{64,96},{80,112},{96,64},{112,80},{1... | collective-permute-start | bytes 245768 | tf_op jit(solution)/shard_map/ppermute | solution.py:57
  108.1 1.7 %collective-permute-start.24 = (bf16[10,16,256]{2,1,0:T(8,128)(2,1)S(1)}, bf16[10,16,256]{2,1,0:T(8,128)(2,1)S(1)}, u32[]{:S(2)}, u32[]{:S(2)}) collective-permute-start(bf16[10,16,256]{2,1,0:T(8,128)(2,1)S(1)} %get-tuple-element.26.refs_0_), channel_id=1, source_target_pairs={{0,48},{16,0},{32,16},{48,32},{64,112},{80,64},{96,80},{112,96},{1... | collective-permute-start | bytes 245768 | tf_op jit(solution)/shard_map/ppermute | solution.py:57
  110.4 2.4 %collective-permute-done.23.refs_5_ = bf16[10,16,256]{2,1,0:T(8,128)(2,1)S(1)} collective-permute-done((bf16[10,16,256]{2,1,0:T(8,128)(2,1)S(1)}, bf16[10,16,256]{2,1,0:T(8,128)(2,1)S(1)}, u32[]{:S(2)}, u32[]{:S(2)}) %collective-permute-start.23) | collective-permute-done | bytes 81952 | tf_op jit(solution)/shard_map/ppermute | solution.py:57
  113.6 3.0 %banks.1 = f32[8,9,16,256]{3,2,1,0:T(8,128)} custom-call(bf16[10,16,256]{2,1,0:T(8,128)(2,1)S(1)} %get-tuple-element.26.refs_0_, bf16[10,16,256]{2,1,0:T(8,128)(2,1)S(1)} %collective-permute-done.19.refs_1_, bf16[10,16,256]{2,1,0:T(8,128)(2,1)S(1)} %collective-permute-done.20.refs_2_, bf16[10,16,256]{2,1,0:T(8,128)(2,1)S(1)} %collective-permute-done.21.refs_3_, ...), custom_call_target="tpu_custom_call" | custom-call | flops 10000000 | bytes 3000000 | tf_op jit(solution)/shard_map/banks/pallas_call | solution.py:353
  (66 shorter events, 16.1 us)
Async XLA Ops:
  3.8 29.8 %collective-permute-start = (bf16[9,16,256]{2,1,0:T(8,128)(2,1)S(1)}, bf16[9,16,256]{2,1,0:T(8,128)(2,1)S(1)}, u32[]{:S(2)}, u32[]{:S(2)}) collective-permute-start(bf16[9,16,256]{2,1,0:T(8,128)(2,1)S(1)} %get-tuple-element.15), channel_id=1, source_target_pairs={{0,2},{1,3},{2,0},{3,1},{4,6},{5,7},{6,4},{7,5},{8,10},{9,11},{10,... | collective-permute-start | bytes 221192 | tf_op jit(solution)/shard_map/ppermute | solution.py:41
  11.0 23.9 %collective-permute-start.1 = (bf16[9,16,256]{2,1,0:T(8,128)(2,1)S(1)}, bf16[9,16,256]{2,1,0:T(8,128)(2,1)S(1)}, u32[]{:S(2)}, u32[]{:S(2)}) collective-permute-start(bf16[9,16,256]{2,1,0:T(8,128)(2,1)S(1)} %get-tuple-element.15), channel_id=1, source_target_pairs={{0,4},{1,5},{2,6},{3,7},{4,8},{5,9},{6,10},{7,11},{8,12},{9,13},{1... | collective-permute-start | bytes 221192 | tf_op jit(solution)/shard_map/ppermute | solution.py:45
  12.5 36.5 %collective-permute-start.3 = (bf16[9,16,256]{2,1,0:T(8,128)(2,1)S(1)}, bf16[9,16,256]{2,1,0:T(8,128)(2,1)S(1)}, u32[]{:S(2)}, u32[]{:S(2)}) collective-permute-start(bf16[9,16,256]{2,1,0:T(8,128)(2,1)S(1)} %get-tuple-element.15), channel_id=1, source_target_pairs={{0,8},{1,9},{2,10},{3,11},{4,12},{5,13},{6,14},{7,15},{8,0},{9,1},... | collective-permute-start | bytes 221192 | tf_op jit(solution)/shard_map/ppermute | solution.py:45
  15.3 34.1 %collective-permute-start.5 = (bf16[9,16,256]{2,1,0:T(8,128)(2,1)S(1)}, bf16[9,16,256]{2,1,0:T(8,128)(2,1)S(1)}, u32[]{:S(2)}, u32[]{:S(2)}) collective-permute-start(bf16[9,16,256]{2,1,0:T(8,128)(2,1)S(1)} %get-tuple-element.15), channel_id=1, source_target_pairs={{0,12},{1,13},{2,14},{3,15},{4,0},{5,1},{6,2},{7,3},{8,4},{9,5},{1... | collective-permute-start | bytes 221192 | tf_op jit(solution)/shard_map/ppermute | solution.py:45
  17.7 25.7 %collective-permute-start.8 = (bf16[256,256]{1,0:T(8,128)(2,1)S(1)}, bf16[256,256]{1,0:T(8,128)(2,1)S(1)}, u32[]{:S(2)}, u32[]{:S(2)}) collective-permute-start(bf16[256,256]{1,0:T(8,128)(2,1)S(1)} %get-tuple-element.30), channel_id=1, source_target_pairs={{0,1},{1,2},{2,3},{3,4},{4,5},{5,6},{6,7},{7,8},{8,9},{9,10},{10,1... | collective-permute-start | bytes 393224 | tf_op jit(solution)/shard_map/ppermute | solution.py:280
  33.6 10.8 %collective-permute-start.9 = (bf16[256,256]{1,0:T(8,128)(2,1)S(1)}, bf16[256,256]{1,0:T(8,128)(2,1)S(1)}, u32[]{:S(2)}, u32[]{:S(2)}) collective-permute-start(bf16[256,256]{1,0:T(8,128)(2,1)S(1)} %get-tuple-element.29), channel_id=1, source_target_pairs={{1,0},{2,1},{3,2},{4,3},{5,4},{6,5},{7,6},{8,7},{9,8},{10,9},{11,1... | collective-permute-start | bytes 393224 | tf_op jit(solution)/shard_map/ppermute | solution.py:281
  34.9 13.9 %collective-permute-start.2 = (bf16[9,16,256]{2,1,0:T(8,128)(2,1)S(1)}, bf16[9,16,256]{2,1,0:T(8,128)(2,1)S(1)}, u32[]{:S(2)}, u32[]{:S(2)}) collective-permute-start(bf16[9,16,256]{2,1,0:T(8,128)(2,1)S(1)} %collective-permute-done), channel_id=1, source_target_pairs={{0,4},{1,5},{2,6},{3,7},{4,8},{5,9},{6,10},{7,11},{8,12},{9,13},{1... | collective-permute-start | bytes 221192 | tf_op jit(solution)/shard_map/ppermute | solution.py:45
  43.4 5.9 %collective-permute-start.4 = (bf16[9,16,256]{2,1,0:T(8,128)(2,1)S(1)}, bf16[9,16,256]{2,1,0:T(8,128)(2,1)S(1)}, u32[]{:S(2)}, u32[]{:S(2)}) collective-permute-start(bf16[9,16,256]{2,1,0:T(8,128)(2,1)S(1)} %collective-permute-done), channel_id=1, source_target_pairs={{0,8},{1,9},{2,10},{3,11},{4,12},{5,13},{6,14},{7,15},{8,0},{9,1},... | collective-permute-start | bytes 221192 | tf_op jit(solution)/shard_map/ppermute | solution.py:45
  44.3 5.0 %collective-permute-start.6 = (bf16[9,16,256]{2,1,0:T(8,128)(2,1)S(1)}, bf16[9,16,256]{2,1,0:T(8,128)(2,1)S(1)}, u32[]{:S(2)}, u32[]{:S(2)}) collective-permute-start(bf16[9,16,256]{2,1,0:T(8,128)(2,1)S(1)} %collective-permute-done), channel_id=1, source_target_pairs={{0,12},{1,13},{2,14},{3,15},{4,0},{5,1},{6,2},{7,3},{8,4},{9,5},{1... | collective-permute-start | bytes 221192 | tf_op jit(solution)/shard_map/ppermute | solution.py:45
  46.2 1.7 %copy-start = (f32[9,2,8,16,256]{4,3,2,1,0:T(8,128)S(1)}, f32[9,2,8,16,256]{4,3,2,1,0:T(8,128)}, u32[]{:S(2)}) copy-start(f32[9,2,8,16,256]{4,3,2,1,0:T(8,128)} %grad.1) | copy-start | bytes 7077892
  48.8 22.8 %copy-start.6 = (f32[1,256]{1,0:T(1,128)S(1)}, f32[1,256]{1,0:T(1,128)}, u32[]{:S(2)}) copy-start(f32[1,256]{1,0:T(1,128)} %style.3) | copy-start | bytes 3076
  48.8 22.8 %copy-start.8 = (s32[1,3]{1,0:T(1,128)S(1)}, s32[1,3]{1,0:T(1,128)}, u32[]{:S(2)}) copy-start(s32[1,3]{1,0:T(1,128)} %sel.3) | copy-start | bytes 40
  48.9 49.4 %copy-start.4 = (bf16[1,16,256,256]{3,2,1,0:T(8,128)(2,1)S(1)}, bf16[1,16,256,256]{3,2,1,0:T(8,128)(2,1)}, u32[]{:S(2)}) copy-start(bf16[1,16,256,256]{3,2,1,0:T(8,128)(2,1)} %param.6) | copy-start | bytes 6291460
  48.9 2.1 %collective-permute-start.10 = (bf16[8,9,16,256]{3,2,1,0:T(8,128)(2,1)S(1)}, bf16[8,9,16,256]{3,2,1,0:T(8,128)(2,1)S(1)}, u32[]{:S(2)}, u32[]{:S(2)}) collective-permute-start(bf16[8,9,16,256]{3,2,1,0:T(8,128)(2,1)S(1)} %get-tuple-element.18), channel_id=1, source_target_pairs={{0,1},{1,0},{2,3},{3,2},{4,5},{5,4},{6,7},{7,6},{8,9},{9,8},{10,11... | collective-permute-start | bytes 1769480 | tf_op jit(solution)/shard_map/ppermute | solution.py:37
  49.4 47.8 %collective-permute-start.7 = (bf16[8,9,16,256]{3,2,1,0:T(8,128)(2,1)S(1)}, bf16[8,9,16,256]{3,2,1,0:T(8,128)(2,1)S(1)}, u32[]{:S(2)}, u32[]{:S(2)}) collective-permute-start(bf16[8,9,16,256]{3,2,1,0:T(8,128)(2,1)S(1)} %bitcast_dynamic-update-slice_fusion.near), channel_id=1, source_target_pairs={{0,1},{1,0},{2,3},{3,2},{4,5},{5,4},{6,7},{7,6},{8,9},{9,8},{10,11... | collective-permute-start | bytes 1769480 | tf_op jit(solution)/shard_map/ppermute | solution.py:37
  51.6 10.3 %collective-permute-start.11 = (bf16[2,9,16,256]{3,2,1,0:T(8,128)(2,1)S(1)}, bf16[2,9,16,256]{3,2,1,0:T(8,128)(2,1)S(1)}, u32[]{:S(2)}, u32[]{:S(2)}) collective-permute-start(bf16[2,9,16,256]{3,2,1,0:T(8,128)(2,1)S(1)} %get-tuple-element.20), channel_id=1, source_target_pairs={{0,4},{1,5},{2,6},{3,7},{4,8},{5,9},{6,10},{7,11},{8,12},{9,13},{1... | collective-permute-start | bytes 442376 | tf_op jit(solution)/shard_map/ppermute | solution.py:45
  52.1 9.8 %collective-permute-start.12 = (bf16[2,9,16,256]{3,2,1,0:T(8,128)(2,1)S(1)}, bf16[2,9,16,256]{3,2,1,0:T(8,128)(2,1)S(1)}, u32[]{:S(2)}, u32[]{:S(2)}) collective-permute-start(bf16[2,9,16,256]{3,2,1,0:T(8,128)(2,1)S(1)} %get-tuple-element.21), channel_id=1, source_target_pairs={{0,8},{1,9},{2,10},{3,11},{4,12},{5,13},{6,14},{7,15},{8,0},{9,1},... | collective-permute-start | bytes 442376 | tf_op jit(solution)/shard_map/ppermute | solution.py:45
  54.5 8.0 %collective-permute-start.13 = (bf16[2,9,16,256]{3,2,1,0:T(8,128)(2,1)S(1)}, bf16[2,9,16,256]{3,2,1,0:T(8,128)(2,1)S(1)}, u32[]{:S(2)}, u32[]{:S(2)}) collective-permute-start(bf16[2,9,16,256]{3,2,1,0:T(8,128)(2,1)S(1)} %get-tuple-element.22), channel_id=1, source_target_pairs={{0,12},{1,13},{2,14},{3,15},{4,0},{5,1},{6,2},{7,3},{8,4},{9,5},{1... | collective-permute-start | bytes 442376 | tf_op jit(solution)/shard_map/ppermute | solution.py:45
  63.1 8.5 %collective-permute-start.14 = (bf16[9,16,256]{2,1,0:T(8,128)(2,1)S(1)}, bf16[9,16,256]{2,1,0:T(8,128)(2,1)S(1)}, u32[]{:S(2)}, u32[]{:S(2)}) collective-permute-start(bf16[9,16,256]{2,1,0:T(8,128)(2,1)S(1)} %get-tuple-element.24), channel_id=1, source_target_pairs={{0,2},{1,3},{2,0},{3,1},{4,6},{5,7},{6,4},{7,5},{8,10},{9,11},{10,... | collective-permute-start | bytes 221192 | tf_op jit(solution)/shard_map/ppermute | solution.py:41
  72.3 16.7 %collective-permute-start.19 = (bf16[10,16,256]{2,1,0:T(8,128)(2,1)S(1)}, bf16[10,16,256]{2,1,0:T(8,128)(2,1)S(1)}, u32[]{:S(2)}, u32[]{:S(2)}) collective-permute-start(bf16[10,16,256]{2,1,0:T(8,128)(2,1)S(1)} %get-tuple-element.26.refs_0_), channel_id=1, source_target_pairs={{0,64},{16,80},{32,96},{48,112},{64,0},{80,16},{96,32},{112,48},{1... | collective-permute-start | bytes 245768 | tf_op jit(solution)/shard_map/ppermute | solution.py:53
  74.7 19.9 %collective-permute-start.20 = (bf16[10,16,256]{2,1,0:T(8,128)(2,1)S(1)}, bf16[10,16,256]{2,1,0:T(8,128)(2,1)S(1)}, u32[]{:S(2)}, u32[]{:S(2)}) collective-permute-start(bf16[10,16,256]{2,1,0:T(8,128)(2,1)S(1)} %get-tuple-element.26.refs_0_), channel_id=1, source_target_pairs={{0,128},{16,144},{32,160},{48,176},{64,192},{80,208},{96,224},{112... | collective-permute-start | bytes 245768 | tf_op jit(solution)/shard_map/ppermute | solution.py:53
  75.0 19.6 %collective-permute-start.21 = (bf16[10,16,256]{2,1,0:T(8,128)(2,1)S(1)}, bf16[10,16,256]{2,1,0:T(8,128)(2,1)S(1)}, u32[]{:S(2)}, u32[]{:S(2)}) collective-permute-start(bf16[10,16,256]{2,1,0:T(8,128)(2,1)S(1)} %get-tuple-element.26.refs_0_), channel_id=1, source_target_pairs={{0,192},{16,208},{32,224},{48,240},{64,128},{80,144},{96,160},{112... | collective-permute-start | bytes 245768 | tf_op jit(solution)/shard_map/ppermute | solution.py:53
  77.2 1.2 %collective-permute-start.15 = (f32[8,256]{1,0:T(8,128)S(1)}, f32[8,256]{1,0:T(8,128)S(1)}, u32[]{:S(2)}, u32[]{:S(2)}) collective-permute-start(f32[8,256]{1,0:T(8,128)S(1)} %get-tuple-element.25), channel_id=1, source_target_pairs={{0,1},{1,0},{2,3},{3,2},{4,5},{5,4},{6,7},{7,6},{8,9},{9,8},{10,11... | collective-permute-start | bytes 24584 | tf_op jit(solution)/shard_map/ppermute | solution.py:37
  78.3 4.0 %collective-permute-start.16 = (f32[8,256]{1,0:T(8,128)S(1)}, f32[8,256]{1,0:T(8,128)S(1)}, u32[]{:S(2)}, u32[]{:S(2)}) collective-permute-start(f32[8,256]{1,0:T(8,128)S(1)} %add.23), channel_id=1, source_target_pairs={{0,4},{1,5},{2,6},{3,7},{4,0},{5,1},{6,2},{7,3},{8,12},{9,13},{10,... | collective-permute-start | bytes 24584 | tf_op jit(solution)/shard_map/ppermute | solution.py:49
  82.3 5.2 %collective-permute-start.17 = (f32[8,256]{1,0:T(8,128)S(1)}, f32[8,256]{1,0:T(8,128)S(1)}, u32[]{:S(2)}, u32[]{:S(2)}) collective-permute-start(f32[8,256]{1,0:T(8,128)S(1)} %add.24), channel_id=1, source_target_pairs={{0,8},{1,9},{2,10},{3,11},{4,12},{5,13},{6,14},{7,15},{8,0},{9,1},... | collective-permute-start | bytes 24584 | tf_op jit(solution)/shard_map/ppermute | solution.py:49
  87.5 20.7 %collective-permute-start.22 = (bf16[10,16,256]{2,1,0:T(8,128)(2,1)S(1)}, bf16[10,16,256]{2,1,0:T(8,128)(2,1)S(1)}, u32[]{:S(2)}, u32[]{:S(2)}) collective-permute-start(bf16[10,16,256]{2,1,0:T(8,128)(2,1)S(1)} %get-tuple-element.26.refs_0_), channel_id=1, source_target_pairs={{0,16},{16,32},{32,48},{48,0},{64,80},{80,96},{96,112},{112,64},{1... | collective-permute-start | bytes 245768 | tf_op jit(solution)/shard_map/ppermute | solution.py:57
  89.0 17.6 %collective-permute-start.18 = (f32[8,256]{1,0:T(8,128)S(1)}, f32[8,256]{1,0:T(8,128)S(1)}, u32[]{:S(2)}, u32[]{:S(2)}) collective-permute-start(f32[8,256]{1,0:T(8,128)S(1)} %add.25), channel_id=1, source_target_pairs={{0,2},{1,3},{2,0},{3,1},{4,6},{5,7},{6,4},{7,5},{8,10},{9,11},{10,... | collective-permute-start | bytes 24584 | tf_op jit(solution)/shard_map/ppermute | solution.py:41
  94.6 19.0 %collective-permute-start.25 = (bf16[3,10,16,256]{3,2,1,0:T(8,128)(2,1)S(1)}, bf16[3,10,16,256]{3,2,1,0:T(8,128)(2,1)S(1)}, u32[]{:S(2)}, u32[]{:S(2)}) collective-permute-start(bf16[3,10,16,256]{3,2,1,0:T(8,128)(2,1)S(1)} %pad_maximum_fusion), channel_id=1, source_target_pairs={{0,16},{16,32},{32,48},{48,0},{64,80},{80,96},{96,112},{112,64},{1... | collective-permute-start | bytes 737288 | tf_op jit(solution)/shard_map/ppermute | solution.py:57
  96.0 17.6 %collective-permute-start.26 = (bf16[3,10,16,256]{3,2,1,0:T(8,128)(2,1)S(1)}, bf16[3,10,16,256]{3,2,1,0:T(8,128)(2,1)S(1)}, u32[]{:S(2)}, u32[]{:S(2)}) collective-permute-start(bf16[3,10,16,256]{3,2,1,0:T(8,128)(2,1)S(1)} %pad_maximum_fusion), channel_id=1, source_target_pairs={{0,32},{16,48},{32,0},{48,16},{64,96},{80,112},{96,64},{112,80},{1... | collective-permute-start | bytes 737288 | tf_op jit(solution)/shard_map/ppermute | solution.py:57
  97.2 16.4 %collective-permute-start.27 = (bf16[3,10,16,256]{3,2,1,0:T(8,128)(2,1)S(1)}, bf16[3,10,16,256]{3,2,1,0:T(8,128)(2,1)S(1)}, u32[]{:S(2)}, u32[]{:S(2)}) collective-permute-start(bf16[3,10,16,256]{3,2,1,0:T(8,128)(2,1)S(1)} %pad_maximum_fusion), channel_id=1, source_target_pairs={{0,48},{16,0},{32,16},{48,32},{64,112},{80,64},{96,80},{112,96},{1... | collective-permute-start | bytes 737288 | tf_op jit(solution)/shard_map/ppermute | solution.py:57
  106.7 6.1 %collective-permute-start.23 = (bf16[10,16,256]{2,1,0:T(8,128)(2,1)S(1)}, bf16[10,16,256]{2,1,0:T(8,128)(2,1)S(1)}, u32[]{:S(2)}, u32[]{:S(2)}) collective-permute-start(bf16[10,16,256]{2,1,0:T(8,128)(2,1)S(1)} %get-tuple-element.26.refs_0_), channel_id=1, source_target_pairs={{0,32},{16,48},{32,0},{48,16},{64,96},{80,112},{96,64},{112,80},{1... | collective-permute-start | bytes 245768 | tf_op jit(solution)/shard_map/ppermute | solution.py:57
  108.1 5.4 %collective-permute-start.24 = (bf16[10,16,256]{2,1,0:T(8,128)(2,1)S(1)}, bf16[10,16,256]{2,1,0:T(8,128)(2,1)S(1)}, u32[]{:S(2)}, u32[]{:S(2)}) collective-permute-start(bf16[10,16,256]{2,1,0:T(8,128)(2,1)S(1)} %get-tuple-element.26.refs_0_), channel_id=1, source_target_pairs={{0,48},{16,0},{32,16},{48,32},{64,112},{80,64},{96,80},{112,96},{1... | collective-permute-start | bytes 245768 | tf_op jit(solution)/shard_map/ppermute | solution.py:57
  (5 other events, 5.6 us)

commit v2 on v1

v2 whole, which is shorter than its diff:
```python
import functools

import jax
import jax.numpy as jnp
from jax import lax
from jax.experimental import pallas as pl
from jax.experimental.pallas import tpu as pltpu
from jax.sharding import PartitionSpec as P

epsilon = 1e-06
F32 = jnp.float32
BF16 = jnp.bfloat16
VMEM = pl.BlockSpec(memory_space=pltpu.VMEM)
SMEM = pl.BlockSpec(memory_space=pltpu.SMEM)
ANY = pl.BlockSpec(memory_space=pl.ANY)
HBM = pl.BlockSpec(memory_space=pltpu.HBM)

NX, NZ, NC = 4, 2, 2
NL, NY = 4, 4


def tile_perm(move):
    place = lambda x, z, c: (x * NZ + z) * NC + c
    return [
        (place(x, z, c), place(*move(x, z, c)))
        for x in range(NX)
        for z in range(NZ)
        for c in range(NC)
    ]


def img_perm(move):
    place = lambda l, y: l * NY + y
    return [(place(l, y), place(*move(l, y))) for l in range(NL) for y in range(NY)]


def swap_core(a):
    return lax.ppermute(a, "tile", tile_perm(lambda x, z, c: (x, z, 1 - c)))


def swap_z(a):
    return lax.ppermute(a, "tile", tile_perm(lambda x, z, c: (x, 1 - z, c)))


def shift_x(a, k):
    return lax.ppermute(a, "tile", tile_perm(lambda x, z, c: ((x + k) % NX, z, c)))


def flip_x(a, k):
    return lax.ppermute(a, "tile", tile_perm(lambda x, z, c: (x ^ k, z, c)))


def flip_l(a, k):
    return lax.ppermute(a, "img", img_perm(lambda l, y: (l ^ k, y)))


def shift_y(a, k):
    return lax.ppermute(a, "img", img_perm(lambda l, y: (l, (y + k) % NY)))


def call(body, outs, in_specs, scratch=(), flops=0, nbytes=0, vmem=16 << 20, name=None):
    return pl.pallas_call(
        body,
        out_shape=outs,
        in_specs=in_specs,
        out_specs=jax.tree.map(lambda _: VMEM, outs),
        scratch_shapes=list(scratch),
        compiler_params=pltpu.CompilerParams(vmem_limit_bytes=vmem),
        cost_estimate=pl.CostEstimate(flops=flops, bytes_accessed=nbytes, transcendentals=0),
        name=name,
    )


def shape(s, dtype):
    return jax.ShapeDtypeStruct(s, dtype)


def demod_of(kernel, style):
    total = None
    for t in range(kernel.shape[0]):
        modded = kernel[t] * style
        total = modded * modded if total is None else total + modded * modded
    return lax.rsqrt(jnp.sum(total, axis=1, keepdims=True) + epsilon)


def fetch(copies):
    for copy in copies:
        copy.start()
    for copy in copies:
        copy.wait()


def rows_body(cot, last, first, sems):
    fetch(
        [
            pltpu.make_async_copy(cot.at[cot.shape[0] - 1], last, sems.at[0]),
            pltpu.make_async_copy(cot.at[0], first, sems.at[1]),
        ]
    )


def mix_body(sel, style, bank, after, kernel, final):
    del after
    banks, taps = bank.shape[:2]
    top = sel.shape[1]
    weights = []
    for k in range(banks):
        w = F32(0)
        for j in range(top):
            w = w + jnp.where(sel[0, j] == k, F32((top - j) / (top * (top + 1) / 2)), F32(0))
        weights.append(w)
    for t in range(taps):
        mixed = None
        for k in range(banks):
            term = weights[k] * bank[k, t].astype(F32)
            mixed = term if mixed is None else mixed + term
        kernel[t] = mixed
    demod = demod_of(kernel, style[...])
    for t in range(taps):
        final[t] = (kernel[t] * style[...] * demod).astype(BF16)


def moved_columns(row):
    width = row.shape[0]
    column = lax.broadcasted_iota(jnp.int32, row.shape, 0)
    before = jnp.where(column == 0, F32(0), pltpu.roll(row, 1, 0))
    after = jnp.where(column == width - 1, F32(0), pltpu.roll(row, width - 1, 0))
    return before, after


def turned(row, core, out, at):
    width, channels = row.shape
    groups = channels // (16 * NC)
    flat = jnp.transpose(row)
    for g in range(groups):
        for c in range(NC):
            start = (g * NC + c) * 16
            out[c ^ core, g, :, at] = flat[start : start + 16]


def grad_body(place, cot_hbm, fm_hbm, grad, cot, fm, cot_t, fm_v, sems, step=4):
    rows, width, channels = cot.shape
    groups = channels // (16 * NC)
    core = place[2]
    parts = rows // step
    copies = []
    for q in range(parts):
        here = pl.ds(q * step, step)
        copies.append(
            (
                pltpu.make_async_copy(cot_hbm.at[here], cot.at[here], sems.at[0, q]),
                pltpu.make_async_copy(fm_hbm.at[here], fm.at[here], sems.at[1, q]),
            )
        )
    for pair in copies:
        for copy in pair:
            copy.start()
    nothing = jnp.zeros((NC, groups, 16, width), BF16)
    cot_t[:, :, :, :width] = nothing
    cot_t[:, :, :, (rows + 1) * width :] = nothing

    def prepare(q):
        for copy in copies[q]:
            copy.wait()
        for r in range(q * step, (q + 1) * step):
            row = fm[r]
            before, after = moved_columns(row.astype(F32))
            here = pl.ds(r * width, width)
            fm_v[0, here] = before.astype(BF16)
            fm_v[1, here] = row
            fm_v[2, here] = after.astype(BF16)
            turned(cot[r], core, cot_t, pl.ds((r + 1) * width, width))

    def add(q):
        for u in range(3):
            left = cot_t[:, :, :, pl.ds((q * step + 2 - u) * width, step * width)]
            left = left.reshape(channels, step * width)
            for v in range(3):
                right = fm_v[v, pl.ds(q * step * width, step * width)]
                out = jnp.dot(left, right, preferred_element_type=F32)
                out = out.reshape(NC, groups, 16, channels)
                grad[3 * u + v] = out if q == 0 else grad[3 * u + v] + out

    prepare(0)
    for q in range(parts):
        if q + 1 < parts:
            prepare(q + 1)
        add(q)


def edge_body(place, grad, low, high, fm, after, mine, theirs, turn_low, turn_high, first, last, sems):
    del after
    taps, _, groups, _, channels = grad.shape
    copies = [
        pltpu.make_async_copy(fm.at[0], first, sems.at[0]),
        pltpu.make_async_copy(fm.at[fm.shape[0] - 1], last, sems.at[1]),
    ]
    for copy in copies:
        copy.start()
    width = low.shape[0]
    core = place[2]
    turned(low[...], core, turn_low, pl.ds(0, width))
    turned(high[...], core, turn_high, pl.ds(0, width))

    def put(t, value):
        for g in range(groups):
            mine[g, t] = value[0, g]
            theirs[g, t] = value[1, g].astype(BF16)

    for t in (3, 4, 5):
        put(t, grad[t])
    for copy in copies:
        copy.wait()
    for turn, row, tap in ((turn_high, last, 0), (turn_low, first, 6)):
        whole = row[...].reshape(width, channels)
        before, after = moved_columns(whole.astype(F32))
        left = turn[...].reshape(channels, width)
        for v, right in enumerate((before.astype(BF16), whole, after.astype(BF16))):
            out = jnp.dot(left, right, preferred_element_type=F32)
            put(tap + v, grad[tap + v] + out.reshape(NC, groups, 16, channels))


def split_x_body(place, mine, got, final, final_c, own, one, two, three, both):
    both[0] = final[...]
    both[1] = final_c[...]
    x = place[0]
    for k, out in ((0, own), (1, one), (2, two), (3, three)):
        base = lax.rem(x + k, NX) * NZ
        for z in range(NZ):
            out[z] = (mine[base + z] + got[base + z].astype(F32)).astype(out.dtype)


def split_z_body(place, mine, one, two, three, total, other):
    z = place[1]
    for k in range(NZ):
        at = z ^ k
        value = mine[at] + one[at].astype(F32) + two[at].astype(F32) + three[at].astype(F32)
        total[k] = value
        if k == 1:
            other[...] = value.astype(BF16)


def style_body(style, total, near, got, part, four):
    taps, outs, channels = total.shape[1:]
    share = jnp.zeros((outs, channels), F32)
    for k, source in enumerate((near, got)):
        dot = jnp.zeros((outs, channels), F32)
        for t in range(taps):
            dot = dot + total[k, t] * source[0, t].astype(F32)
        dot = jnp.sum(dot, axis=1, keepdims=True)
        for t in range(taps):
            final = source[0, t].astype(F32)
            share = share + (total[k, t] - final * dot) * final
    row = jnp.sum(share, axis=0, keepdims=True) / style[...]
    part[...] = jnp.broadcast_to(row, part.shape)
    four[pl.ds(0, NC)] = near[...]
    four[pl.ds(NC, NC)] = got[...]


def owner_body(sel, style, kernel, total, got, message):
    taps, outs, channels = kernel.shape
    top = sel.shape[1]
    s = style[...]
    demod = demod_of(kernel, s)
    dot = jnp.zeros((outs, channels), F32)
    for t in range(taps):
        grad = total[0, t] + got[t].astype(F32)
        dot = dot + grad * (kernel[t] * s)
    curvature = jnp.sum(dot, axis=1, keepdims=True)
    slope = demod * demod * demod * curvature
    for t in range(taps):
        grad = total[0, t] + got[t].astype(F32)
        modded_grad = demod * grad - slope * (kernel[t] * s)
        message[t] = (modded_grad * s).astype(BF16)
    bank = lax.broadcasted_iota(jnp.int32, (outs, channels), 0)
    rank = jnp.zeros((outs, channels), F32)
    for j in range(top):
        rank = rank + jnp.where(bank == sel[0, j], F32(top - j), F32(0))
    message[taps] = rank.astype(BF16)


def ahead_body(one, two, three, out):
    for k, piece in enumerate((one, two, three)):
        out[k] = piece[...]


def banks_body(*refs):
    out, both, sems = refs[-3:]
    banks, taps, outs, channels = out.shape
    pieces = []
    for ref in refs[:-3]:
        if len(ref.shape) == 3:
            pieces.append(ref)
        else:
            pieces.extend(ref.at[n] for n in range(ref.shape[0]))
    lane = lax.broadcasted_iota(jnp.int32, (outs, channels), 1)
    row = lax.broadcasted_iota(jnp.int32, (outs, channels), 0)
    ranks = jnp.zeros((outs, channels), F32)
    for n, piece in enumerate(pieces):
        ranks = jnp.where(lane // outs == n, piece[taps].astype(F32), ranks)
    left = jnp.concatenate(
        [jnp.where(lane % outs == row, ranks[k : k + 1], F32(0)) for k in range(banks)], axis=0
    ).astype(BF16)
    copies = []
    for t in range(taps):
        right = jnp.concatenate([piece[t] for piece in pieces], axis=0)
        total = jnp.dot(left, right, preferred_element_type=F32) / F32(6)
        both[:, t] = total.reshape(banks, outs, channels)
        copy = pltpu.make_async_copy(both.at[:, t], out.at[:, t], sems.at[t])
        copy.start()
        copies.append(copy)
    for copy in copies:
        copy.wait()


def input_body(place, *refs):
    finals = refs[:NX]
    low, high, cot, after, out, final, padded, sem = refs[NX:]
    del after
    rows, width, channels = out.shape
    copy = pltpu.make_async_copy(cot, padded.at[pl.ds(1, rows)], sem)
    copy.start()
    padded[0] = low[...]
    padded[rows + 1] = high[...]
    x, z, core = place[0], place[1], place[2]
    for k in range(NX):
        for n in range(NZ):
            for c in range(NC):
                at = (lax.rem(x + NX - k, NX) * NZ + (z ^ n)) * NC + (core ^ c)
                here = pl.ds(pl.multiple_of(at * 16, 16), 16)
                for t in range(9):
                    u, v = t // 3, t % 3
                    final[u, here, v * channels : (v + 1) * channels] = finals[k][n * NC + c, t]
    copy.wait()
    step = 2

    @pl.loop(0, rows // step)
    def _(q):
        r = q * step
        left = jnp.concatenate(
            [padded[pl.ds(r + 2 - u, step)].reshape(step * width, channels) for u in range(3)], axis=1
        )
        right = final[...].reshape(3 * channels, 3 * channels)
        sums = jnp.dot(left, right, preferred_element_type=F32)
        for n in range(step):
            part = sums[n * width : (n + 1) * width]
            _, after = moved_columns(part[:, :channels])
            before, _ = moved_columns(part[:, 2 * channels :])
            out[r + n] = (part[:, channels : 2 * channels] + after + before).astype(BF16)


def local(feature_map, cotangent, style, bank, selection):
    _, rows, width, channels = feature_map.shape
    fm = feature_map.reshape(rows, width, channels)
    cot = cotangent.reshape(rows, width, channels)
    banks, own_out, taps, _ = bank.shape
    groups = NX * NZ
    tile = lax.axis_index("tile")
    place = jnp.stack([tile // (NZ * NC), (tile // NC) % NZ, tile % NC]).astype(jnp.int32)
    dma = pltpu.SemaphoreType.DMA
    piece = (taps, own_out, channels)
    pair = (NZ,) + piece

    last, first = call(
        rows_body, (shape((width, channels), BF16),) * 2, [HBM], [dma((2,))], nbytes=10**6, vmem=60 << 20, name="rows"
    )(cot)
    count = lax.axis_size("tile")
    low = lax.ppermute(last, "tile", [(i, i + 1) for i in range(count - 1)])
    high = lax.ppermute(first, "tile", [(i + 1, i) for i in range(count - 1)])

    kernel, final = call(
        mix_body, (shape(piece, F32), shape(piece, BF16)), [SMEM, VMEM, VMEM, VMEM], flops=10**6, nbytes=10**6, name="mix"
    )(selection, style, jnp.transpose(bank, (0, 2, 1, 3)), last)
    final_c = swap_core(final)

    grad = call(
        grad_body,
        shape((taps, NC, groups, 16, channels), F32),
        [SMEM, HBM, HBM],
        [
            pltpu.VMEM((rows, width, channels), BF16),
            pltpu.VMEM((rows, width, channels), BF16),
            pltpu.VMEM((NC, groups, 16, (rows + 2) * width), BF16),
            pltpu.VMEM((3, rows * width, channels), BF16),
            dma((2, 4)),
        ],
        flops=2 * 9 * rows * width * channels * channels,
        nbytes=4 * rows * width * channels,
        vmem=50 << 20,
        name="grad",
    )(place, cot, fm)
    mine, theirs = call(
        edge_body,
        (shape((groups,) + piece, F32), shape((groups,) + piece, BF16)),
        [SMEM] + [VMEM] * 3 + [HBM, VMEM],
        [pltpu.VMEM((NC, groups, 16, width), BF16)] * 2 + [pltpu.VMEM((width, channels), BF16)] * 2 + [dma((2,))],
        flops=2 * 6 * width * channels * channels,
        nbytes=4 * 10**6,
        vmem=50 << 20,
        name="edge",
    )(place, grad, low, high, fm, final_c)

    own_x, one, two, three, both = call(
        split_x_body,
        (shape(pair, F32),) + (shape(pair, BF16),) * 3 + (shape((NC,) + piece, BF16),),
        [SMEM] + [VMEM] * 4,
        flops=10**6,
        nbytes=3 * 10**6,
        name="split_x",
    )(place, mine, swap_core(theirs), final, final_c)
    got_z = swap_z(both)
    total, other = call(
        split_z_body,
        (shape(pair, F32), shape(piece, BF16)),
        [SMEM] + [VMEM] * 4,
        flops=10**6,
        nbytes=10**6,
        name="split_z",
    )(place, own_x, shift_x(one, 1), shift_x(two, 2), shift_x(three, 3))
    message = call(
        owner_body,
        shape((taps + 1, own_out, channels), BF16),
        [SMEM] + [VMEM] * 4,
        flops=10**6,
        nbytes=10**6,
        name="owner",
    )(selection, style, kernel, total, swap_z(other))
    style_part, four = call(
        style_body,
        (shape((8, channels), F32), shape((NZ * NC,) + piece, BF16)),
        [VMEM] * 4,
        flops=10**9,
        nbytes=10**7,
        name="style",
    )(style, total, both, got_z)

    finals = [four] + [shift_x(four, k) for k in range(1, NX)]

    over_l = [flip_l(message, k) for k in range(1, NL)]
    over_y = [shift_y(message, k) for k in range(1, NY)]
    ahead = call(ahead_body, shape((3, taps + 1, own_out, channels), BF16), [VMEM] * 3, name="ahead")(*over_l)
    rest = [shift_y(ahead, k) for k in range(1, NY)]

    style_sum = style_part + swap_core(style_part)
    style_sum = style_sum + flip_x(style_sum, 1)
    style_sum = style_sum + flip_x(style_sum, 2)
    style_sum = style_sum + swap_z(style_sum)

    input_grad = call(
        input_body,
        shape((rows, width, channels), BF16),
        [SMEM] + [VMEM] * (NX + 2) + [HBM, VMEM],
        [
            pltpu.VMEM((3, channels, 3 * channels), BF16),
            pltpu.VMEM((rows + 2, width, channels), BF16),
            dma,
        ],
        flops=2 * 9 * rows * width * channels * channels,
        nbytes=4 * rows * width * channels,
        vmem=50 << 20,
        name="input",
    )(place, *finals, low, high, cot, ahead)

    bank_grad = pl.pallas_call(
        banks_body,
        out_shape=shape((banks,) + piece, F32),
        in_specs=[VMEM] * 10,
        out_specs=HBM,
        scratch_shapes=[pltpu.VMEM((banks,) + piece, F32), dma((taps,))],
        compiler_params=pltpu.CompilerParams(vmem_limit_bytes=16 << 20),
        cost_estimate=pl.CostEstimate(flops=10**7, bytes_accessed=3 * 10**6, transcendentals=0),
        name="banks",
    )(message, *over_l, *over_y, *rest)

    return (
        input_grad.reshape(feature_map.shape),
        style_sum[:1],
        jnp.transpose(bank_grad, (0, 2, 1, 3)),
    )


def solution(mesh):
    in_specs = (
        P("img", "tile", None, None),
        P("img", "tile", None, None),
        P("img", None),
        P(None, "tile", None, None),
        P("img", None),
    )
    out_specs = (P("img", "tile", None, None), P("img", None), P(None, "tile", None, None))
    return jax.shard_map(local, mesh=mesh, in_specs=in_specs, out_specs=out_specs, check_vma=False)
```

time: 119 us -> 95.8 us (0.81); the launches traced: 117 us -> 95.5 us
  waiting for transfers between devices: 18.3 us -> 8.98 us
  local copies, waits for them, and re-layouts: 9.29 us -> 1.98 us
  starting transfers between devices: 62.1 us -> 55.3 us
  Pallas kernels: 25.4 us -> 27.6 us
    ppermute x9 -> x6, starting transfers between devices: 22.1 us -> 10.2 us  [shift_x(): lax.ppermute(a, 'tile', tile_perm(lambda x, z, c: ((x + k) % NX, z, c)))]
    ppermute x3, starting transfers between devices: 0.37 us -> 8.39 us  [swap_core(): return lax.ppermute(a, 'tile', tile_perm(lambda x, z, c: (x, z, 1 - c)))]
    ppermute x9 -> x6, waiting for transfers between devices: 6.04 us -> 0.02 us  [shift_x(): lax.ppermute(a, 'tile', tile_perm(lambda x, z, c: ((x + k) % NX, z, c)))]
    unnamed x25 -> x10, local copies, waits for them, and re-layouts: 7.3 us -> 1.98 us
    ppermute x6, waiting for transfers between devices: 3.22 us -> 0.02 us  [shift_y(): return lax.ppermute(a, 'img', img_perm(lambda l, y: (l, (y + k) % NY)))]
    ppermute x3, waiting for transfers between devices: 0.01 us -> 2.96 us  [flip_l(): return lax.ppermute(a, 'img', img_perm(lambda l, y: (l ^ k, y)))]
    pallas_call x1, Pallas kernels: 0.97 us -> 3.06 us  [local(): call(edge_body, (shape((groups,) + piece, F32), shape((groups,) + piece,...]
    ppermute x3, starting transfers between devices: 18.8 us -> 16.7 us  [swap_z(): return lax.ppermute(a, 'tile', tile_perm(lambda x, z, c: (x, 1 - z, c)))]
  transfers between devices with their start and end apart: 28 -> 25, of which waited for: 10 -> 5; matrix products, arithmetic and copies ran while one was open for 2% -> 1% of each run, Pallas kernels for 19% -> 22%
where the time goes in v2:
time: 95.8 us; the launch traced here: 95.5 us
  starting transfers between devices  55.3 us (58%)
  Pallas kernels  27.6 us (29%)
  waiting for transfers between devices  8.98 us (9%)
  local copies, waits for them, and re-layouts  1.98 us (2%)
  between operations  1.01 us (1%)
    ppermute x3, starting transfers between devices, swap_z(): return lax.ppermute(a, 'tile', tile_perm(lambda x, z, c: (x, 1 - z, c)))  16.7 us
    ppermute x6, starting transfers between devices, shift_x(): lax.ppermute(a, 'tile', tile_perm(lambda x, z, c: ((x + k) % NX, z, c)))  10.2 us
    pallas_call x1, Pallas kernels, local(): call(grad_body, shape((taps, NC, groups, 16, channels), F32), [SMEM, HBM,...  10.1 us
    ppermute x6, starting transfers between devices, shift_y(): return lax.ppermute(a, 'img', img_perm(lambda l, y: (l, (y + k) % NY)))  9.24 us
    pallas_call x1, Pallas kernels, local(): call(input_body, shape((rows, width, channels), BF16), [SMEM] + [VMEM] *...  8.4 us
    ppermute x3, starting transfers between devices, swap_core(): return lax.ppermute(a, 'tile', tile_perm(lambda x, z, c: (x, z, 1 - c)))  8.39 us
    ppermute x2, starting transfers between devices, flip_x(): return lax.ppermute(a, 'tile', tile_perm(lambda x, z, c: (x ^ k, z, c)))  3.99 us
    ppermute x3, starting transfers between devices, flip_l(): return lax.ppermute(a, 'img', img_perm(lambda l, y: (l ^ k, y)))  3.72 us
  transfers between devices with their start and end apart: 25, of which 5 were waited for; matrix products, arithmetic and copies ran while one was open for 1% of the time, Pallas kernels for 22%

profile of v2, /device:TPU:8, one launch (start us, length us, event | category | flops | bytes accessed | tf_op | source)
XLA Modules:
  0.0 95.5 jit_solution(1628323839932316572)
XLA Ops:
  0.7 1.8 %rows.1 = (bf16[256,256]{1,0:T(8,128)(2,1)}, bf16[256,256]{1,0:T(8,128)(2,1)}) custom-call(bf16[16,256,256]{2,1,0:T(8,128)(2,1)} %bitcast.8), custom_call_target="tpu_custom_call" | custom-call | bytes 1000000 | tf_op jit(solution)/shard_map/rows/pallas_call | solution.py:364
  2.5 1.7 %collective-permute-start = (bf16[256,256]{1,0:T(8,128)(2,1)}, bf16[256,256]{1,0:T(8,128)(2,1)S(1)}, u32[]{:S(2)}, u32[]{:S(2)}) collective-permute-start(bf16[256,256]{1,0:T(8,128)(2,1)} %get-tuple-element.18.after), channel_id=1, source_target_pairs={{0,1},{1,2},{2,3},{3,4},{4,5},{5,6},{6,7},{7,8},{8,9},{9,10},{10,1... | collective-permute-start | bytes 393224 | tf_op jit(solution)/shard_map/ppermute | solution.py:368
  4.2 1.3 %collective-permute-start.1 = (bf16[256,256]{1,0:T(8,128)(2,1)}, bf16[256,256]{1,0:T(8,128)(2,1)S(1)}, u32[]{:S(2)}, u32[]{:S(2)}) collective-permute-start(bf16[256,256]{1,0:T(8,128)(2,1)} %get-tuple-element.19), channel_id=1, source_target_pairs={{1,0},{2,1},{3,2},{4,3},{5,4},{6,5},{7,6},{8,7},{9,8},{10,9},{11,1... | collective-permute-start | bytes 393224 | tf_op jit(solution)/shard_map/ppermute | solution.py:369
  5.6 1.1 %copy-done.1 = bf16[8,16,9,256]{3,1,2,0:T(8,128)(2,1)S(1)} copy-done((bf16[8,16,9,256]{3,1,2,0:T(8,128)(2,1)S(1)}, bf16[8,16,9,256]{3,1,2,0:T(8,128)(2,1)}, u32[]{:S(2)}) %copy-start.1) | copy-done | bytes 589848
  6.6 0.9 copy-done.2
  8.3 8.2 %collective-permute-start.2 = (bf16[9,16,256]{2,1,0:T(8,128)(2,1)S(1)}, bf16[9,16,256]{2,1,0:T(8,128)(2,1)S(1)}, u32[]{:S(2)}, u32[]{:S(2)}) collective-permute-start(bf16[9,16,256]{2,1,0:T(8,128)(2,1)S(1)} %get-tuple-element.20.final), channel_id=1, source_target_pairs={{0,1},{1,0},{2,3},{3,2},{4,5},{5,4},{6,7},{7,6},{8,9},{9,8},{10,11... | collective-permute-start | bytes 221192 | tf_op jit(solution)/shard_map/ppermute | solution.py:38
  16.5 10.1 %grad.1 = f32[9,2,8,16,256]{4,3,2,1,0:T(8,128)} custom-call(s32[3]{0:T(128)S(1)} %pad_add_fusion.place, bf16[16,256,256]{2,1,0:T(8,128)(2,1)S(1)} %bitcast.9, bf16[16,256,256]{2,1,0:T(8,128)(2,1)} %bitcast.12), custom_call_target="tpu_custom_call" | custom-call | flops 4831838208 | bytes 4194304 | tf_op jit(solution)/shard_map/grad/pallas_call | solution.py:376
  26.7 3.1 %edge.1 = (f32[8,9,16,256]{3,2,1,0:T(8,128)S(1)}, bf16[8,9,16,256]{3,2,1,0:T(8,128)(2,1)S(1)}) custom-call(s32[3]{0:T(128)S(1)} %pad_add_fusion.place, f32[9,2,8,16,256]{4,3,2,1,0:T(8,128)} %grad.1, bf16[256,256]{1,0:T(8,128)(2,1)S(1)} %collective-permute-done.low.refs_4_, bf16[256,256]{1,0:T(8,128)(2,1)S(1)} %collective-permute-done.1.high.refs_5_, ...), custom_call_target="tpu_custom_call" | custom-call | flops 201326592 | bytes 4000000 | tf_op jit(solution)/shard_map/edge/pallas_call | solution.py:392
  29.9 1.9 %collective-permute-done.3.got = bf16[8,9,16,256]{3,2,1,0:T(8,128)(2,1)S(1)} collective-permute-done((bf16[8,9,16,256]{3,2,1,0:T(8,128)(2,1)S(1)}, bf16[8,9,16,256]{3,2,1,0:T(8,128)(2,1)S(1)}, u32[]{:S(2)}, u32[]{:S(2)}) %collective-permute-start.3) | collective-permute-done | bytes 589856 | tf_op jit(solution)/shard_map/ppermute | solution.py:38
  32.5 1.6 %collective-permute-start.4 = (bf16[2,9,16,256]{3,2,1,0:T(8,128)(2,1)S(1)}, bf16[2,9,16,256]{3,2,1,0:T(8,128)(2,1)S(1)}, u32[]{:S(2)}, u32[]{:S(2)}) collective-permute-start(bf16[2,9,16,256]{3,2,1,0:T(8,128)(2,1)S(1)} %get-tuple-element.24), channel_id=1, source_target_pairs={{0,4},{1,5},{2,6},{3,7},{4,8},{5,9},{6,10},{7,11},{8,12},{9,13},{1... | collective-permute-start | bytes 442376 | tf_op jit(solution)/shard_map/ppermute | solution.py:46
  34.1 2.7 %collective-permute-start.5 = (bf16[2,9,16,256]{3,2,1,0:T(8,128)(2,1)S(1)}, bf16[2,9,16,256]{3,2,1,0:T(8,128)(2,1)S(1)}, u32[]{:S(2)}, u32[]{:S(2)}) collective-permute-start(bf16[2,9,16,256]{3,2,1,0:T(8,128)(2,1)S(1)} %get-tuple-element.25), channel_id=1, source_target_pairs={{0,8},{1,9},{2,10},{3,11},{4,12},{5,13},{6,14},{7,15},{8,0},{9,1},... | collective-permute-start | bytes 442376 | tf_op jit(solution)/shard_map/ppermute | solution.py:46
  36.8 1.4 %collective-permute-start.6 = (bf16[2,9,16,256]{3,2,1,0:T(8,128)(2,1)S(1)}, bf16[2,9,16,256]{3,2,1,0:T(8,128)(2,1)S(1)}, u32[]{:S(2)}, u32[]{:S(2)}) collective-permute-start(bf16[2,9,16,256]{3,2,1,0:T(8,128)(2,1)S(1)} %get-tuple-element.26), channel_id=1, source_target_pairs={{0,12},{1,13},{2,14},{3,15},{4,0},{5,1},{6,2},{7,3},{8,4},{9,5},{1... | collective-permute-start | bytes 442376 | tf_op jit(solution)/shard_map/ppermute | solution.py:46
  38.3 5.7 %collective-permute-start.7 = (bf16[2,9,16,256]{3,2,1,0:T(8,128)(2,1)S(1)}, bf16[2,9,16,256]{3,2,1,0:T(8,128)(2,1)S(1)}, u32[]{:S(2)}, u32[]{:S(2)}) collective-permute-start(bf16[2,9,16,256]{3,2,1,0:T(8,128)(2,1)S(1)} %get-tuple-element.28.near), channel_id=1, source_target_pairs={{0,2},{1,3},{2,0},{3,1},{4,6},{5,7},{6,4},{7,5},{8,10},{9,11},{10,... | collective-permute-start | bytes 442376 | tf_op jit(solution)/shard_map/ppermute | solution.py:42
  44.6 5.9 %collective-permute-start.11 = (bf16[9,16,256]{2,1,0:T(8,128)(2,1)S(1)}, bf16[9,16,256]{2,1,0:T(8,128)(2,1)S(1)}, u32[]{:S(2)}, u32[]{:S(2)}) collective-permute-start(bf16[9,16,256]{2,1,0:T(8,128)(2,1)S(1)} %get-tuple-element.31), channel_id=1, source_target_pairs={{0,2},{1,3},{2,0},{3,1},{4,6},{5,7},{6,4},{7,5},{8,10},{9,11},{10,... | collective-permute-start | bytes 221192 | tf_op jit(solution)/shard_map/ppermute | solution.py:42
  50.7 1.2 %collective-permute-done.15 = f32[8,256]{1,0:T(8,128)S(1)} collective-permute-done((f32[8,256]{1,0:T(8,128)S(1)}, f32[8,256]{1,0:T(8,128)S(1)}, u32[]{:S(2)}, u32[]{:S(2)}) %collective-permute-start.15) | collective-permute-done | bytes 8224 | tf_op jit(solution)/shard_map/ppermute | solution.py:38
  51.9 1.3 %collective-permute-start.16 = (f32[8,256]{1,0:T(8,128)S(1)}, f32[8,256]{1,0:T(8,128)S(1)}, u32[]{:S(2)}, u32[]{:S(2)}) collective-permute-start(f32[8,256]{1,0:T(8,128)S(1)} %add.23), channel_id=1, source_target_pairs={{0,4},{1,5},{2,6},{3,7},{4,0},{5,1},{6,2},{7,3},{8,12},{9,13},{10,... | collective-permute-start | bytes 24584 | tf_op jit(solution)/shard_map/ppermute | solution.py:50
  53.2 2.3 %collective-permute-done.16 = f32[8,256]{1,0:T(8,128)S(1)} collective-permute-done((f32[8,256]{1,0:T(8,128)S(1)}, f32[8,256]{1,0:T(8,128)S(1)}, u32[]{:S(2)}, u32[]{:S(2)}) %collective-permute-start.16) | collective-permute-done | bytes 8224 | tf_op jit(solution)/shard_map/ppermute | solution.py:50
  55.5 2.6 %collective-permute-start.17 = (f32[8,256]{1,0:T(8,128)S(1)}, f32[8,256]{1,0:T(8,128)S(1)}, u32[]{:S(2)}, u32[]{:S(2)}) collective-permute-start(f32[8,256]{1,0:T(8,128)S(1)} %add.24), channel_id=1, source_target_pairs={{0,8},{1,9},{2,10},{3,11},{4,12},{5,13},{6,14},{7,15},{8,0},{9,1},... | collective-permute-start | bytes 24584 | tf_op jit(solution)/shard_map/ppermute | solution.py:50
  58.9 1.1 %collective-permute-start.12 = (bf16[10,16,256]{2,1,0:T(8,128)(2,1)S(1)}, bf16[10,16,256]{2,1,0:T(8,128)(2,1)S(1)}, u32[]{:S(2)}, u32[]{:S(2)}) collective-permute-start(bf16[10,16,256]{2,1,0:T(8,128)(2,1)S(1)} %owner.1.refs_0_), channel_id=1, source_target_pairs={{0,64},{16,80},{32,96},{48,112},{64,0},{80,16},{96,32},{112,48},{1... | collective-permute-start | bytes 245768 | tf_op jit(solution)/shard_map/ppermute | solution.py:54
  60.0 1.5 %collective-permute-start.13 = (bf16[10,16,256]{2,1,0:T(8,128)(2,1)S(1)}, bf16[10,16,256]{2,1,0:T(8,128)(2,1)S(1)}, u32[]{:S(2)}, u32[]{:S(2)}) collective-permute-start(bf16[10,16,256]{2,1,0:T(8,128)(2,1)S(1)} %owner.1.refs_0_), channel_id=1, source_target_pairs={{0,128},{16,144},{32,160},{48,176},{64,192},{80,208},{96,224},{112... | collective-permute-start | bytes 245768 | tf_op jit(solution)/shard_map/ppermute | solution.py:54
  61.5 5.2 %collective-permute-start.18 = (f32[8,256]{1,0:T(8,128)S(1)}, f32[8,256]{1,0:T(8,128)S(1)}, u32[]{:S(2)}, u32[]{:S(2)}) collective-permute-start(f32[8,256]{1,0:T(8,128)S(1)} %add.25), channel_id=1, source_target_pairs={{0,2},{1,3},{2,0},{3,1},{4,6},{5,7},{6,4},{7,5},{8,10},{9,11},{10,... | collective-permute-start | bytes 24584 | tf_op jit(solution)/shard_map/ppermute | solution.py:42
  67.1 1.3 %collective-permute-start.9 = (bf16[4,9,16,256]{3,2,1,0:T(8,128)(2,1)S(1)}, bf16[4,9,16,256]{3,2,1,0:T(8,128)(2,1)S(1)}, u32[]{:S(2)}, u32[]{:S(2)}) collective-permute-start(bf16[4,9,16,256]{3,2,1,0:T(8,128)(2,1)S(1)} %get-tuple-element.29.refs_0_), channel_id=1, source_target_pairs={{0,8},{1,9},{2,10},{3,11},{4,12},{5,13},{6,14},{7,15},{8,0},{9,1},... | collective-permute-start | bytes 884744 | tf_op jit(solution)/shard_map/ppermute | solution.py:46
  69.0 2.6 %collective-permute-start.10 = (bf16[4,9,16,256]{3,2,1,0:T(8,128)(2,1)S(1)}, bf16[4,9,16,256]{3,2,1,0:T(8,128)(2,1)S(1)}, u32[]{:S(2)}, u32[]{:S(2)}) collective-permute-start(bf16[4,9,16,256]{3,2,1,0:T(8,128)(2,1)S(1)} %get-tuple-element.29.refs_0_), channel_id=1, source_target_pairs={{0,12},{1,13},{2,14},{3,15},{4,0},{5,1},{6,2},{7,3},{8,4},{9,5},{1... | collective-permute-start | bytes 884744 | tf_op jit(solution)/shard_map/ppermute | solution.py:46
  71.6 1.1 %collective-permute-start.14 = (bf16[10,16,256]{2,1,0:T(8,128)(2,1)S(1)}, bf16[10,16,256]{2,1,0:T(8,128)(2,1)S(1)}, u32[]{:S(2)}, u32[]{:S(2)}) collective-permute-start(bf16[10,16,256]{2,1,0:T(8,128)(2,1)S(1)} %owner.1.refs_0_), channel_id=1, source_target_pairs={{0,192},{16,208},{32,224},{48,240},{64,128},{80,144},{96,160},{112... | collective-permute-start | bytes 245768 | tf_op jit(solution)/shard_map/ppermute | solution.py:54
  72.8 1.6 %collective-permute-start.19 = (bf16[10,16,256]{2,1,0:T(8,128)(2,1)S(1)}, bf16[10,16,256]{2,1,0:T(8,128)(2,1)S(1)}, u32[]{:S(2)}, u32[]{:S(2)}) collective-permute-start(bf16[10,16,256]{2,1,0:T(8,128)(2,1)S(1)} %owner.1.refs_0_), channel_id=1, source_target_pairs={{0,16},{16,32},{32,48},{48,0},{64,80},{80,96},{96,112},{112,64},{1... | collective-permute-start | bytes 245768 | tf_op jit(solution)/shard_map/ppermute | solution.py:58
  74.9 3.0 %collective-permute-done.14.three.refs_3_ = bf16[10,16,256]{2,1,0:T(8,128)(2,1)S(1)} collective-permute-done((bf16[10,16,256]{2,1,0:T(8,128)(2,1)S(1)}, bf16[10,16,256]{2,1,0:T(8,128)(2,1)S(1)}, u32[]{:S(2)}, u32[]{:S(2)}) %collective-permute-start.14) | collective-permute-done | bytes 81952 | tf_op jit(solution)/shard_map/ppermute | solution.py:54
  77.9 2.3 %collective-permute-start.20 = (bf16[10,16,256]{2,1,0:T(8,128)(2,1)S(1)}, bf16[10,16,256]{2,1,0:T(8,128)(2,1)S(1)}, u32[]{:S(2)}, u32[]{:S(2)}) collective-permute-start(bf16[10,16,256]{2,1,0:T(8,128)(2,1)S(1)} %owner.1.refs_0_), channel_id=1, source_target_pairs={{0,32},{16,48},{32,0},{48,16},{64,96},{80,112},{96,64},{112,80},{1... | collective-permute-start | bytes 245768 | tf_op jit(solution)/shard_map/ppermute | solution.py:58
  80.2 1.4 %collective-permute-start.21 = (bf16[10,16,256]{2,1,0:T(8,128)(2,1)S(1)}, bf16[10,16,256]{2,1,0:T(8,128)(2,1)S(1)}, u32[]{:S(2)}, u32[]{:S(2)}) collective-permute-start(bf16[10,16,256]{2,1,0:T(8,128)(2,1)S(1)} %owner.1.refs_0_), channel_id=1, source_target_pairs={{0,48},{16,0},{32,16},{48,32},{64,112},{80,64},{96,80},{112,96},{1... | collective-permute-start | bytes 245768 | tf_op jit(solution)/shard_map/ppermute | solution.py:58
  82.3 2.4 %collective-permute-start.23 = (bf16[3,10,16,256]{3,2,1,0:T(8,128)(2,1)S(1)}, bf16[3,10,16,256]{3,2,1,0:T(8,128)(2,1)S(1)}, u32[]{:S(2)}, u32[]{:S(2)}) collective-permute-start(bf16[3,10,16,256]{3,2,1,0:T(8,128)(2,1)S(1)} %ahead.1.refs_7_), channel_id=1, source_target_pairs={{0,32},{16,48},{32,0},{48,16},{64,96},{80,112},{96,64},{112,80},{1... | collective-permute-start | bytes 737288 | tf_op jit(solution)/shard_map/ppermute | solution.py:58
  84.8 0.8 collective-permute-start.24
  85.6 8.4 %input.1 = bf16[16,256,256]{2,1,0:T(8,128)(2,1)} custom-call(s32[3]{0:T(128)S(1)} %pad_add_fusion.place, bf16[4,9,16,256]{3,2,1,0:T(8,128)(2,1)S(1)} %get-tuple-element.29.refs_0_, bf16[4,9,16,256]{3,2,1,0:T(8,128)(2,1)S(1)} %collective-permute-done.8.refs_1_, bf16[4,9,16,256]{3,2,1,0:T(8,128)(2,1)S(1)} %collective-permute-done.9.refs_2_, ...), custom_call_target="tpu_custom_call" | custom-call | flops 4831838208 | bytes 4194304 | tf_op jit(solution)/shard_map/input/pallas_call | solution.py:449
  94.0 1.3 %banks.1 = f32[8,9,16,256]{3,2,1,0:T(8,128)} custom-call(bf16[10,16,256]{2,1,0:T(8,128)(2,1)S(1)} %owner.1.refs_0_, bf16[10,16,256]{2,1,0:T(8,128)(2,1)S(1)} %collective-permute-done.12.one.refs_1_, bf16[10,16,256]{2,1,0:T(8,128)(2,1)S(1)} %collective-permute-done.13.two.refs_2_, bf16[10,16,256]{2,1,0:T(8,128)(2,1)S(1)} %collective-permute-done.14.three.refs_3_, ...), custom_call_target="tpu_custom_call" | custom-call | flops 10000000 | bytes 3000000 | tf_op jit(solution)/shard_map/banks/pallas_call | solution.py:464
  (44 shorter events, 5.6 us)
Async XLA Ops:
  0.6 15.9 %copy-start = (bf16[1,16,256,256]{3,2,1,0:T(8,128)(2,1)S(1)}, bf16[1,16,256,256]{3,2,1,0:T(8,128)(2,1)}, u32[]{:S(2)}) copy-start(bf16[1,16,256,256]{3,2,1,0:T(8,128)(2,1)} %param.6) | copy-start | bytes 6291460
  0.6 4.9 %copy-start.3 = (f32[1,256]{1,0:T(1,128)S(1)}, f32[1,256]{1,0:T(1,128)}, u32[]{:S(2)}) copy-start(f32[1,256]{1,0:T(1,128)} %style.7) | copy-start | bytes 3076
  0.7 4.9 %copy-start.4 = (s32[1,3]{1,0:T(1,128)S(1)}, s32[1,3]{1,0:T(1,128)}, u32[]{:S(2)}) copy-start(s32[1,3]{1,0:T(1,128)} %sel.3) | copy-start | bytes 40
  2.5 24.2 %collective-permute-start = (bf16[256,256]{1,0:T(8,128)(2,1)}, bf16[256,256]{1,0:T(8,128)(2,1)S(1)}, u32[]{:S(2)}, u32[]{:S(2)}) collective-permute-start(bf16[256,256]{1,0:T(8,128)(2,1)} %get-tuple-element.18.after), channel_id=1, source_target_pairs={{0,1},{1,2},{2,3},{3,4},{4,5},{5,6},{6,7},{7,8},{8,9},{9,10},{10,1... | collective-permute-start | bytes 393224 | tf_op jit(solution)/shard_map/ppermute | solution.py:368
  4.2 22.4 %collective-permute-start.1 = (bf16[256,256]{1,0:T(8,128)(2,1)}, bf16[256,256]{1,0:T(8,128)(2,1)S(1)}, u32[]{:S(2)}, u32[]{:S(2)}) collective-permute-start(bf16[256,256]{1,0:T(8,128)(2,1)} %get-tuple-element.19), channel_id=1, source_target_pairs={{1,0},{2,1},{3,2},{4,3},{5,4},{6,5},{7,6},{8,7},{9,8},{10,9},{11,1... | collective-permute-start | bytes 393224 | tf_op jit(solution)/shard_map/ppermute | solution.py:369
  5.6 1.1 %copy-start.1 = (bf16[8,16,9,256]{3,1,2,0:T(8,128)(2,1)S(1)}, bf16[8,16,9,256]{3,1,2,0:T(8,128)(2,1)}, u32[]{:S(2)}) copy-start(bf16[8,16,9,256]{3,1,2,0:T(8,128)(2,1)} %param.8) | copy-start | bytes 1769476
  6.6 0.9 copy-start.2
  8.3 18.4 %collective-permute-start.2 = (bf16[9,16,256]{2,1,0:T(8,128)(2,1)S(1)}, bf16[9,16,256]{2,1,0:T(8,128)(2,1)S(1)}, u32[]{:S(2)}, u32[]{:S(2)}) collective-permute-start(bf16[9,16,256]{2,1,0:T(8,128)(2,1)S(1)} %get-tuple-element.20.final), channel_id=1, source_target_pairs={{0,1},{1,0},{2,3},{3,2},{4,5},{5,4},{6,7},{7,6},{8,9},{9,8},{10,11... | collective-permute-start | bytes 221192 | tf_op jit(solution)/shard_map/ppermute | solution.py:38
  29.8 2.1 %collective-permute-start.3 = (bf16[8,9,16,256]{3,2,1,0:T(8,128)(2,1)S(1)}, bf16[8,9,16,256]{3,2,1,0:T(8,128)(2,1)S(1)}, u32[]{:S(2)}, u32[]{:S(2)}) collective-permute-start(bf16[8,9,16,256]{3,2,1,0:T(8,128)(2,1)S(1)} %get-tuple-element.22), channel_id=1, source_target_pairs={{0,1},{1,0},{2,3},{3,2},{4,5},{5,4},{6,7},{7,6},{8,9},{9,8},{10,11... | collective-permute-start | bytes 1769480 | tf_op jit(solution)/shard_map/ppermute | solution.py:38
  32.5 11.4 %collective-permute-start.4 = (bf16[2,9,16,256]{3,2,1,0:T(8,128)(2,1)S(1)}, bf16[2,9,16,256]{3,2,1,0:T(8,128)(2,1)S(1)}, u32[]{:S(2)}, u32[]{:S(2)}) collective-permute-start(bf16[2,9,16,256]{3,2,1,0:T(8,128)(2,1)S(1)} %get-tuple-element.24), channel_id=1, source_target_pairs={{0,4},{1,5},{2,6},{3,7},{4,8},{5,9},{6,10},{7,11},{8,12},{9,13},{1... | collective-permute-start | bytes 442376 | tf_op jit(solution)/shard_map/ppermute | solution.py:46
  34.1 9.8 %collective-permute-start.5 = (bf16[2,9,16,256]{3,2,1,0:T(8,128)(2,1)S(1)}, bf16[2,9,16,256]{3,2,1,0:T(8,128)(2,1)S(1)}, u32[]{:S(2)}, u32[]{:S(2)}) collective-permute-start(bf16[2,9,16,256]{3,2,1,0:T(8,128)(2,1)S(1)} %get-tuple-element.25), channel_id=1, source_target_pairs={{0,8},{1,9},{2,10},{3,11},{4,12},{5,13},{6,14},{7,15},{8,0},{9,1},... | collective-permute-start | bytes 442376 | tf_op jit(solution)/shard_map/ppermute | solution.py:46
  36.8 7.1 %collective-permute-start.6 = (bf16[2,9,16,256]{3,2,1,0:T(8,128)(2,1)S(1)}, bf16[2,9,16,256]{3,2,1,0:T(8,128)(2,1)S(1)}, u32[]{:S(2)}, u32[]{:S(2)}) collective-permute-start(bf16[2,9,16,256]{3,2,1,0:T(8,128)(2,1)S(1)} %get-tuple-element.26), channel_id=1, source_target_pairs={{0,12},{1,13},{2,14},{3,15},{4,0},{5,1},{6,2},{7,3},{8,4},{9,5},{1... | collective-permute-start | bytes 442376 | tf_op jit(solution)/shard_map/ppermute | solution.py:46
  38.3 12.2 %collective-permute-start.7 = (bf16[2,9,16,256]{3,2,1,0:T(8,128)(2,1)S(1)}, bf16[2,9,16,256]{3,2,1,0:T(8,128)(2,1)S(1)}, u32[]{:S(2)}, u32[]{:S(2)}) collective-permute-start(bf16[2,9,16,256]{3,2,1,0:T(8,128)(2,1)S(1)} %get-tuple-element.28.near), channel_id=1, source_target_pairs={{0,2},{1,3},{2,0},{3,1},{4,6},{5,7},{6,4},{7,5},{8,10},{9,11},{10,... | collective-permute-start | bytes 442376 | tf_op jit(solution)/shard_map/ppermute | solution.py:42
  44.6 13.6 %collective-permute-start.11 = (bf16[9,16,256]{2,1,0:T(8,128)(2,1)S(1)}, bf16[9,16,256]{2,1,0:T(8,128)(2,1)S(1)}, u32[]{:S(2)}, u32[]{:S(2)}) collective-permute-start(bf16[9,16,256]{2,1,0:T(8,128)(2,1)S(1)} %get-tuple-element.31), channel_id=1, source_target_pairs={{0,2},{1,3},{2,0},{3,1},{4,6},{5,7},{6,4},{7,5},{8,10},{9,11},{10,... | collective-permute-start | bytes 221192 | tf_op jit(solution)/shard_map/ppermute | solution.py:42
  50.6 1.3 %collective-permute-start.15 = (f32[8,256]{1,0:T(8,128)S(1)}, f32[8,256]{1,0:T(8,128)S(1)}, u32[]{:S(2)}, u32[]{:S(2)}) collective-permute-start(f32[8,256]{1,0:T(8,128)S(1)} %get-tuple-element.32), channel_id=1, source_target_pairs={{0,1},{1,0},{2,3},{3,2},{4,5},{5,4},{6,7},{7,6},{8,9},{9,8},{10,11... | collective-permute-start | bytes 24584 | tf_op jit(solution)/shard_map/ppermute | solution.py:38
  51.9 3.7 %collective-permute-start.16 = (f32[8,256]{1,0:T(8,128)S(1)}, f32[8,256]{1,0:T(8,128)S(1)}, u32[]{:S(2)}, u32[]{:S(2)}) collective-permute-start(f32[8,256]{1,0:T(8,128)S(1)} %add.23), channel_id=1, source_target_pairs={{0,4},{1,5},{2,6},{3,7},{4,0},{5,1},{6,2},{7,3},{8,12},{9,13},{10,... | collective-permute-start | bytes 24584 | tf_op jit(solution)/shard_map/ppermute | solution.py:50
  55.5 5.9 %collective-permute-start.17 = (f32[8,256]{1,0:T(8,128)S(1)}, f32[8,256]{1,0:T(8,128)S(1)}, u32[]{:S(2)}, u32[]{:S(2)}) collective-permute-start(f32[8,256]{1,0:T(8,128)S(1)} %add.24), channel_id=1, source_target_pairs={{0,8},{1,9},{2,10},{3,11},{4,12},{5,13},{6,14},{7,15},{8,0},{9,1},... | collective-permute-start | bytes 24584 | tf_op jit(solution)/shard_map/ppermute | solution.py:50
  58.9 12.8 %collective-permute-start.12 = (bf16[10,16,256]{2,1,0:T(8,128)(2,1)S(1)}, bf16[10,16,256]{2,1,0:T(8,128)(2,1)S(1)}, u32[]{:S(2)}, u32[]{:S(2)}) collective-permute-start(bf16[10,16,256]{2,1,0:T(8,128)(2,1)S(1)} %owner.1.refs_0_), channel_id=1, source_target_pairs={{0,64},{16,80},{32,96},{48,112},{64,0},{80,16},{96,32},{112,48},{1... | collective-permute-start | bytes 245768 | tf_op jit(solution)/shard_map/ppermute | solution.py:54
  60.0 12.8 %collective-permute-start.13 = (bf16[10,16,256]{2,1,0:T(8,128)(2,1)S(1)}, bf16[10,16,256]{2,1,0:T(8,128)(2,1)S(1)}, u32[]{:S(2)}, u32[]{:S(2)}) collective-permute-start(bf16[10,16,256]{2,1,0:T(8,128)(2,1)S(1)} %owner.1.refs_0_), channel_id=1, source_target_pairs={{0,128},{16,144},{32,160},{48,176},{64,192},{80,208},{96,224},{112... | collective-permute-start | bytes 245768 | tf_op jit(solution)/shard_map/ppermute | solution.py:54
  61.5 7.6 %collective-permute-start.18 = (f32[8,256]{1,0:T(8,128)S(1)}, f32[8,256]{1,0:T(8,128)S(1)}, u32[]{:S(2)}, u32[]{:S(2)}) collective-permute-start(f32[8,256]{1,0:T(8,128)S(1)} %add.25), channel_id=1, source_target_pairs={{0,2},{1,3},{2,0},{3,1},{4,6},{5,7},{6,4},{7,5},{8,10},{9,11},{10,... | collective-permute-start | bytes 24584 | tf_op jit(solution)/shard_map/ppermute | solution.py:42
  66.6 15.0 %collective-permute-start.8 = (bf16[4,9,16,256]{3,2,1,0:T(8,128)(2,1)S(1)}, bf16[4,9,16,256]{3,2,1,0:T(8,128)(2,1)S(1)}, u32[]{:S(2)}, u32[]{:S(2)}) collective-permute-start(bf16[4,9,16,256]{3,2,1,0:T(8,128)(2,1)S(1)} %get-tuple-element.29.refs_0_), channel_id=1, source_target_pairs={{0,4},{1,5},{2,6},{3,7},{4,8},{5,9},{6,10},{7,11},{8,12},{9,13},{1... | collective-permute-start | bytes 884744 | tf_op jit(solution)/shard_map/ppermute | solution.py:46
  67.1 15.2 %collective-permute-start.9 = (bf16[4,9,16,256]{3,2,1,0:T(8,128)(2,1)S(1)}, bf16[4,9,16,256]{3,2,1,0:T(8,128)(2,1)S(1)}, u32[]{:S(2)}, u32[]{:S(2)}) collective-permute-start(bf16[4,9,16,256]{3,2,1,0:T(8,128)(2,1)S(1)} %get-tuple-element.29.refs_0_), channel_id=1, source_target_pairs={{0,8},{1,9},{2,10},{3,11},{4,12},{5,13},{6,14},{7,15},{8,0},{9,1},... | collective-permute-start | bytes 884744 | tf_op jit(solution)/shard_map/ppermute | solution.py:46
  69.0 15.8 %collective-permute-start.10 = (bf16[4,9,16,256]{3,2,1,0:T(8,128)(2,1)S(1)}, bf16[4,9,16,256]{3,2,1,0:T(8,128)(2,1)S(1)}, u32[]{:S(2)}, u32[]{:S(2)}) collective-permute-start(bf16[4,9,16,256]{3,2,1,0:T(8,128)(2,1)S(1)} %get-tuple-element.29.refs_0_), channel_id=1, source_target_pairs={{0,12},{1,13},{2,14},{3,15},{4,0},{5,1},{6,2},{7,3},{8,4},{9,5},{1... | collective-permute-start | bytes 884744 | tf_op jit(solution)/shard_map/ppermute | solution.py:46
  71.6 6.2 %collective-permute-start.14 = (bf16[10,16,256]{2,1,0:T(8,128)(2,1)S(1)}, bf16[10,16,256]{2,1,0:T(8,128)(2,1)S(1)}, u32[]{:S(2)}, u32[]{:S(2)}) collective-permute-start(bf16[10,16,256]{2,1,0:T(8,128)(2,1)S(1)} %owner.1.refs_0_), channel_id=1, source_target_pairs={{0,192},{16,208},{32,224},{48,240},{64,128},{80,144},{96,160},{112... | collective-permute-start | bytes 245768 | tf_op jit(solution)/shard_map/ppermute | solution.py:54
  72.8 7.4 %collective-permute-start.19 = (bf16[10,16,256]{2,1,0:T(8,128)(2,1)S(1)}, bf16[10,16,256]{2,1,0:T(8,128)(2,1)S(1)}, u32[]{:S(2)}, u32[]{:S(2)}) collective-permute-start(bf16[10,16,256]{2,1,0:T(8,128)(2,1)S(1)} %owner.1.refs_0_), channel_id=1, source_target_pairs={{0,16},{16,32},{32,48},{48,0},{64,80},{80,96},{96,112},{112,64},{1... | collective-permute-start | bytes 245768 | tf_op jit(solution)/shard_map/ppermute | solution.py:58
  77.9 16.1 %collective-permute-start.20 = (bf16[10,16,256]{2,1,0:T(8,128)(2,1)S(1)}, bf16[10,16,256]{2,1,0:T(8,128)(2,1)S(1)}, u32[]{:S(2)}, u32[]{:S(2)}) collective-permute-start(bf16[10,16,256]{2,1,0:T(8,128)(2,1)S(1)} %owner.1.refs_0_), channel_id=1, source_target_pairs={{0,32},{16,48},{32,0},{48,16},{64,96},{80,112},{96,64},{112,80},{1... | collective-permute-start | bytes 245768 | tf_op jit(solution)/shard_map/ppermute | solution.py:58
  80.2 13.8 %collective-permute-start.21 = (bf16[10,16,256]{2,1,0:T(8,128)(2,1)S(1)}, bf16[10,16,256]{2,1,0:T(8,128)(2,1)S(1)}, u32[]{:S(2)}, u32[]{:S(2)}) collective-permute-start(bf16[10,16,256]{2,1,0:T(8,128)(2,1)S(1)} %owner.1.refs_0_), channel_id=1, source_target_pairs={{0,48},{16,0},{32,16},{48,32},{64,112},{80,64},{96,80},{112,96},{1... | collective-permute-start | bytes 245768 | tf_op jit(solution)/shard_map/ppermute | solution.py:58
  81.6 12.4 %collective-permute-start.22 = (bf16[3,10,16,256]{3,2,1,0:T(8,128)(2,1)S(1)}, bf16[3,10,16,256]{3,2,1,0:T(8,128)(2,1)S(1)}, u32[]{:S(2)}, u32[]{:S(2)}) collective-permute-start(bf16[3,10,16,256]{3,2,1,0:T(8,128)(2,1)S(1)} %ahead.1.refs_7_), channel_id=1, source_target_pairs={{0,16},{16,32},{32,48},{48,0},{64,80},{80,96},{96,112},{112,64},{1... | collective-permute-start | bytes 737288 | tf_op jit(solution)/shard_map/ppermute | solution.py:58
  82.3 11.7 %collective-permute-start.23 = (bf16[3,10,16,256]{3,2,1,0:T(8,128)(2,1)S(1)}, bf16[3,10,16,256]{3,2,1,0:T(8,128)(2,1)S(1)}, u32[]{:S(2)}, u32[]{:S(2)}) collective-permute-start(bf16[3,10,16,256]{3,2,1,0:T(8,128)(2,1)S(1)} %ahead.1.refs_7_), channel_id=1, source_target_pairs={{0,32},{16,48},{32,0},{48,16},{64,96},{80,112},{96,64},{112,80},{1... | collective-permute-start | bytes 737288 | tf_op jit(solution)/shard_map/ppermute | solution.py:58
  84.8 9.3 %collective-permute-start.24 = (bf16[3,10,16,256]{3,2,1,0:T(8,128)(2,1)S(1)}, bf16[3,10,16,256]{3,2,1,0:T(8,128)(2,1)S(1)}, u32[]{:S(2)}, u32[]{:S(2)}) collective-permute-start(bf16[3,10,16,256]{3,2,1,0:T(8,128)(2,1)S(1)} %ahead.1.refs_7_), channel_id=1, source_target_pairs={{0,48},{16,0},{32,16},{48,32},{64,112},{80,64},{96,80},{112,96},{1... | collective-permute-start | bytes 737288 | tf_op jit(solution)/shard_map/ppermute | solution.py:58

commit v3 on v2

--- a/solution.py
+++ b/solution.py
@@ -91,16 +91,17 @@
 
 
 def rows_body(cot, last, first, sems):
-    fetch(
-        [
-            pltpu.make_async_copy(cot.at[cot.shape[0] - 1], last, sems.at[0]),
-            pltpu.make_async_copy(cot.at[0], first, sems.at[1]),
-        ]
-    )
-
-
-def mix_body(sel, style, bank, after, kernel, final):
-    del after
+    rows, width = cot.shape[:2]
+    parts = sems.shape[1]
+    copies = []
+    for n, (row, out) in enumerate(((rows - 1, last), (0, first))):
+        for p in range(parts):
+            here = pl.ds(p * (width // parts), width // parts)
+            copies.append(pltpu.make_async_copy(cot.at[row, here], out.at[here], sems.at[n, p]))
+    fetch(copies)
+
+
+def mix_body(sel, style, bank, kernel, final):
     banks, taps = bank.shape[:2]
     top = sel.shape[1]
     weights = []
@@ -138,7 +139,7 @@
             out[c ^ core, g, :, at] = flat[start : start + 16]
 
 
-def grad_body(place, cot_hbm, fm_hbm, grad, cot, fm, cot_t, fm_v, sems, step=4):
+def grad_body(place, cot, fm_hbm, grad, ends, fm, cot_t, fm_v, sems, step=4):
     rows, width, channels = cot.shape
     groups = channels // (16 * NC)
     core = place[2]
@@ -146,22 +147,15 @@
     copies = []
     for q in range(parts):
         here = pl.ds(q * step, step)
-        copies.append(
-            (
-                pltpu.make_async_copy(cot_hbm.at[here], cot.at[here], sems.at[0, q]),
-                pltpu.make_async_copy(fm_hbm.at[here], fm.at[here], sems.at[1, q]),
-            )
-        )
-    for pair in copies:
-        for copy in pair:
-            copy.start()
+        copies.append(pltpu.make_async_copy(fm_hbm.at[here], fm.at[here], sems.at[q]))
+    for copy in copies:
+        copy.start()
     nothing = jnp.zeros((NC, groups, 16, width), BF16)
     cot_t[:, :, :, :width] = nothing
     cot_t[:, :, :, (rows + 1) * width :] = nothing
 
     def prepare(q):
-        for copy in copies[q]:
-            copy.wait()
+        copies[q].wait()
         for r in range(q * step, (q + 1) * step):
             row = fm[r]
             before, after = moved_columns(row.astype(F32))
@@ -169,6 +163,8 @@
             fm_v[0, here] = before.astype(BF16)
             fm_v[1, here] = row
             fm_v[2, here] = after.astype(BF16)
+            if r in (0, rows - 1):
+                ends[int(r > 0)] = row
             turned(cot[r], core, cot_t, pl.ds((r + 1) * width, width))
 
     def add(q):
@@ -188,15 +184,9 @@
         add(q)
 
 
-def edge_body(place, grad, low, high, fm, after, mine, theirs, turn_low, turn_high, first, last, sems):
+def edge_body(place, grad, ends, low, high, after, mine, theirs, turn_low, turn_high):
     del after
     taps, _, groups, _, channels = grad.shape
-    copies = [
-        pltpu.make_async_copy(fm.at[0], first, sems.at[0]),
-        pltpu.make_async_copy(fm.at[fm.shape[0] - 1], last, sems.at[1]),
-    ]
-    for copy in copies:
-        copy.start()
     width = low.shape[0]
     core = place[2]
     turned(low[...], core, turn_low, pl.ds(0, width))
@@ -209,10 +199,8 @@
 
     for t in (3, 4, 5):
         put(t, grad[t])
-    for copy in copies:
-        copy.wait()
-    for turn, row, tap in ((turn_high, last, 0), (turn_low, first, 6)):
-        whole = row[...].reshape(width, channels)
+    for turn, end, tap in ((turn_high, 1, 0), (turn_low, 0, 6)):
+        whole = ends[end]
         before, after = moved_columns(whole.astype(F32))
         left = turn[...].reshape(channels, width)
         for v, right in enumerate((before.astype(BF16), whole, after.astype(BF16))):
@@ -230,46 +218,58 @@
             out[z] = (mine[base + z] + got[base + z].astype(F32)).astype(out.dtype)
 
 
-def split_z_body(place, mine, one, two, three, total, other):
+def put_row(block, row):
+    at = lax.broadcasted_iota(jnp.int32, block.shape, 0)
+    out = jnp.zeros(block.shape, F32)
+    for n in range(3):
+        part = row.astype(BF16).astype(F32)
+        out = jnp.where(at == n, part, out)
+        row = row - part
+    block[...] = out.astype(BF16)
+
+
+def take_row(block):
+    rows = block[...].astype(F32)
+    return (rows[0:1] + rows[1:2]) + rows[2:3]
+
+
+def split_z_body(place, style, mine, one, two, three, near, got, total, other):
+    taps, outs, channels = total.shape
     z = place[1]
-    for k in range(NZ):
-        at = z ^ k
-        value = mine[at] + one[at].astype(F32) + two[at].astype(F32) + three[at].astype(F32)
-        total[k] = value
-        if k == 1:
-            other[...] = value.astype(BF16)
-
-
-def style_body(style, total, near, got, part, four):
-    taps, outs, channels = total.shape[1:]
     share = jnp.zeros((outs, channels), F32)
     for k, source in enumerate((near, got)):
+        at = z ^ k
         dot = jnp.zeros((outs, channels), F32)
+        values = []
         for t in range(taps):
-            dot = dot + total[k, t] * source[0, t].astype(F32)
+            value = mine[at, t] + one[at, t].astype(F32) + two[at, t].astype(F32) + three[at, t].astype(F32)
+            if k == 0:
+                total[t] = value
+            else:
+                other[t] = value.astype(BF16)
+            dot = dot + value * source[0, t].astype(F32)
+            values.append(value)
         dot = jnp.sum(dot, axis=1, keepdims=True)
         for t in range(taps):
             final = source[0, t].astype(F32)
-            share = share + (total[k, t] - final * dot) * final
-    row = jnp.sum(share, axis=0, keepdims=True) / style[...]
-    part[...] = jnp.broadcast_to(row, part.shape)
-    four[pl.ds(0, NC)] = near[...]
-    four[pl.ds(NC, NC)] = got[...]
-
-
-def owner_body(sel, style, kernel, total, got, message):
+            share = share + (values[t] - final * dot) * final
+    put_row(other.at[taps], jnp.sum(share, axis=0, keepdims=True) / style[...])
+
+
+def owner_body(sel, style, kernel, total, sent, got, message, style_row):
     taps, outs, channels = kernel.shape
     top = sel.shape[1]
     s = style[...]
+    style_row[...] = jnp.broadcast_to(take_row(sent.at[taps]) + take_row(got.at[taps]), style_row.shape)
     demod = demod_of(kernel, s)
     dot = jnp.zeros((outs, channels), F32)
     for t in range(taps):
-        grad = total[0, t] + got[t].astype(F32)
+        grad = total[t] + got[t].astype(F32)
         dot = dot + grad * (kernel[t] * s)
     curvature = jnp.sum(dot, axis=1, keepdims=True)
     slope = demod * demod * demod * curvature
     for t in range(taps):
-        grad = total[0, t] + got[t].astype(F32)
+        grad = total[t] + got[t].astype(F32)
         modded_grad = demod * grad - slope * (kernel[t] * s)
         message[t] = (modded_grad * s).astype(BF16)
     bank = lax.broadcasted_iota(jnp.int32, (outs, channels), 0)
@@ -279,8 +279,24 @@
     message[taps] = rank.astype(BF16)
 
 
-def ahead_body(one, two, three, out):
-    for k, piece in enumerate((one, two, three)):
+def four_body(style_row, near, got, four):
+    taps = near.shape[1]
+    for k, source in enumerate((near, got)):
+        for c in range(NC):
+            four[pl.ds((k * NC + c) * taps, taps)] = source[c]
+    put_row(four.at[NZ * NC * taps], style_row[0:1])
+
+
+def style_body(zero, one, two, three, out):
+    last = zero.shape[0] - 1
+    even = take_row(zero.at[last]) + take_row(two.at[last])
+    odd = take_row(one.at[last]) + take_row(three.at[last])
+    out[...] = jnp.broadcast_to(even + odd, out.shape)
+
+
+def ahead_body(*refs):
+    out = refs[-1]
+    for k, piece in enumerate(refs[:-1]):
         out[k] = piece[...]
 
 
@@ -330,7 +346,7 @@
                 here = pl.ds(pl.multiple_of(at * 16, 16), 16)
                 for t in range(9):
                     u, v = t // 3, t % 3
-                    final[u, here, v * channels : (v + 1) * channels] = finals[k][n * NC + c, t]
+                    final[u, here, v * channels : (v + 1) * channels] = finals[k][(n * NC + c) * 9 + t]
     copy.wait()
     step = 2
 
@@ -360,29 +376,29 @@
     dma = pltpu.SemaphoreType.DMA
     piece = (taps, own_out, channels)
     pair = (NZ,) + piece
+    message_of = (taps + 1, own_out, channels)
 
     last, first = call(
-        rows_body, (shape((width, channels), BF16),) * 2, [HBM], [dma((2,))], nbytes=10**6, vmem=60 << 20, name="rows"
+        rows_body, (shape((width, channels), BF16),) * 2, [HBM], [dma((2, 4))], nbytes=10**6, vmem=60 << 20, name="rows"
     )(cot)
     count = lax.axis_size("tile")
     low = lax.ppermute(last, "tile", [(i, i + 1) for i in range(count - 1)])
     high = lax.ppermute(first, "tile", [(i + 1, i) for i in range(count - 1)])
 
     kernel, final = call(
-        mix_body, (shape(piece, F32), shape(piece, BF16)), [SMEM, VMEM, VMEM, VMEM], flops=10**6, nbytes=10**6, name="mix"
-    )(selection, style, jnp.transpose(bank, (0, 2, 1, 3)), last)
+        mix_body, (shape(piece, F32), shape(piece, BF16)), [SMEM, VMEM, VMEM], flops=10**6, nbytes=10**6, name="mix"
+    )(selection, style, jnp.transpose(bank, (0, 2, 1, 3)))
     final_c = swap_core(final)
 
-    grad = call(
+    grad, ends = call(
         grad_body,
-        shape((taps, NC, groups, 16, channels), F32),
-        [SMEM, HBM, HBM],
+        (shape((taps, NC, groups, 16, channels), F32), shape((2, width, channels), BF16)),
+        [SMEM, VMEM, HBM],
         [
-            pltpu.VMEM((rows, width, channels), BF16),
             pltpu.VMEM((rows, width, channels), BF16),
             pltpu.VMEM((NC, groups, 16, (rows + 2) * width), BF16),
             pltpu.VMEM((3, rows * width, channels), BF16),
-            dma((2, 4)),
+            dma((4,)),
         ],
         flops=2 * 9 * rows * width * channels * channels,
         nbytes=4 * rows * width * channels,
@@ -392,13 +408,13 @@
     mine, theirs = call(
         edge_body,
         (shape((groups,) + piece, F32), shape((groups,) + piece, BF16)),
-        [SMEM] + [VMEM] * 3 + [HBM, VMEM],
-        [pltpu.VMEM((NC, groups, 16, width), BF16)] * 2 + [pltpu.VMEM((width, channels), BF16)] * 2 + [dma((2,))],
+        [SMEM] + [VMEM] * 5,
+        [pltpu.VMEM((NC, groups, 16, width), BF16)] * 2,
         flops=2 * 6 * width * channels * channels,
         nbytes=4 * 10**6,
         vmem=50 << 20,
         name="edge",
-    )(place, grad, low, high, fm, final_c)
+    )(place, grad, ends, low, high, final_c)
 
     own_x, one, two, three, both = call(
         split_x_body,
@@ -411,40 +427,36 @@
     got_z = swap_z(both)
     total, other = call(
         split_z_body,
-        (shape(pair, F32), shape(piece, BF16)),
-        [SMEM] + [VMEM] * 4,
+        (shape(piece, F32), shape(message_of, BF16)),
+        [SMEM] + [VMEM] * 7,
         flops=10**6,
         nbytes=10**6,
         name="split_z",
-    )(place, own_x, shift_x(one, 1), shift_x(two, 2), shift_x(three, 3))
-    message = call(
+    )(place, style, own_x, shift_x(one, 1), shift_x(two, 2), shift_x(three, 3), both, got_z)
+    message, style_row = call(
         owner_body,
-        shape((taps + 1, own_out, channels), BF16),
-        [SMEM] + [VMEM] * 4,
+        (shape(message_of, BF16), shape((8, channels), F32)),
+        [SMEM] + [VMEM] * 5,
         flops=10**6,
         nbytes=10**6,
         name="owner",
-    )(selection, style, kernel, total, swap_z(other))
-    style_part, four = call(
-        style_body,
-        (shape((8, channels), F32), shape((NZ * NC,) + piece, BF16)),
-        [VMEM] * 4,
+    )(selection, style, kernel, total, other, swap_z(other))
+
+    four = call(
+        four_body,
+        shape((NZ * NC * taps + 1, own_out, channels), BF16),
+        [VMEM] * 3,
         flops=10**9,
         nbytes=10**7,
-        name="style",
-    )(style, total, both, got_z)
-
+        name="four",
+    )(style_row, both, got_z)
     finals = [four] + [shift_x(four, k) for k in range(1, NX)]
+    style_part = call(style_body, shape((8, channels), F32), [VMEM] * NX, name="style")(*finals)
+    style_sum = style_part + swap_core(style_part)
 
     over_l = [flip_l(message, k) for k in range(1, NL)]
-    over_y = [shift_y(message, k) for k in range(1, NY)]
-    ahead = call(ahead_body, shape((3, taps + 1, own_out, channels), BF16), [VMEM] * 3, name="ahead")(*over_l)
-    rest = [shift_y(ahead, k) for k in range(1, NY)]
-
-    style_sum = style_part + swap_core(style_part)
-    style_sum = style_sum + flip_x(style_sum, 1)
-    style_sum = style_sum + flip_x(style_sum, 2)
-    style_sum = style_sum + swap_z(style_sum)
+    ahead = call(ahead_body, shape((NL,) + message_of, BF16), [VMEM] * NL, name="ahead")(message, *over_l)
+    over_y = [shift_y(ahead, k) for k in range(1, NY)]
 
     input_grad = call(
         input_body,
@@ -464,13 +476,13 @@
     bank_grad = pl.pallas_call(
         banks_body,
         out_shape=shape((banks,) + piece, F32),
-        in_specs=[VMEM] * 10,
+        in_specs=[VMEM] * NY,
         out_specs=HBM,
         scratch_shapes=[pltpu.VMEM((banks,) + piece, F32), dma((taps,))],
         compiler_params=pltpu.CompilerParams(vmem_limit_bytes=16 << 20),
         cost_estimate=pl.CostEstimate(flops=10**7, bytes_accessed=3 * 10**6, transcendentals=0),
         name="banks",
-    )(message, *over_l, *over_y, *rest)
+    )(ahead, *over_y)
 
     return (
         input_grad.reshape(feature_map.shape),

time: 95.8 us -> 91.6 us (0.956); the launches traced: 95.5 us -> 90 us
  starting transfers between devices: 55.3 us -> 45.5 us
  waiting for transfers between devices: 8.98 us -> 15.3 us
  Pallas kernels: 27.6 us -> 26.6 us
    ppermute x3 -> x2, waiting for transfers between devices: 0.57 us -> 9.11 us  [swap_z(): return lax.ppermute(a, 'tile', tile_perm(lambda x, z, c: (x, 1 - z, c)))]
    ppermute x3 -> x2, starting transfers between devices: 16.7 us -> 12.1 us  [swap_z(): return lax.ppermute(a, 'tile', tile_perm(lambda x, z, c: (x, 1 - z, c)))]
    ppermute x6 -> x3, starting transfers between devices: 9.24 us -> 5 us  [shift_y(): return lax.ppermute(a, 'img', img_perm(lambda l, y: (l, (y + k) % NY)))]
    ppermute x3, starting transfers between devices: 3.72 us -> 7.77 us  [flip_l(): return lax.ppermute(a, 'img', img_perm(lambda l, y: (l ^ k, y)))]
    ppermute x2 -> x0, starting transfers between devices: 3.99 us -> none  [flip_x(): return lax.ppermute(a, 'tile', tile_perm(lambda x, z, c: (x ^ k, z, c)))]
    ppermute x2 -> x0, waiting for transfers between devices: 2.31 us -> none  [flip_x(): return lax.ppermute(a, 'tile', tile_perm(lambda x, z, c: (x ^ k, z, c)))]
    ppermute x3, waiting for transfers between devices: 3.11 us -> 1.95 us  [swap_core(): return lax.ppermute(a, 'tile', tile_perm(lambda x, z, c: (x, z, 1 - c)))]
    ppermute x6 -> x3, waiting for transfers between devices: 0.02 us -> 1.15 us  [shift_y(): return lax.ppermute(a, 'img', img_perm(lambda l, y: (l, (y + k) % NY)))]
  transfers between devices with their start and end apart: 25 -> 19, of which waited for: 5 -> 7; matrix products, arithmetic and copies ran while one was open for 1% -> 1% of each run, Pallas kernels for 22% -> 21%
where the time goes in v3:
time: 91.6 us; the launch traced here: 90 us
  starting transfers between devices  45.5 us (50%)
  Pallas kernels  26.6 us (29%)
  waiting for transfers between devices  15.3 us (17%)
  local copies, waits for them, and re-layouts  1.07 us (1%)
  between operations  0.96 us (1%)
    ppermute x2, starting transfers between devices, swap_z(): return lax.ppermute(a, 'tile', tile_perm(lambda x, z, c: (x, 1 - z, c)))  12.1 us
    pallas_call x1, Pallas kernels, local(): call(grad_body, (shape((taps, NC, groups, 16, channels), F32), shape((2,...  10.1 us
    ppermute x6, starting transfers between devices, shift_x(): lax.ppermute(a, 'tile', tile_perm(lambda x, z, c: ((x + k) % NX, z, c)))  9.16 us
    ppermute x2, waiting for transfers between devices, swap_z(): return lax.ppermute(a, 'tile', tile_perm(lambda x, z, c: (x, 1 - z, c)))  9.11 us
    pallas_call x1, Pallas kernels, local(): call(input_body, shape((rows, width, channels), BF16), [SMEM] + [VMEM] *...  8.4 us
    ppermute x3, starting transfers between devices, swap_core(): return lax.ppermute(a, 'tile', tile_perm(lambda x, z, c: (x, z, 1 - c)))  8.39 us
    ppermute x3, starting transfers between devices, flip_l(): return lax.ppermute(a, 'img', img_perm(lambda l, y: (l ^ k, y)))  7.77 us
    ppermute x3, starting transfers between devices, shift_y(): return lax.ppermute(a, 'img', img_perm(lambda l, y: (l, (y + k) % NY)))  5 us
  transfers between devices with their start and end apart: 19, of which 7 were waited for; matrix products, arithmetic and copies ran while one was open for 1% of the time, Pallas kernels for 21%

profile of v3, /device:TPU:8, one launch (start us, length us, event | category | flops | bytes accessed | tf_op | source)
XLA Modules:
  0.0 90.0 jit_solution(4312064606114157769)
XLA Ops:
  0.7 1.8 %rows.1 = (bf16[256,256]{1,0:T(8,128)(2,1)}, bf16[256,256]{1,0:T(8,128)(2,1)}) custom-call(bf16[16,256,256]{2,1,0:T(8,128)(2,1)} %bitcast.8), custom_call_target="tpu_custom_call" | custom-call | bytes 1000000 | tf_op jit(solution)/shard_map/rows/pallas_call | solution.py:381
  2.4 1.7 %collective-permute-start = (bf16[256,256]{1,0:T(8,128)(2,1)}, bf16[256,256]{1,0:T(8,128)(2,1)S(1)}, u32[]{:S(2)}, u32[]{:S(2)}) collective-permute-start(bf16[256,256]{1,0:T(8,128)(2,1)} %get-tuple-element.23), channel_id=1, source_target_pairs={{0,1},{1,2},{2,3},{3,4},{4,5},{5,6},{6,7},{7,8},{8,9},{9,10},{10,1... | collective-permute-start | bytes 393224 | tf_op jit(solution)/shard_map/ppermute | solution.py:385
  4.2 1.3 %collective-permute-start.1 = (bf16[256,256]{1,0:T(8,128)(2,1)}, bf16[256,256]{1,0:T(8,128)(2,1)S(1)}, u32[]{:S(2)}, u32[]{:S(2)}) collective-permute-start(bf16[256,256]{1,0:T(8,128)(2,1)} %get-tuple-element.24), channel_id=1, source_target_pairs={{1,0},{2,1},{3,2},{4,3},{5,4},{6,5},{7,6},{8,7},{9,8},{10,9},{11,1... | collective-permute-start | bytes 393224 | tf_op jit(solution)/shard_map/ppermute | solution.py:386
  5.5 1.1 %copy-done.1 = bf16[8,16,9,256]{3,1,2,0:T(8,128)(2,1)S(1)} copy-done((bf16[8,16,9,256]{3,1,2,0:T(8,128)(2,1)S(1)}, bf16[8,16,9,256]{3,1,2,0:T(8,128)(2,1)}, u32[]{:S(2)}) %copy-start.1) | copy-done | bytes 589848
  6.6 0.8 mix.1
  7.3 8.2 %collective-permute-start.2 = (bf16[9,16,256]{2,1,0:T(8,128)(2,1)S(1)}, bf16[9,16,256]{2,1,0:T(8,128)(2,1)S(1)}, u32[]{:S(2)}, u32[]{:S(2)}) collective-permute-start(bf16[9,16,256]{2,1,0:T(8,128)(2,1)S(1)} %get-tuple-element.25.final), channel_id=1, source_target_pairs={{0,1},{1,0},{2,3},{3,2},{4,5},{5,4},{6,7},{7,6},{8,9},{9,8},{10,11... | collective-permute-start | bytes 221192 | tf_op jit(solution)/shard_map/ppermute | solution.py:38
  15.6 10.1 %grad.1 = (f32[9,2,8,16,256]{4,3,2,1,0:T(8,128)}, bf16[2,256,256]{2,1,0:T(8,128)(2,1)S(1)}) custom-call(s32[3]{0:T(128)S(1)} %pad_add_fusion.place, bf16[16,256,256]{2,1,0:T(8,128)(2,1)S(1)} %bitcast.9, bf16[16,256,256]{2,1,0:T(8,128)(2,1)} %bitcast.13), custom_call_target="tpu_custom_call" | custom-call | flops 4831838208 | bytes 4194304 | tf_op jit(solution)/shard_map/grad/pallas_call | solution.py:393
  25.7 2.1 %edge.1 = (f32[8,9,16,256]{3,2,1,0:T(8,128)S(1)}, bf16[8,9,16,256]{3,2,1,0:T(8,128)(2,1)S(1)}) custom-call(s32[3]{0:T(128)S(1)} %pad_add_fusion.place, f32[9,2,8,16,256]{4,3,2,1,0:T(8,128)} %get-tuple-element.21.grad, bf16[2,256,256]{2,1,0:T(8,128)(2,1)S(1)} %get-tuple-element.22.ends, bf16[256,256]{1,0:T(8,128)(2,1)S(1)} %collective-permute-done.low.refs_4_, ...), custom_call_target="tpu_custom_call" | custom-call | flops 201326592 | bytes 4000000 | tf_op jit(solution)/shard_map/edge/pallas_call | solution.py:408
  28.0 1.9 %collective-permute-done.3.got = bf16[8,9,16,256]{3,2,1,0:T(8,128)(2,1)S(1)} collective-permute-done((bf16[8,9,16,256]{3,2,1,0:T(8,128)(2,1)S(1)}, bf16[8,9,16,256]{3,2,1,0:T(8,128)(2,1)S(1)}, u32[]{:S(2)}, u32[]{:S(2)}) %collective-permute-start.3) | collective-permute-done | bytes 589856 | tf_op jit(solution)/shard_map/ppermute | solution.py:38
  29.9 0.7 split_x.1
  30.6 1.6 %collective-permute-start.4 = (bf16[2,9,16,256]{3,2,1,0:T(8,128)(2,1)S(1)}, bf16[2,9,16,256]{3,2,1,0:T(8,128)(2,1)S(1)}, u32[]{:S(2)}, u32[]{:S(2)}) collective-permute-start(bf16[2,9,16,256]{3,2,1,0:T(8,128)(2,1)S(1)} %get-tuple-element.29), channel_id=1, source_target_pairs={{0,4},{1,5},{2,6},{3,7},{4,8},{5,9},{6,10},{7,11},{8,12},{9,13},{1... | collective-permute-start | bytes 442376 | tf_op jit(solution)/shard_map/ppermute | solution.py:46
  32.2 2.7 %collective-permute-start.5 = (bf16[2,9,16,256]{3,2,1,0:T(8,128)(2,1)S(1)}, bf16[2,9,16,256]{3,2,1,0:T(8,128)(2,1)S(1)}, u32[]{:S(2)}, u32[]{:S(2)}) collective-permute-start(bf16[2,9,16,256]{3,2,1,0:T(8,128)(2,1)S(1)} %get-tuple-element.30), channel_id=1, source_target_pairs={{0,8},{1,9},{2,10},{3,11},{4,12},{5,13},{6,14},{7,15},{8,0},{9,1},... | collective-permute-start | bytes 442376 | tf_op jit(solution)/shard_map/ppermute | solution.py:46
  34.9 1.4 %collective-permute-start.6 = (bf16[2,9,16,256]{3,2,1,0:T(8,128)(2,1)S(1)}, bf16[2,9,16,256]{3,2,1,0:T(8,128)(2,1)S(1)}, u32[]{:S(2)}, u32[]{:S(2)}) collective-permute-start(bf16[2,9,16,256]{3,2,1,0:T(8,128)(2,1)S(1)} %get-tuple-element.31), channel_id=1, source_target_pairs={{0,12},{1,13},{2,14},{3,15},{4,0},{5,1},{6,2},{7,3},{8,4},{9,5},{1... | collective-permute-start | bytes 442376 | tf_op jit(solution)/shard_map/ppermute | solution.py:46
  36.3 5.7 %collective-permute-start.7 = (bf16[2,9,16,256]{3,2,1,0:T(8,128)(2,1)S(1)}, bf16[2,9,16,256]{3,2,1,0:T(8,128)(2,1)S(1)}, u32[]{:S(2)}, u32[]{:S(2)}) collective-permute-start(bf16[2,9,16,256]{3,2,1,0:T(8,128)(2,1)S(1)} %get-tuple-element.32.near), channel_id=1, source_target_pairs={{0,2},{1,3},{2,0},{3,1},{4,6},{5,7},{6,4},{7,5},{8,10},{9,11},{10,... | collective-permute-start | bytes 442376 | tf_op jit(solution)/shard_map/ppermute | solution.py:42
  42.0 6.0 %collective-permute-done.7.got = bf16[2,9,16,256]{3,2,1,0:T(8,128)(2,1)S(1)} collective-permute-done((bf16[2,9,16,256]{3,2,1,0:T(8,128)(2,1)S(1)}, bf16[2,9,16,256]{3,2,1,0:T(8,128)(2,1)S(1)}, u32[]{:S(2)}, u32[]{:S(2)}) %collective-permute-start.7) | collective-permute-done | bytes 147488 | tf_op jit(solution)/shard_map/ppermute | solution.py:42
  48.0 0.7 split_z.1
  48.7 6.4 %collective-permute-start.8 = (bf16[10,16,256]{2,1,0:T(8,128)(2,1)S(1)}, bf16[10,16,256]{2,1,0:T(8,128)(2,1)S(1)}, u32[]{:S(2)}, u32[]{:S(2)}) collective-permute-start(bf16[10,16,256]{2,1,0:T(8,128)(2,1)S(1)} %get-tuple-element.34.sent), channel_id=1, source_target_pairs={{0,2},{1,3},{2,0},{3,1},{4,6},{5,7},{6,4},{7,5},{8,10},{9,11},{10,... | collective-permute-start | bytes 245768 | tf_op jit(solution)/shard_map/ppermute | solution.py:42
  55.2 3.1 %collective-permute-done.8.got = bf16[10,16,256]{2,1,0:T(8,128)(2,1)S(1)} collective-permute-done((bf16[10,16,256]{2,1,0:T(8,128)(2,1)S(1)}, bf16[10,16,256]{2,1,0:T(8,128)(2,1)S(1)}, u32[]{:S(2)}, u32[]{:S(2)}) %collective-permute-start.8) | collective-permute-done | bytes 81952 | tf_op jit(solution)/shard_map/ppermute | solution.py:42
  58.3 0.7 owner.1
  59.0 0.6 collective-permute-start.9
  59.7 1.0 %collective-permute-start.10 = (bf16[37,16,256]{2,1,0:T(8,128)(2,1)S(1)}, bf16[37,16,256]{2,1,0:T(8,128)(2,1)S(1)}, u32[]{:S(2)}, u32[]{:S(2)}) collective-permute-start(bf16[37,16,256]{2,1,0:T(8,128)(2,1)S(1)} %four.1.refs_0_.zero), channel_id=1, source_target_pairs={{0,8},{1,9},{2,10},{3,11},{4,12},{5,13},{6,14},{7,15},{8,0},{9,1},... | collective-permute-start | bytes 909320 | tf_op jit(solution)/shard_map/ppermute | solution.py:46
  60.7 1.8 %collective-permute-start.11 = (bf16[37,16,256]{2,1,0:T(8,128)(2,1)S(1)}, bf16[37,16,256]{2,1,0:T(8,128)(2,1)S(1)}, u32[]{:S(2)}, u32[]{:S(2)}) collective-permute-start(bf16[37,16,256]{2,1,0:T(8,128)(2,1)S(1)} %four.1.refs_0_.zero), channel_id=1, source_target_pairs={{0,12},{1,13},{2,14},{3,15},{4,0},{5,1},{6,2},{7,3},{8,4},{9,5},{1... | collective-permute-start | bytes 909320 | tf_op jit(solution)/shard_map/ppermute | solution.py:46
  62.5 0.7 collective-permute-start.12
  63.2 3.2 %collective-permute-start.13 = (bf16[10,16,256]{2,1,0:T(8,128)(2,1)S(1)}, bf16[10,16,256]{2,1,0:T(8,128)(2,1)S(1)}, u32[]{:S(2)}, u32[]{:S(2)}) collective-permute-start(bf16[10,16,256]{2,1,0:T(8,128)(2,1)S(1)} %get-tuple-element.36.refs_0_), channel_id=1, source_target_pairs={{0,128},{16,144},{32,160},{48,176},{64,192},{80,208},{96,224},{112... | collective-permute-start | bytes 245768 | tf_op jit(solution)/shard_map/ppermute | solution.py:54
  66.9 3.9 %collective-permute-start.14 = (bf16[10,16,256]{2,1,0:T(8,128)(2,1)S(1)}, bf16[10,16,256]{2,1,0:T(8,128)(2,1)S(1)}, u32[]{:S(2)}, u32[]{:S(2)}) collective-permute-start(bf16[10,16,256]{2,1,0:T(8,128)(2,1)S(1)} %get-tuple-element.36.refs_0_), channel_id=1, source_target_pairs={{0,192},{16,208},{32,224},{48,240},{64,128},{80,144},{96,160},{112... | collective-permute-start | bytes 245768 | tf_op jit(solution)/shard_map/ppermute | solution.py:54
  71.1 2.2 %collective-permute-done.14.refs_3_ = bf16[10,16,256]{2,1,0:T(8,128)(2,1)S(1)} collective-permute-done((bf16[10,16,256]{2,1,0:T(8,128)(2,1)S(1)}, bf16[10,16,256]{2,1,0:T(8,128)(2,1)S(1)}, u32[]{:S(2)}, u32[]{:S(2)}) %collective-permute-start.14) | collective-permute-done | bytes 81952 | tf_op jit(solution)/shard_map/ppermute | solution.py:54
  73.3 1.7 %collective-permute-start.16 = (bf16[4,10,16,256]{3,2,1,0:T(8,128)(2,1)S(1)}, bf16[4,10,16,256]{3,2,1,0:T(8,128)(2,1)S(1)}, u32[]{:S(2)}, u32[]{:S(2)}) collective-permute-start(bf16[4,10,16,256]{3,2,1,0:T(8,128)(2,1)S(1)} %ahead.1.refs_7_.refs_0_), channel_id=1, source_target_pairs={{0,16},{16,32},{32,48},{48,0},{64,80},{80,96},{96,112},{112,64},{1... | collective-permute-start | bytes 983048 | tf_op jit(solution)/shard_map/ppermute | solution.py:58
  75.0 0.9 %collective-permute-start.17 = (bf16[4,10,16,256]{3,2,1,0:T(8,128)(2,1)S(1)}, bf16[4,10,16,256]{3,2,1,0:T(8,128)(2,1)S(1)}, u32[]{:S(2)}, u32[]{:S(2)}) collective-permute-start(bf16[4,10,16,256]{3,2,1,0:T(8,128)(2,1)S(1)} %ahead.1.refs_7_.refs_0_), channel_id=1, source_target_pairs={{0,32},{16,48},{32,0},{48,16},{64,96},{80,112},{96,64},{112,80},{1... | collective-permute-start | bytes 983048 | tf_op jit(solution)/shard_map/ppermute | solution.py:58
  75.9 2.4 %collective-permute-start.18 = (bf16[4,10,16,256]{3,2,1,0:T(8,128)(2,1)S(1)}, bf16[4,10,16,256]{3,2,1,0:T(8,128)(2,1)S(1)}, u32[]{:S(2)}, u32[]{:S(2)}) collective-permute-start(bf16[4,10,16,256]{3,2,1,0:T(8,128)(2,1)S(1)} %ahead.1.refs_7_.refs_0_), channel_id=1, source_target_pairs={{0,48},{16,0},{32,16},{48,32},{64,112},{80,64},{96,80},{112,96},{1... | collective-permute-start | bytes 983048 | tf_op jit(solution)/shard_map/ppermute | solution.py:58
  78.4 8.4 %input.1 = bf16[16,256,256]{2,1,0:T(8,128)(2,1)} custom-call(s32[3]{0:T(128)S(1)} %pad_add_fusion.place, bf16[37,16,256]{2,1,0:T(8,128)(2,1)S(1)} %four.1.refs_0_.zero, bf16[37,16,256]{2,1,0:T(8,128)(2,1)S(1)} %collective-permute-done.9.refs_1_.one, bf16[37,16,256]{2,1,0:T(8,128)(2,1)S(1)} %collective-permute-done.10.refs_2_.two, ...), custom_call_target="tpu_custom_call" | custom-call | flops 4831838208 | bytes 4194304 | tf_op jit(solution)/shard_map/input/pallas_call | solution.py:461
  87.4 1.1 %collective-permute-done.18.refs_3_ = bf16[4,10,16,256]{3,2,1,0:T(8,128)(2,1)S(1)} collective-permute-done((bf16[4,10,16,256]{3,2,1,0:T(8,128)(2,1)S(1)}, bf16[4,10,16,256]{3,2,1,0:T(8,128)(2,1)S(1)}, u32[]{:S(2)}, u32[]{:S(2)}) %collective-permute-start.18) | collective-permute-done | bytes 327712 | tf_op jit(solution)/shard_map/ppermute | solution.py:58
  88.6 1.3 %banks.1 = f32[8,9,16,256]{3,2,1,0:T(8,128)} custom-call(bf16[4,10,16,256]{3,2,1,0:T(8,128)(2,1)S(1)} %ahead.1.refs_7_.refs_0_, bf16[4,10,16,256]{3,2,1,0:T(8,128)(2,1)S(1)} %collective-permute-done.16.refs_1_, bf16[4,10,16,256]{3,2,1,0:T(8,128)(2,1)S(1)} %collective-permute-done.17.refs_2_, bf16[4,10,16,256]{3,2,1,0:T(8,128)(2,1)S(1)} %collective-permute-done.18.refs_3_), custom_call_target="tpu_custom_call" | custom-call | flops 10000000 | bytes 3000000 | tf_op jit(solution)/shard_map/banks/pallas_call | solution.py:476
  (28 shorter events, 1.9 us)
Async XLA Ops:
  0.6 14.9 %copy-start = (bf16[1,16,256,256]{3,2,1,0:T(8,128)(2,1)S(1)}, bf16[1,16,256,256]{3,2,1,0:T(8,128)(2,1)}, u32[]{:S(2)}) copy-start(bf16[1,16,256,256]{3,2,1,0:T(8,128)(2,1)} %param.6) | copy-start | bytes 6291460
  0.6 4.9 %copy-start.3 = (s32[1,3]{1,0:T(1,128)S(1)}, s32[1,3]{1,0:T(1,128)}, u32[]{:S(2)}) copy-start(s32[1,3]{1,0:T(1,128)} %sel.3) | copy-start | bytes 40
  0.7 4.9 %copy-start.2 = (f32[1,256]{1,0:T(1,128)S(1)}, f32[1,256]{1,0:T(1,128)}, u32[]{:S(2)}) copy-start(f32[1,256]{1,0:T(1,128)} %style.6) | copy-start | bytes 3076
  2.4 23.2 %collective-permute-start = (bf16[256,256]{1,0:T(8,128)(2,1)}, bf16[256,256]{1,0:T(8,128)(2,1)S(1)}, u32[]{:S(2)}, u32[]{:S(2)}) collective-permute-start(bf16[256,256]{1,0:T(8,128)(2,1)} %get-tuple-element.23), channel_id=1, source_target_pairs={{0,1},{1,2},{2,3},{3,4},{4,5},{5,6},{6,7},{7,8},{8,9},{9,10},{10,1... | collective-permute-start | bytes 393224 | tf_op jit(solution)/shard_map/ppermute | solution.py:385
  4.2 21.5 %collective-permute-start.1 = (bf16[256,256]{1,0:T(8,128)(2,1)}, bf16[256,256]{1,0:T(8,128)(2,1)S(1)}, u32[]{:S(2)}, u32[]{:S(2)}) collective-permute-start(bf16[256,256]{1,0:T(8,128)(2,1)} %get-tuple-element.24), channel_id=1, source_target_pairs={{1,0},{2,1},{3,2},{4,3},{5,4},{6,5},{7,6},{8,7},{9,8},{10,9},{11,1... | collective-permute-start | bytes 393224 | tf_op jit(solution)/shard_map/ppermute | solution.py:386
  5.5 1.1 %copy-start.1 = (bf16[8,16,9,256]{3,1,2,0:T(8,128)(2,1)S(1)}, bf16[8,16,9,256]{3,1,2,0:T(8,128)(2,1)}, u32[]{:S(2)}) copy-start(bf16[8,16,9,256]{3,1,2,0:T(8,128)(2,1)} %param.8) | copy-start | bytes 1769476
  7.3 18.3 %collective-permute-start.2 = (bf16[9,16,256]{2,1,0:T(8,128)(2,1)S(1)}, bf16[9,16,256]{2,1,0:T(8,128)(2,1)S(1)}, u32[]{:S(2)}, u32[]{:S(2)}) collective-permute-start(bf16[9,16,256]{2,1,0:T(8,128)(2,1)S(1)} %get-tuple-element.25.final), channel_id=1, source_target_pairs={{0,1},{1,0},{2,3},{3,2},{4,5},{5,4},{6,7},{7,6},{8,9},{9,8},{10,11... | collective-permute-start | bytes 221192 | tf_op jit(solution)/shard_map/ppermute | solution.py:38
  27.8 2.1 %collective-permute-start.3 = (bf16[8,9,16,256]{3,2,1,0:T(8,128)(2,1)S(1)}, bf16[8,9,16,256]{3,2,1,0:T(8,128)(2,1)S(1)}, u32[]{:S(2)}, u32[]{:S(2)}) collective-permute-start(bf16[8,9,16,256]{3,2,1,0:T(8,128)(2,1)S(1)} %get-tuple-element.27), channel_id=1, source_target_pairs={{0,1},{1,0},{2,3},{3,2},{4,5},{5,4},{6,7},{7,6},{8,9},{9,8},{10,11... | collective-permute-start | bytes 1769480 | tf_op jit(solution)/shard_map/ppermute | solution.py:38
  30.6 11.4 %collective-permute-start.4 = (bf16[2,9,16,256]{3,2,1,0:T(8,128)(2,1)S(1)}, bf16[2,9,16,256]{3,2,1,0:T(8,128)(2,1)S(1)}, u32[]{:S(2)}, u32[]{:S(2)}) collective-permute-start(bf16[2,9,16,256]{3,2,1,0:T(8,128)(2,1)S(1)} %get-tuple-element.29), channel_id=1, source_target_pairs={{0,4},{1,5},{2,6},{3,7},{4,8},{5,9},{6,10},{7,11},{8,12},{9,13},{1... | collective-permute-start | bytes 442376 | tf_op jit(solution)/shard_map/ppermute | solution.py:46
  32.2 9.8 %collective-permute-start.5 = (bf16[2,9,16,256]{3,2,1,0:T(8,128)(2,1)S(1)}, bf16[2,9,16,256]{3,2,1,0:T(8,128)(2,1)S(1)}, u32[]{:S(2)}, u32[]{:S(2)}) collective-permute-start(bf16[2,9,16,256]{3,2,1,0:T(8,128)(2,1)S(1)} %get-tuple-element.30), channel_id=1, source_target_pairs={{0,8},{1,9},{2,10},{3,11},{4,12},{5,13},{6,14},{7,15},{8,0},{9,1},... | collective-permute-start | bytes 442376 | tf_op jit(solution)/shard_map/ppermute | solution.py:46
  34.9 7.1 %collective-permute-start.6 = (bf16[2,9,16,256]{3,2,1,0:T(8,128)(2,1)S(1)}, bf16[2,9,16,256]{3,2,1,0:T(8,128)(2,1)S(1)}, u32[]{:S(2)}, u32[]{:S(2)}) collective-permute-start(bf16[2,9,16,256]{3,2,1,0:T(8,128)(2,1)S(1)} %get-tuple-element.31), channel_id=1, source_target_pairs={{0,12},{1,13},{2,14},{3,15},{4,0},{5,1},{6,2},{7,3},{8,4},{9,5},{1... | collective-permute-start | bytes 442376 | tf_op jit(solution)/shard_map/ppermute | solution.py:46
  36.3 11.7 %collective-permute-start.7 = (bf16[2,9,16,256]{3,2,1,0:T(8,128)(2,1)S(1)}, bf16[2,9,16,256]{3,2,1,0:T(8,128)(2,1)S(1)}, u32[]{:S(2)}, u32[]{:S(2)}) collective-permute-start(bf16[2,9,16,256]{3,2,1,0:T(8,128)(2,1)S(1)} %get-tuple-element.32.near), channel_id=1, source_target_pairs={{0,2},{1,3},{2,0},{3,1},{4,6},{5,7},{6,4},{7,5},{8,10},{9,11},{10,... | collective-permute-start | bytes 442376 | tf_op jit(solution)/shard_map/ppermute | solution.py:42
  48.7 9.6 %collective-permute-start.8 = (bf16[10,16,256]{2,1,0:T(8,128)(2,1)S(1)}, bf16[10,16,256]{2,1,0:T(8,128)(2,1)S(1)}, u32[]{:S(2)}, u32[]{:S(2)}) collective-permute-start(bf16[10,16,256]{2,1,0:T(8,128)(2,1)S(1)} %get-tuple-element.34.sent), channel_id=1, source_target_pairs={{0,2},{1,3},{2,0},{3,1},{4,6},{5,7},{6,4},{7,5},{8,10},{9,11},{10,... | collective-permute-start | bytes 245768 | tf_op jit(solution)/shard_map/ppermute | solution.py:42
  59.0 16.9 %collective-permute-start.9 = (bf16[37,16,256]{2,1,0:T(8,128)(2,1)S(1)}, bf16[37,16,256]{2,1,0:T(8,128)(2,1)S(1)}, u32[]{:S(2)}, u32[]{:S(2)}) collective-permute-start(bf16[37,16,256]{2,1,0:T(8,128)(2,1)S(1)} %four.1.refs_0_.zero), channel_id=1, source_target_pairs={{0,4},{1,5},{2,6},{3,7},{4,8},{5,9},{6,10},{7,11},{8,12},{9,13},{1... | collective-permute-start | bytes 909320 | tf_op jit(solution)/shard_map/ppermute | solution.py:46
  59.7 18.6 %collective-permute-start.10 = (bf16[37,16,256]{2,1,0:T(8,128)(2,1)S(1)}, bf16[37,16,256]{2,1,0:T(8,128)(2,1)S(1)}, u32[]{:S(2)}, u32[]{:S(2)}) collective-permute-start(bf16[37,16,256]{2,1,0:T(8,128)(2,1)S(1)} %four.1.refs_0_.zero), channel_id=1, source_target_pairs={{0,8},{1,9},{2,10},{3,11},{4,12},{5,13},{6,14},{7,15},{8,0},{9,1},... | collective-permute-start | bytes 909320 | tf_op jit(solution)/shard_map/ppermute | solution.py:46
  60.7 17.6 %collective-permute-start.11 = (bf16[37,16,256]{2,1,0:T(8,128)(2,1)S(1)}, bf16[37,16,256]{2,1,0:T(8,128)(2,1)S(1)}, u32[]{:S(2)}, u32[]{:S(2)}) collective-permute-start(bf16[37,16,256]{2,1,0:T(8,128)(2,1)S(1)} %four.1.refs_0_.zero), channel_id=1, source_target_pairs={{0,12},{1,13},{2,14},{3,15},{4,0},{5,1},{6,2},{7,3},{8,4},{9,5},{1... | collective-permute-start | bytes 909320 | tf_op jit(solution)/shard_map/ppermute | solution.py:46
  62.5 4.4 %collective-permute-start.12 = (bf16[10,16,256]{2,1,0:T(8,128)(2,1)S(1)}, bf16[10,16,256]{2,1,0:T(8,128)(2,1)S(1)}, u32[]{:S(2)}, u32[]{:S(2)}) collective-permute-start(bf16[10,16,256]{2,1,0:T(8,128)(2,1)S(1)} %get-tuple-element.36.refs_0_), channel_id=1, source_target_pairs={{0,64},{16,80},{32,96},{48,112},{64,0},{80,16},{96,32},{112,48},{1... | collective-permute-start | bytes 245768 | tf_op jit(solution)/shard_map/ppermute | solution.py:54
  63.2 7.9 %collective-permute-start.13 = (bf16[10,16,256]{2,1,0:T(8,128)(2,1)S(1)}, bf16[10,16,256]{2,1,0:T(8,128)(2,1)S(1)}, u32[]{:S(2)}, u32[]{:S(2)}) collective-permute-start(bf16[10,16,256]{2,1,0:T(8,128)(2,1)S(1)} %get-tuple-element.36.refs_0_), channel_id=1, source_target_pairs={{0,128},{16,144},{32,160},{48,176},{64,192},{80,208},{96,224},{112... | collective-permute-start | bytes 245768 | tf_op jit(solution)/shard_map/ppermute | solution.py:54
  66.9 6.4 %collective-permute-start.14 = (bf16[10,16,256]{2,1,0:T(8,128)(2,1)S(1)}, bf16[10,16,256]{2,1,0:T(8,128)(2,1)S(1)}, u32[]{:S(2)}, u32[]{:S(2)}) collective-permute-start(bf16[10,16,256]{2,1,0:T(8,128)(2,1)S(1)} %get-tuple-element.36.refs_0_), channel_id=1, source_target_pairs={{0,192},{16,208},{32,224},{48,240},{64,128},{80,144},{96,160},{112... | collective-permute-start | bytes 245768 | tf_op jit(solution)/shard_map/ppermute | solution.py:54
  73.3 14.1 %collective-permute-start.16 = (bf16[4,10,16,256]{3,2,1,0:T(8,128)(2,1)S(1)}, bf16[4,10,16,256]{3,2,1,0:T(8,128)(2,1)S(1)}, u32[]{:S(2)}, u32[]{:S(2)}) collective-permute-start(bf16[4,10,16,256]{3,2,1,0:T(8,128)(2,1)S(1)} %ahead.1.refs_7_.refs_0_), channel_id=1, source_target_pairs={{0,16},{16,32},{32,48},{48,0},{64,80},{80,96},{96,112},{112,64},{1... | collective-permute-start | bytes 983048 | tf_op jit(solution)/shard_map/ppermute | solution.py:58
  75.0 12.5 %collective-permute-start.17 = (bf16[4,10,16,256]{3,2,1,0:T(8,128)(2,1)S(1)}, bf16[4,10,16,256]{3,2,1,0:T(8,128)(2,1)S(1)}, u32[]{:S(2)}, u32[]{:S(2)}) collective-permute-start(bf16[4,10,16,256]{3,2,1,0:T(8,128)(2,1)S(1)} %ahead.1.refs_7_.refs_0_), channel_id=1, source_target_pairs={{0,32},{16,48},{32,0},{48,16},{64,96},{80,112},{96,64},{112,80},{1... | collective-permute-start | bytes 983048 | tf_op jit(solution)/shard_map/ppermute | solution.py:58
  75.9 12.7 %collective-permute-start.18 = (bf16[4,10,16,256]{3,2,1,0:T(8,128)(2,1)S(1)}, bf16[4,10,16,256]{3,2,1,0:T(8,128)(2,1)S(1)}, u32[]{:S(2)}, u32[]{:S(2)}) collective-permute-start(bf16[4,10,16,256]{3,2,1,0:T(8,128)(2,1)S(1)} %ahead.1.refs_7_.refs_0_), channel_id=1, source_target_pairs={{0,48},{16,0},{32,16},{48,32},{64,112},{80,64},{96,80},{112,96},{1... | collective-permute-start | bytes 983048 | tf_op jit(solution)/shard_map/ppermute | solution.py:58
  78.3 8.5 %collective-permute-start.15 = (f32[8,256]{1,0:T(8,128)S(1)}, f32[8,256]{1,0:T(8,128)S(1)}, u32[]{:S(2)}, u32[]{:S(2)}) collective-permute-start(f32[8,256]{1,0:T(8,128)S(1)} %style.7), channel_id=1, source_target_pairs={{0,1},{1,0},{2,3},{3,2},{4,5},{5,4},{6,7},{7,6},{8,9},{9,8},{10,11... | collective-permute-start | bytes 24584 | tf_op jit(solution)/shard_map/ppermute | solution.py:38

commit v4 on v3

--- a/solution.py
+++ b/solution.py
@@ -58,12 +58,12 @@
     return lax.ppermute(a, "img", img_perm(lambda l, y: (l, (y + k) % NY)))
 
 
-def call(body, outs, in_specs, scratch=(), flops=0, nbytes=0, vmem=16 << 20, name=None):
+def call(body, outs, in_specs, scratch=(), flops=0, nbytes=0, vmem=16 << 20, out=VMEM, name=None):
     return pl.pallas_call(
         body,
         out_shape=outs,
         in_specs=in_specs,
-        out_specs=jax.tree.map(lambda _: VMEM, outs),
+        out_specs=jax.tree.map(lambda _: out, outs),
         scratch_shapes=list(scratch),
         compiler_params=pltpu.CompilerParams(vmem_limit_bytes=vmem),
         cost_estimate=pl.CostEstimate(flops=flops, bytes_accessed=nbytes, transcendentals=0),
@@ -139,23 +139,16 @@
             out[c ^ core, g, :, at] = flat[start : start + 16]
 
 
-def grad_body(place, cot, fm_hbm, grad, ends, fm, cot_t, fm_v, sems, step=4):
+def grad_body(place, cot, fm, grad, ends, cot_t, fm_v, step=4):
     rows, width, channels = cot.shape
     groups = channels // (16 * NC)
     core = place[2]
     parts = rows // step
-    copies = []
-    for q in range(parts):
-        here = pl.ds(q * step, step)
-        copies.append(pltpu.make_async_copy(fm_hbm.at[here], fm.at[here], sems.at[q]))
-    for copy in copies:
-        copy.start()
     nothing = jnp.zeros((NC, groups, 16, width), BF16)
     cot_t[:, :, :, :width] = nothing
     cot_t[:, :, :, (rows + 1) * width :] = nothing
 
     def prepare(q):
-        copies[q].wait()
         for r in range(q * step, (q + 1) * step):
             row = fm[r]
             before, after = moved_columns(row.astype(F32))
@@ -208,9 +201,7 @@
             put(tap + v, grad[tap + v] + out.reshape(NC, groups, 16, channels))
 
 
-def split_x_body(place, mine, got, final, final_c, own, one, two, three, both):
-    both[0] = final[...]
-    both[1] = final_c[...]
+def split_x_body(place, mine, got, own, one, two, three):
     x = place[0]
     for k, out in ((0, own), (1, one), (2, two), (3, three)):
         base = lax.rem(x + k, NX) * NZ
@@ -233,7 +224,8 @@
     return (rows[0:1] + rows[1:2]) + rows[2:3]
 
 
-def split_z_body(place, style, mine, one, two, three, near, got, total, other):
+def split_z_body(place, style, mine, one, two, three, near, got, after, after_too, total, other):
+    del after, after_too
     taps, outs, channels = total.shape
     z = place[1]
     share = jnp.zeros((outs, channels), F32)
@@ -247,11 +239,11 @@
                 total[t] = value
             else:
                 other[t] = value.astype(BF16)
-            dot = dot + value * source[0, t].astype(F32)
+            dot = dot + value * source[t].astype(F32)
             values.append(value)
         dot = jnp.sum(dot, axis=1, keepdims=True)
         for t in range(taps):
-            final = source[0, t].astype(F32)
+            final = source[t].astype(F32)
             share = share + (values[t] - final * dot) * final
     put_row(other.at[taps], jnp.sum(share, axis=0, keepdims=True) / style[...])
 
@@ -279,19 +271,18 @@
     message[taps] = rank.astype(BF16)
 
 
-def four_body(style_row, near, got, four):
-    taps = near.shape[1]
-    for k, source in enumerate((near, got)):
-        for c in range(NC):
-            four[pl.ds((k * NC + c) * taps, taps)] = source[c]
-    put_row(four.at[NZ * NC * taps], style_row[0:1])
-
-
-def style_body(zero, one, two, three, out):
-    last = zero.shape[0] - 1
-    even = take_row(zero.at[last]) + take_row(two.at[last])
-    odd = take_row(one.at[last]) + take_row(three.at[last])
-    out[...] = jnp.broadcast_to(even + odd, out.shape)
+def kernels_body(style_row, *refs):
+    out = refs[-1]
+    taps = refs[0].shape[0]
+    for n, piece in enumerate(refs[:-1]):
+        out[pl.ds(n * taps, taps)] = piece[...]
+    put_row(out.at[(len(refs) - 1) * taps], style_row[0:1])
+
+
+def style_body(*refs):
+    out = refs[-1]
+    zero, one, two, three = [take_row(ref.at[ref.shape[0] - 1]) for ref in refs[:-1]]
+    out[...] = jnp.broadcast_to((zero + two) + (one + three), out.shape)
 
 
 def ahead_body(*refs):
@@ -329,15 +320,11 @@
         copy.wait()
 
 
-def input_body(place, *refs):
+def input_body(place, *refs, step=2):
     finals = refs[:NX]
-    low, high, cot, after, out, final, padded, sem = refs[NX:]
+    low, high, cot, after, out, final, done, sems = refs[NX:]
     del after
-    rows, width, channels = out.shape
-    copy = pltpu.make_async_copy(cot, padded.at[pl.ds(1, rows)], sem)
-    copy.start()
-    padded[0] = low[...]
-    padded[rows + 1] = high[...]
+    rows, width, channels = cot.shape
     x, z, core = place[0], place[1], place[2]
     for k in range(NX):
         for n in range(NZ):
@@ -347,22 +334,30 @@
                 for t in range(9):
                     u, v = t // 3, t % 3
                     final[u, here, v * channels : (v + 1) * channels] = finals[k][(n * NC + c) * 9 + t]
-    copy.wait()
-    step = 2
-
-    @pl.loop(0, rows // step)
-    def _(q):
+
+    def part(start):
+        if start < 0:
+            return jnp.concatenate([low[...], cot[0 : step - 1].reshape((step - 1) * width, channels)], axis=0)
+        if start + step > rows:
+            return jnp.concatenate([cot[start:rows].reshape((rows - start) * width, channels), high[...]], axis=0)
+        return cot[start : start + step].reshape(step * width, channels)
+
+    copies = []
+    for q in range(rows // step):
         r = q * step
-        left = jnp.concatenate(
-            [padded[pl.ds(r + 2 - u, step)].reshape(step * width, channels) for u in range(3)], axis=1
-        )
+        left = jnp.concatenate([part(r + 1 - u) for u in range(3)], axis=1)
         right = final[...].reshape(3 * channels, 3 * channels)
         sums = jnp.dot(left, right, preferred_element_type=F32)
         for n in range(step):
-            part = sums[n * width : (n + 1) * width]
-            _, after = moved_columns(part[:, :channels])
-            before, _ = moved_columns(part[:, 2 * channels :])
-            out[r + n] = (part[:, channels : 2 * channels] + after + before).astype(BF16)
+            piece = sums[n * width : (n + 1) * width]
+            _, after = moved_columns(piece[:, :channels])
+            before, _ = moved_columns(piece[:, 2 * channels :])
+            done[q * step + n] = (piece[:, channels : 2 * channels] + after + before).astype(BF16)
+        copy = pltpu.make_async_copy(done.at[pl.ds(q * step, step)], out.at[pl.ds(r, step)], sems.at[q])
+        copy.start()
+        copies.append(copy)
+    for copy in copies:
+        copy.wait()
 
 
 def local(feature_map, cotangent, style, bank, selection):
@@ -379,7 +374,14 @@
     message_of = (taps + 1, own_out, channels)
 
     last, first = call(
-        rows_body, (shape((width, channels), BF16),) * 2, [HBM], [dma((2, 4))], nbytes=10**6, vmem=60 << 20, name="rows"
+        rows_body,
+        (shape((width, channels), BF16),) * 2,
+        [HBM],
+        [dma((2, 2))],
+        nbytes=10**6,
+        vmem=60 << 20,
+        out=HBM,
+        name="rows",
     )(cot)
     count = lax.axis_size("tile")
     low = lax.ppermute(last, "tile", [(i, i + 1) for i in range(count - 1)])
@@ -388,21 +390,21 @@
     kernel, final = call(
         mix_body, (shape(piece, F32), shape(piece, BF16)), [SMEM, VMEM, VMEM], flops=10**6, nbytes=10**6, name="mix"
     )(selection, style, jnp.transpose(bank, (0, 2, 1, 3)))
+    final_z = swap_z(final)
     final_c = swap_core(final)
+    final_cz = swap_core(final_z)
 
     grad, ends = call(
         grad_body,
         (shape((taps, NC, groups, 16, channels), F32), shape((2, width, channels), BF16)),
-        [SMEM, VMEM, HBM],
+        [SMEM, VMEM, VMEM],
         [
-            pltpu.VMEM((rows, width, channels), BF16),
             pltpu.VMEM((NC, groups, 16, (rows + 2) * width), BF16),
             pltpu.VMEM((3, rows * width, channels), BF16),
-            dma((4,)),
         ],
         flops=2 * 9 * rows * width * channels * channels,
         nbytes=4 * rows * width * channels,
-        vmem=50 << 20,
+        vmem=24 << 20,
         name="grad",
     )(place, cot, fm)
     mine, theirs = call(
@@ -412,27 +414,25 @@
         [pltpu.VMEM((NC, groups, 16, width), BF16)] * 2,
         flops=2 * 6 * width * channels * channels,
         nbytes=4 * 10**6,
-        vmem=50 << 20,
         name="edge",
-    )(place, grad, ends, low, high, final_c)
-
-    own_x, one, two, three, both = call(
+    )(place, grad, ends, low, high, final_z)
+
+    own_x, one, two, three = call(
         split_x_body,
-        (shape(pair, F32),) + (shape(pair, BF16),) * 3 + (shape((NC,) + piece, BF16),),
-        [SMEM] + [VMEM] * 4,
+        (shape(pair, F32),) + (shape(pair, BF16),) * 3,
+        [SMEM] + [VMEM] * 2,
         flops=10**6,
         nbytes=3 * 10**6,
         name="split_x",
-    )(place, mine, swap_core(theirs), final, final_c)
-    got_z = swap_z(both)
+    )(place, mine, swap_core(theirs))
     total, other = call(
         split_z_body,
         (shape(piece, F32), shape(message_of, BF16)),
-        [SMEM] + [VMEM] * 7,
+        [SMEM] + [VMEM] * 9,
         flops=10**6,
         nbytes=10**6,
         name="split_z",
-    )(place, style, own_x, shift_x(one, 1), shift_x(two, 2), shift_x(three, 3), both, got_z)
+    )(place, style, own_x, shift_x(one, 1), shift_x(two, 2), shift_x(three, 3), final, final_z, final_c, final_cz)
     message, style_row = call(
         owner_body,
         (shape(message_of, BF16), shape((8, channels), F32)),
@@ -442,15 +442,15 @@
         name="owner",
     )(selection, style, kernel, total, other, swap_z(other))
 
-    four = call(
-        four_body,
+    kernels = call(
+        kernels_body,
         shape((NZ * NC * taps + 1, own_out, channels), BF16),
-        [VMEM] * 3,
+        [VMEM] * 5,
         flops=10**9,
         nbytes=10**7,
-        name="four",
-    )(style_row, both, got_z)
-    finals = [four] + [shift_x(four, k) for k in range(1, NX)]
+        name="kernels",
+    )(style_row, final, final_c, final_z, final_cz)
+    finals = [kernels] + [shift_x(kernels, k) for k in range(1, NX)]
     style_part = call(style_body, shape((8, channels), F32), [VMEM] * NX, name="style")(*finals)
     style_sum = style_part + swap_core(style_part)
 
@@ -461,15 +461,16 @@
     input_grad = call(
         input_body,
         shape((rows, width, channels), BF16),
-        [SMEM] + [VMEM] * (NX + 2) + [HBM, VMEM],
+        [SMEM] + [VMEM] * (NX + 4),
         [
             pltpu.VMEM((3, channels, 3 * channels), BF16),
-            pltpu.VMEM((rows + 2, width, channels), BF16),
-            dma,
+            pltpu.VMEM((rows, width, channels), BF16),
+            dma((8,)),
         ],
         flops=2 * 9 * rows * width * channels * channels,
         nbytes=4 * rows * width * channels,
-        vmem=50 << 20,
+        vmem=24 << 20,
+        out=HBM,
         name="input",
     )(place, *finals, low, high, cot, ahead)
 

time: 91.6 us -> 94.7 us (1.034); the launches traced: 90 us -> 94.5 us
  waiting for transfers between devices: 15.3 us -> 23 us
  starting transfers between devices: 45.5 us -> 40.4 us
  local copies, waits for them, and re-layouts: 1.07 us -> 2.66 us
    ppermute x3 -> x4, starting transfers between devices: 8.39 us -> 0.7 us  [swap_core(): return lax.ppermute(a, 'tile', tile_perm(lambda x, z, c: (x, z, 1 - c)))]
    pallas_call x3, Pallas kernels: 2.51 us -> 9.77 us  [the longest x1 9.08 us: local(): call(rows_body, (shape((width, channels), BF16),) * 2, [HBM], [dma((2, 2)...]
    ppermute x6, waiting for transfers between devices: 0.02 us -> 4.17 us  [shift_x(): lax.ppermute(a, 'tile', tile_perm(lambda x, z, c: ((x + k) % NX, z, c)))]
    pallas_call x1, Pallas kernels: 10.1 us -> 6.12 us  [local(): call(grad_body, (shape((taps, NC, groups, 16, channels), F32), shape((2,...]
    ppermute x2, starting transfers between devices: 12.1 us -> 15.7 us  [swap_z(): return lax.ppermute(a, 'tile', tile_perm(lambda x, z, c: (x, 1 - z, c)))]
    ppermute x3, waiting for transfers between devices: 1.15 us -> 3.49 us  [shift_y(): return lax.ppermute(a, 'img', img_perm(lambda l, y: (l, (y + k) % NY)))]
    ppermute x3, starting transfers between devices: 7.77 us -> 5.67 us  [flip_l(): return lax.ppermute(a, 'img', img_perm(lambda l, y: (l ^ k, y)))]
    ppermute x3, waiting for transfers between devices: 3.06 us -> 5.11 us  [flip_l(): return lax.ppermute(a, 'img', img_perm(lambda l, y: (l ^ k, y)))]
  transfers between devices with their start and end apart: 19 -> 20, of which waited for: 7 -> 9; matrix products, arithmetic and copies ran while one was open for 1% -> 1% of each run, Pallas kernels for 21% -> 14%
where the time goes in v4:
time: 94.7 us; the launch traced here: 94.5 us
  starting transfers between devices  40.4 us (43%)
  Pallas kernels  26.8 us (28%)
  waiting for transfers between devices  23 us (24%)
  local copies, waits for them, and re-layouts  2.66 us (3%)
  between operations  0.98 us (1%)
    ppermute x2, starting transfers between devices, swap_z(): return lax.ppermute(a, 'tile', tile_perm(lambda x, z, c: (x, 1 - z, c)))  15.7 us
    ppermute x6, starting transfers between devices, shift_x(): lax.ppermute(a, 'tile', tile_perm(lambda x, z, c: ((x + k) % NX, z, c)))  10.2 us
    pallas_call x1, Pallas kernels, local(): call(rows_body, (shape((width, channels), BF16),) * 2, [HBM], [dma((2, 2)...  9.08 us
    ppermute x2, waiting for transfers between devices, swap_z(): return lax.ppermute(a, 'tile', tile_perm(lambda x, z, c: (x, 1 - z, c)))  7.35 us
    pallas_call x1, Pallas kernels, local(): call(input_body, shape((rows, width, channels), BF16), [SMEM] + [VMEM] *...  6.47 us
    pallas_call x1, Pallas kernels, local(): call(grad_body, (shape((taps, NC, groups, 16, channels), F32), shape((2,...  6.12 us
    ppermute x3, starting transfers between devices, flip_l(): return lax.ppermute(a, 'img', img_perm(lambda l, y: (l ^ k, y)))  5.67 us
    ppermute x3, waiting for transfers between devices, flip_l(): return lax.ppermute(a, 'img', img_perm(lambda l, y: (l ^ k, y)))  5.11 us
  transfers between devices with their start and end apart: 20, of which 9 were waited for; matrix products, arithmetic and copies ran while one was open for 1% of the time, Pallas kernels for 14%

profile of v4, /device:TPU:8, one launch (start us, length us, event | category | flops | bytes accessed | tf_op | source)
XLA Modules:
  0.0 94.5 jit_solution(16671120199648197494)
XLA Ops:
  0.7 9.1 %rows.1 = (bf16[256,256]{1,0:T(8,128)(2,1)}, bf16[256,256]{1,0:T(8,128)(2,1)}) custom-call(bf16[16,256,256]{2,1,0:T(8,128)(2,1)} %bitcast.8), custom_call_target="tpu_custom_call" | custom-call | bytes 1000000 | tf_op jit(solution)/shard_map/rows/pallas_call | solution.py:376
  9.7 1.7 %collective-permute-start = (bf16[256,256]{1,0:T(8,128)(2,1)}, bf16[256,256]{1,0:T(8,128)(2,1)S(1)}, u32[]{:S(2)}, u32[]{:S(2)}) collective-permute-start(bf16[256,256]{1,0:T(8,128)(2,1)} %get-tuple-element.22), channel_id=1, source_target_pairs={{0,1},{1,2},{2,3},{3,4},{4,5},{5,6},{6,7},{7,8},{8,9},{9,10},{10,1... | collective-permute-start | bytes 393224 | tf_op jit(solution)/shard_map/ppermute | solution.py:387
  11.5 1.3 %collective-permute-start.1 = (bf16[256,256]{1,0:T(8,128)(2,1)}, bf16[256,256]{1,0:T(8,128)(2,1)S(1)}, u32[]{:S(2)}, u32[]{:S(2)}) collective-permute-start(bf16[256,256]{1,0:T(8,128)(2,1)} %get-tuple-element.23), channel_id=1, source_target_pairs={{1,0},{2,1},{3,2},{4,3},{5,4},{6,5},{7,6},{8,7},{9,8},{10,9},{11,1... | collective-permute-start | bytes 393224 | tf_op jit(solution)/shard_map/ppermute | solution.py:388
  12.8 1.1 %copy-done.1 = bf16[8,16,9,256]{3,1,2,0:T(8,128)(2,1)S(1)} copy-done((bf16[8,16,9,256]{3,1,2,0:T(8,128)(2,1)S(1)}, bf16[8,16,9,256]{3,1,2,0:T(8,128)(2,1)}, u32[]{:S(2)}) %copy-start.1) | copy-done | bytes 589848
  13.9 0.8 mix.1
  14.6 13.7 %collective-permute-start.2 = (bf16[9,16,256]{2,1,0:T(8,128)(2,1)S(1)}, bf16[9,16,256]{2,1,0:T(8,128)(2,1)S(1)}, u32[]{:S(2)}, u32[]{:S(2)}) collective-permute-start(bf16[9,16,256]{2,1,0:T(8,128)(2,1)S(1)} %get-tuple-element.24.near.refs_0_), channel_id=1, source_target_pairs={{0,2},{1,3},{2,0},{3,1},{4,6},{5,7},{6,4},{7,5},{8,10},{9,11},{10,... | collective-permute-start | bytes 221192 | tf_op jit(solution)/shard_map/ppermute | solution.py:42
  28.4 1.6 %copy-done.4 = bf16[1,16,256,256]{3,2,1,0:T(8,128)(2,1)S(1)} copy-done((bf16[1,16,256,256]{3,2,1,0:T(8,128)(2,1)S(1)}, bf16[1,16,256,256]{3,2,1,0:T(8,128)(2,1)}, u32[]{:S(2)}) %copy-start.4) | copy-done | bytes 2097176
  30.0 6.1 %grad.1 = (f32[9,2,8,16,256]{4,3,2,1,0:T(8,128)S(1)}, bf16[2,256,256]{2,1,0:T(8,128)(2,1)S(1)}) custom-call(s32[3]{0:T(128)S(1)} %pad_add_fusion.place, bf16[16,256,256]{2,1,0:T(8,128)(2,1)S(1)} %bitcast.9, bf16[16,256,256]{2,1,0:T(8,128)(2,1)S(1)} %bitcast.12), custom_call_target="tpu_custom_call" | custom-call | flops 4831838208 | bytes 4194304 | tf_op jit(solution)/shard_map/grad/pallas_call | solution.py:397
  36.2 1.0 %edge.1 = (f32[8,9,16,256]{3,2,1,0:T(8,128)S(1)}, bf16[8,9,16,256]{3,2,1,0:T(8,128)(2,1)S(1)}) custom-call(s32[3]{0:T(128)S(1)} %pad_add_fusion.place, f32[9,2,8,16,256]{4,3,2,1,0:T(8,128)S(1)} %get-tuple-element.20.grad, bf16[2,256,256]{2,1,0:T(8,128)(2,1)S(1)} %get-tuple-element.21.ends, bf16[256,256]{1,0:T(8,128)(2,1)S(1)} %collective-permute-done.low.refs_4_, ...), custom_call_target="tpu_custom_call" | custom-call | flops 201326592 | bytes 4000000 | tf_op jit(solution)/shard_map/edge/pallas_call | solution.py:410
  37.3 2.0 %collective-permute-done.3.got = bf16[8,9,16,256]{3,2,1,0:T(8,128)(2,1)S(1)} collective-permute-done((bf16[8,9,16,256]{3,2,1,0:T(8,128)(2,1)S(1)}, bf16[8,9,16,256]{3,2,1,0:T(8,128)(2,1)S(1)}, u32[]{:S(2)}, u32[]{:S(2)}) %collective-permute-start.3) | collective-permute-done | bytes 589856 | tf_op jit(solution)/shard_map/ppermute | solution.py:38
  39.9 1.6 %collective-permute-start.4 = (bf16[2,9,16,256]{3,2,1,0:T(8,128)(2,1)S(1)}, bf16[2,9,16,256]{3,2,1,0:T(8,128)(2,1)S(1)}, u32[]{:S(2)}, u32[]{:S(2)}) collective-permute-start(bf16[2,9,16,256]{3,2,1,0:T(8,128)(2,1)S(1)} %get-tuple-element.28), channel_id=1, source_target_pairs={{0,4},{1,5},{2,6},{3,7},{4,8},{5,9},{6,10},{7,11},{8,12},{9,13},{1... | collective-permute-start | bytes 442376 | tf_op jit(solution)/shard_map/ppermute | solution.py:46
  41.5 2.7 %collective-permute-start.5 = (bf16[2,9,16,256]{3,2,1,0:T(8,128)(2,1)S(1)}, bf16[2,9,16,256]{3,2,1,0:T(8,128)(2,1)S(1)}, u32[]{:S(2)}, u32[]{:S(2)}) collective-permute-start(bf16[2,9,16,256]{3,2,1,0:T(8,128)(2,1)S(1)} %get-tuple-element.29), channel_id=1, source_target_pairs={{0,8},{1,9},{2,10},{3,11},{4,12},{5,13},{6,14},{7,15},{8,0},{9,1},... | collective-permute-start | bytes 442376 | tf_op jit(solution)/shard_map/ppermute | solution.py:46
  44.2 1.4 %collective-permute-start.6 = (bf16[2,9,16,256]{3,2,1,0:T(8,128)(2,1)S(1)}, bf16[2,9,16,256]{3,2,1,0:T(8,128)(2,1)S(1)}, u32[]{:S(2)}, u32[]{:S(2)}) collective-permute-start(bf16[2,9,16,256]{3,2,1,0:T(8,128)(2,1)S(1)} %get-tuple-element.30), channel_id=1, source_target_pairs={{0,12},{1,13},{2,14},{3,15},{4,0},{5,1},{6,2},{7,3},{8,4},{9,5},{1... | collective-permute-start | bytes 442376 | tf_op jit(solution)/shard_map/ppermute | solution.py:46
  46.2 0.8 collective-permute-done.7.after.refs_1_
  47.1 4.1 %collective-permute-done.5.two = bf16[2,9,16,256]{3,2,1,0:T(8,128)(2,1)S(1)} collective-permute-done((bf16[2,9,16,256]{3,2,1,0:T(8,128)(2,1)S(1)}, bf16[2,9,16,256]{3,2,1,0:T(8,128)(2,1)S(1)}, u32[]{:S(2)}, u32[]{:S(2)}) %collective-permute-start.5) | collective-permute-done | bytes 147488 | tf_op jit(solution)/shard_map/ppermute | solution.py:46
  51.2 0.7 split_z.1
  52.0 2.1 %collective-permute-start.9 = (bf16[10,16,256]{2,1,0:T(8,128)(2,1)S(1)}, bf16[10,16,256]{2,1,0:T(8,128)(2,1)S(1)}, u32[]{:S(2)}, u32[]{:S(2)}) collective-permute-start(bf16[10,16,256]{2,1,0:T(8,128)(2,1)S(1)} %get-tuple-element.32.sent), channel_id=1, source_target_pairs={{0,2},{1,3},{2,0},{3,1},{4,6},{5,7},{6,4},{7,5},{8,10},{9,11},{10,... | collective-permute-start | bytes 245768 | tf_op jit(solution)/shard_map/ppermute | solution.py:42
  54.0 7.3 %collective-permute-done.9.got = bf16[10,16,256]{2,1,0:T(8,128)(2,1)S(1)} collective-permute-done((bf16[10,16,256]{2,1,0:T(8,128)(2,1)S(1)}, bf16[10,16,256]{2,1,0:T(8,128)(2,1)S(1)}, u32[]{:S(2)}, u32[]{:S(2)}) %collective-permute-start.9) | collective-permute-done | bytes 81952 | tf_op jit(solution)/shard_map/ppermute | solution.py:42
  62.1 1.2 %collective-permute-start.10 = (bf16[37,16,256]{2,1,0:T(8,128)(2,1)S(1)}, bf16[37,16,256]{2,1,0:T(8,128)(2,1)S(1)}, u32[]{:S(2)}, u32[]{:S(2)}) collective-permute-start(bf16[37,16,256]{2,1,0:T(8,128)(2,1)S(1)} %kernels.1.refs_0_), channel_id=1, source_target_pairs={{0,4},{1,5},{2,6},{3,7},{4,8},{5,9},{6,10},{7,11},{8,12},{9,13},{1... | collective-permute-start | bytes 909320 | tf_op jit(solution)/shard_map/ppermute | solution.py:46
  63.3 2.7 %collective-permute-start.11 = (bf16[37,16,256]{2,1,0:T(8,128)(2,1)S(1)}, bf16[37,16,256]{2,1,0:T(8,128)(2,1)S(1)}, u32[]{:S(2)}, u32[]{:S(2)}) collective-permute-start(bf16[37,16,256]{2,1,0:T(8,128)(2,1)S(1)} %kernels.1.refs_0_), channel_id=1, source_target_pairs={{0,8},{1,9},{2,10},{3,11},{4,12},{5,13},{6,14},{7,15},{8,0},{9,1},... | collective-permute-start | bytes 909320 | tf_op jit(solution)/shard_map/ppermute | solution.py:46
  66.6 0.9 collective-permute-start.13
  67.5 2.0 %collective-permute-start.14 = (bf16[10,16,256]{2,1,0:T(8,128)(2,1)S(1)}, bf16[10,16,256]{2,1,0:T(8,128)(2,1)S(1)}, u32[]{:S(2)}, u32[]{:S(2)}) collective-permute-start(bf16[10,16,256]{2,1,0:T(8,128)(2,1)S(1)} %get-tuple-element.34.refs_0_), channel_id=1, source_target_pairs={{0,128},{16,144},{32,160},{48,176},{64,192},{80,208},{96,224},{112... | collective-permute-start | bytes 245768 | tf_op jit(solution)/shard_map/ppermute | solution.py:54
  69.5 1.5 %collective-permute-done.13.refs_1_ = bf16[10,16,256]{2,1,0:T(8,128)(2,1)S(1)} collective-permute-done((bf16[10,16,256]{2,1,0:T(8,128)(2,1)S(1)}, bf16[10,16,256]{2,1,0:T(8,128)(2,1)S(1)}, u32[]{:S(2)}, u32[]{:S(2)}) %collective-permute-start.13) | collective-permute-done | bytes 81952 | tf_op jit(solution)/shard_map/ppermute | solution.py:54
  71.0 2.7 %collective-permute-start.15 = (bf16[10,16,256]{2,1,0:T(8,128)(2,1)S(1)}, bf16[10,16,256]{2,1,0:T(8,128)(2,1)S(1)}, u32[]{:S(2)}, u32[]{:S(2)}) collective-permute-start(bf16[10,16,256]{2,1,0:T(8,128)(2,1)S(1)} %get-tuple-element.34.refs_0_), channel_id=1, source_target_pairs={{0,192},{16,208},{32,224},{48,240},{64,128},{80,144},{96,160},{112... | collective-permute-start | bytes 245768 | tf_op jit(solution)/shard_map/ppermute | solution.py:54
  73.8 3.6 %collective-permute-done.15.refs_3_ = bf16[10,16,256]{2,1,0:T(8,128)(2,1)S(1)} collective-permute-done((bf16[10,16,256]{2,1,0:T(8,128)(2,1)S(1)}, bf16[10,16,256]{2,1,0:T(8,128)(2,1)S(1)}, u32[]{:S(2)}, u32[]{:S(2)}) %collective-permute-start.15) | collective-permute-done | bytes 81952 | tf_op jit(solution)/shard_map/ppermute | solution.py:54
  77.4 1.7 %collective-permute-start.17 = (bf16[4,10,16,256]{3,2,1,0:T(8,128)(2,1)S(1)}, bf16[4,10,16,256]{3,2,1,0:T(8,128)(2,1)S(1)}, u32[]{:S(2)}, u32[]{:S(2)}) collective-permute-start(bf16[4,10,16,256]{3,2,1,0:T(8,128)(2,1)S(1)} %ahead.1.refs_7_.refs_0_), channel_id=1, source_target_pairs={{0,16},{16,32},{32,48},{48,0},{64,80},{80,96},{96,112},{112,64},{1... | collective-permute-start | bytes 983048 | tf_op jit(solution)/shard_map/ppermute | solution.py:58
  79.1 0.9 collective-permute-start.18
  80.0 2.4 %collective-permute-start.19 = (bf16[4,10,16,256]{3,2,1,0:T(8,128)(2,1)S(1)}, bf16[4,10,16,256]{3,2,1,0:T(8,128)(2,1)S(1)}, u32[]{:S(2)}, u32[]{:S(2)}) collective-permute-start(bf16[4,10,16,256]{3,2,1,0:T(8,128)(2,1)S(1)} %ahead.1.refs_7_.refs_0_), channel_id=1, source_target_pairs={{0,48},{16,0},{32,16},{48,32},{64,112},{80,64},{96,80},{112,96},{1... | collective-permute-start | bytes 983048 | tf_op jit(solution)/shard_map/ppermute | solution.py:58
  82.6 6.5 %input.1 = bf16[16,256,256]{2,1,0:T(8,128)(2,1)} custom-call(s32[3]{0:T(128)S(1)} %pad_add_fusion.place, bf16[37,16,256]{2,1,0:T(8,128)(2,1)S(1)} %kernels.1.refs_0_, bf16[37,16,256]{2,1,0:T(8,128)(2,1)S(1)} %collective-permute-done.10.refs_1_, bf16[37,16,256]{2,1,0:T(8,128)(2,1)S(1)} %collective-permute-done.11.refs_2_, ...), custom_call_target="tpu_custom_call" | custom-call | flops 4831838208 | bytes 4194304 | tf_op jit(solution)/shard_map/input/pallas_call | solution.py:461
  89.6 0.8 collective-permute-done.18.refs_2_
  90.4 2.7 %collective-permute-done.19.refs_3_ = bf16[4,10,16,256]{3,2,1,0:T(8,128)(2,1)S(1)} collective-permute-done((bf16[4,10,16,256]{3,2,1,0:T(8,128)(2,1)S(1)}, bf16[4,10,16,256]{3,2,1,0:T(8,128)(2,1)S(1)}, u32[]{:S(2)}, u32[]{:S(2)}) %collective-permute-start.19) | collective-permute-done | bytes 327712 | tf_op jit(solution)/shard_map/ppermute | solution.py:58
  93.1 1.3 %banks.1 = f32[8,9,16,256]{3,2,1,0:T(8,128)} custom-call(bf16[4,10,16,256]{3,2,1,0:T(8,128)(2,1)S(1)} %ahead.1.refs_7_.refs_0_, bf16[4,10,16,256]{3,2,1,0:T(8,128)(2,1)S(1)} %collective-permute-done.17.refs_1_, bf16[4,10,16,256]{3,2,1,0:T(8,128)(2,1)S(1)} %collective-permute-done.18.refs_2_, bf16[4,10,16,256]{3,2,1,0:T(8,128)(2,1)S(1)} %collective-permute-done.19.refs_3_), custom_call_target="tpu_custom_call" | custom-call | flops 10000000 | bytes 3000000 | tf_op jit(solution)/shard_map/banks/pallas_call | solution.py:477
  (32 shorter events, 3.5 us)
Async XLA Ops:
  0.6 27.8 %copy-start = (bf16[1,16,256,256]{3,2,1,0:T(8,128)(2,1)S(1)}, bf16[1,16,256,256]{3,2,1,0:T(8,128)(2,1)}, u32[]{:S(2)}) copy-start(bf16[1,16,256,256]{3,2,1,0:T(8,128)(2,1)} %param.6) | copy-start | bytes 6291460
  0.6 12.2 %copy-start.3 = (s32[1,3]{1,0:T(1,128)S(1)}, s32[1,3]{1,0:T(1,128)}, u32[]{:S(2)}) copy-start(s32[1,3]{1,0:T(1,128)} %sel.3) | copy-start | bytes 40
  0.7 12.2 %copy-start.2 = (f32[1,256]{1,0:T(1,128)S(1)}, f32[1,256]{1,0:T(1,128)}, u32[]{:S(2)}) copy-start(f32[1,256]{1,0:T(1,128)} %style.6) | copy-start | bytes 3076
  9.7 26.4 %collective-permute-start = (bf16[256,256]{1,0:T(8,128)(2,1)}, bf16[256,256]{1,0:T(8,128)(2,1)S(1)}, u32[]{:S(2)}, u32[]{:S(2)}) collective-permute-start(bf16[256,256]{1,0:T(8,128)(2,1)} %get-tuple-element.22), channel_id=1, source_target_pairs={{0,1},{1,2},{2,3},{3,4},{4,5},{5,6},{6,7},{7,8},{8,9},{9,10},{10,1... | collective-permute-start | bytes 393224 | tf_op jit(solution)/shard_map/ppermute | solution.py:387
  11.5 24.6 %collective-permute-start.1 = (bf16[256,256]{1,0:T(8,128)(2,1)}, bf16[256,256]{1,0:T(8,128)(2,1)S(1)}, u32[]{:S(2)}, u32[]{:S(2)}) collective-permute-start(bf16[256,256]{1,0:T(8,128)(2,1)} %get-tuple-element.23), channel_id=1, source_target_pairs={{1,0},{2,1},{3,2},{4,3},{5,4},{6,5},{7,6},{8,7},{9,8},{10,9},{11,1... | collective-permute-start | bytes 393224 | tf_op jit(solution)/shard_map/ppermute | solution.py:388
  12.8 1.1 %copy-start.1 = (bf16[8,16,9,256]{3,1,2,0:T(8,128)(2,1)S(1)}, bf16[8,16,9,256]{3,1,2,0:T(8,128)(2,1)}, u32[]{:S(2)}) copy-start(bf16[8,16,9,256]{3,1,2,0:T(8,128)(2,1)} %param.8) | copy-start | bytes 1769476
  14.6 21.5 %collective-permute-start.2 = (bf16[9,16,256]{2,1,0:T(8,128)(2,1)S(1)}, bf16[9,16,256]{2,1,0:T(8,128)(2,1)S(1)}, u32[]{:S(2)}, u32[]{:S(2)}) collective-permute-start(bf16[9,16,256]{2,1,0:T(8,128)(2,1)S(1)} %get-tuple-element.24.near.refs_0_), channel_id=1, source_target_pairs={{0,2},{1,3},{2,0},{3,1},{4,6},{5,7},{6,4},{7,5},{8,10},{9,11},{10,... | collective-permute-start | bytes 221192 | tf_op jit(solution)/shard_map/ppermute | solution.py:42
  28.4 1.6 %copy-start.4 = (bf16[1,16,256,256]{3,2,1,0:T(8,128)(2,1)S(1)}, bf16[1,16,256,256]{3,2,1,0:T(8,128)(2,1)}, u32[]{:S(2)}) copy-start(bf16[1,16,256,256]{3,2,1,0:T(8,128)(2,1)} %param.5) | copy-start | bytes 6291460
  37.2 2.1 %collective-permute-start.3 = (bf16[8,9,16,256]{3,2,1,0:T(8,128)(2,1)S(1)}, bf16[8,9,16,256]{3,2,1,0:T(8,128)(2,1)S(1)}, u32[]{:S(2)}, u32[]{:S(2)}) collective-permute-start(bf16[8,9,16,256]{3,2,1,0:T(8,128)(2,1)S(1)} %get-tuple-element.26), channel_id=1, source_target_pairs={{0,1},{1,0},{2,3},{3,2},{4,5},{5,4},{6,7},{7,6},{8,9},{9,8},{10,11... | collective-permute-start | bytes 1769480 | tf_op jit(solution)/shard_map/ppermute | solution.py:38
  39.9 7.2 %collective-permute-start.4 = (bf16[2,9,16,256]{3,2,1,0:T(8,128)(2,1)S(1)}, bf16[2,9,16,256]{3,2,1,0:T(8,128)(2,1)S(1)}, u32[]{:S(2)}, u32[]{:S(2)}) collective-permute-start(bf16[2,9,16,256]{3,2,1,0:T(8,128)(2,1)S(1)} %get-tuple-element.28), channel_id=1, source_target_pairs={{0,4},{1,5},{2,6},{3,7},{4,8},{5,9},{6,10},{7,11},{8,12},{9,13},{1... | collective-permute-start | bytes 442376 | tf_op jit(solution)/shard_map/ppermute | solution.py:46
  41.5 9.7 %collective-permute-start.5 = (bf16[2,9,16,256]{3,2,1,0:T(8,128)(2,1)S(1)}, bf16[2,9,16,256]{3,2,1,0:T(8,128)(2,1)S(1)}, u32[]{:S(2)}, u32[]{:S(2)}) collective-permute-start(bf16[2,9,16,256]{3,2,1,0:T(8,128)(2,1)S(1)} %get-tuple-element.29), channel_id=1, source_target_pairs={{0,8},{1,9},{2,10},{3,11},{4,12},{5,13},{6,14},{7,15},{8,0},{9,1},... | collective-permute-start | bytes 442376 | tf_op jit(solution)/shard_map/ppermute | solution.py:46
  44.2 7.0 %collective-permute-start.6 = (bf16[2,9,16,256]{3,2,1,0:T(8,128)(2,1)S(1)}, bf16[2,9,16,256]{3,2,1,0:T(8,128)(2,1)S(1)}, u32[]{:S(2)}, u32[]{:S(2)}) collective-permute-start(bf16[2,9,16,256]{3,2,1,0:T(8,128)(2,1)S(1)} %get-tuple-element.30), channel_id=1, source_target_pairs={{0,12},{1,13},{2,14},{3,15},{4,0},{5,1},{6,2},{7,3},{8,4},{9,5},{1... | collective-permute-start | bytes 442376 | tf_op jit(solution)/shard_map/ppermute | solution.py:46
  45.6 1.3 %collective-permute-start.7 = (bf16[9,16,256]{2,1,0:T(8,128)(2,1)S(1)}, bf16[9,16,256]{2,1,0:T(8,128)(2,1)S(1)}, u32[]{:S(2)}, u32[]{:S(2)}) collective-permute-start(bf16[9,16,256]{2,1,0:T(8,128)(2,1)S(1)} %get-tuple-element.24.near.refs_0_), channel_id=1, source_target_pairs={{0,1},{1,0},{2,3},{3,2},{4,5},{5,4},{6,7},{7,6},{8,9},{9,8},{10,11... | collective-permute-start | bytes 221192 | tf_op jit(solution)/shard_map/ppermute | solution.py:38
  45.7 1.4 %collective-permute-start.8 = (bf16[9,16,256]{2,1,0:T(8,128)(2,1)S(1)}, bf16[9,16,256]{2,1,0:T(8,128)(2,1)S(1)}, u32[]{:S(2)}, u32[]{:S(2)}) collective-permute-start(bf16[9,16,256]{2,1,0:T(8,128)(2,1)S(1)} %collective-permute-done.2.after.got.refs_2_), channel_id=1, source_target_pairs={{0,1},{1,0},{2,3},{3,2},{4,5},{5,4},{6,7},{7,6},{8,9},{9,8},{10,11... | collective-permute-start | bytes 221192 | tf_op jit(solution)/shard_map/ppermute | solution.py:38
  52.0 9.4 %collective-permute-start.9 = (bf16[10,16,256]{2,1,0:T(8,128)(2,1)S(1)}, bf16[10,16,256]{2,1,0:T(8,128)(2,1)S(1)}, u32[]{:S(2)}, u32[]{:S(2)}) collective-permute-start(bf16[10,16,256]{2,1,0:T(8,128)(2,1)S(1)} %get-tuple-element.32.sent), channel_id=1, source_target_pairs={{0,2},{1,3},{2,0},{3,1},{4,6},{5,7},{6,4},{7,5},{8,10},{9,11},{10,... | collective-permute-start | bytes 245768 | tf_op jit(solution)/shard_map/ppermute | solution.py:42
  62.1 17.9 %collective-permute-start.10 = (bf16[37,16,256]{2,1,0:T(8,128)(2,1)S(1)}, bf16[37,16,256]{2,1,0:T(8,128)(2,1)S(1)}, u32[]{:S(2)}, u32[]{:S(2)}) collective-permute-start(bf16[37,16,256]{2,1,0:T(8,128)(2,1)S(1)} %kernels.1.refs_0_), channel_id=1, source_target_pairs={{0,4},{1,5},{2,6},{3,7},{4,8},{5,9},{6,10},{7,11},{8,12},{9,13},{1... | collective-permute-start | bytes 909320 | tf_op jit(solution)/shard_map/ppermute | solution.py:46
  63.3 19.1 %collective-permute-start.11 = (bf16[37,16,256]{2,1,0:T(8,128)(2,1)S(1)}, bf16[37,16,256]{2,1,0:T(8,128)(2,1)S(1)}, u32[]{:S(2)}, u32[]{:S(2)}) collective-permute-start(bf16[37,16,256]{2,1,0:T(8,128)(2,1)S(1)} %kernels.1.refs_0_), channel_id=1, source_target_pairs={{0,8},{1,9},{2,10},{3,11},{4,12},{5,13},{6,14},{7,15},{8,0},{9,1},... | collective-permute-start | bytes 909320 | tf_op jit(solution)/shard_map/ppermute | solution.py:46
  66.0 16.4 %collective-permute-start.12 = (bf16[37,16,256]{2,1,0:T(8,128)(2,1)S(1)}, bf16[37,16,256]{2,1,0:T(8,128)(2,1)S(1)}, u32[]{:S(2)}, u32[]{:S(2)}) collective-permute-start(bf16[37,16,256]{2,1,0:T(8,128)(2,1)S(1)} %kernels.1.refs_0_), channel_id=1, source_target_pairs={{0,12},{1,13},{2,14},{3,15},{4,0},{5,1},{6,2},{7,3},{8,4},{9,5},{1... | collective-permute-start | bytes 909320 | tf_op jit(solution)/shard_map/ppermute | solution.py:46
  66.6 4.4 %collective-permute-start.13 = (bf16[10,16,256]{2,1,0:T(8,128)(2,1)S(1)}, bf16[10,16,256]{2,1,0:T(8,128)(2,1)S(1)}, u32[]{:S(2)}, u32[]{:S(2)}) collective-permute-start(bf16[10,16,256]{2,1,0:T(8,128)(2,1)S(1)} %get-tuple-element.34.refs_0_), channel_id=1, source_target_pairs={{0,64},{16,80},{32,96},{48,112},{64,0},{80,16},{96,32},{112,48},{1... | collective-permute-start | bytes 245768 | tf_op jit(solution)/shard_map/ppermute | solution.py:54
  67.5 6.2 %collective-permute-start.14 = (bf16[10,16,256]{2,1,0:T(8,128)(2,1)S(1)}, bf16[10,16,256]{2,1,0:T(8,128)(2,1)S(1)}, u32[]{:S(2)}, u32[]{:S(2)}) collective-permute-start(bf16[10,16,256]{2,1,0:T(8,128)(2,1)S(1)} %get-tuple-element.34.refs_0_), channel_id=1, source_target_pairs={{0,128},{16,144},{32,160},{48,176},{64,192},{80,208},{96,224},{112... | collective-permute-start | bytes 245768 | tf_op jit(solution)/shard_map/ppermute | solution.py:54
  71.0 6.3 %collective-permute-start.15 = (bf16[10,16,256]{2,1,0:T(8,128)(2,1)S(1)}, bf16[10,16,256]{2,1,0:T(8,128)(2,1)S(1)}, u32[]{:S(2)}, u32[]{:S(2)}) collective-permute-start(bf16[10,16,256]{2,1,0:T(8,128)(2,1)S(1)} %get-tuple-element.34.refs_0_), channel_id=1, source_target_pairs={{0,192},{16,208},{32,224},{48,240},{64,128},{80,144},{96,160},{112... | collective-permute-start | bytes 245768 | tf_op jit(solution)/shard_map/ppermute | solution.py:54
  77.4 12.2 %collective-permute-start.17 = (bf16[4,10,16,256]{3,2,1,0:T(8,128)(2,1)S(1)}, bf16[4,10,16,256]{3,2,1,0:T(8,128)(2,1)S(1)}, u32[]{:S(2)}, u32[]{:S(2)}) collective-permute-start(bf16[4,10,16,256]{3,2,1,0:T(8,128)(2,1)S(1)} %ahead.1.refs_7_.refs_0_), channel_id=1, source_target_pairs={{0,16},{16,32},{32,48},{48,0},{64,80},{80,96},{96,112},{112,64},{1... | collective-permute-start | bytes 983048 | tf_op jit(solution)/shard_map/ppermute | solution.py:58
  79.1 11.3 %collective-permute-start.18 = (bf16[4,10,16,256]{3,2,1,0:T(8,128)(2,1)S(1)}, bf16[4,10,16,256]{3,2,1,0:T(8,128)(2,1)S(1)}, u32[]{:S(2)}, u32[]{:S(2)}) collective-permute-start(bf16[4,10,16,256]{3,2,1,0:T(8,128)(2,1)S(1)} %ahead.1.refs_7_.refs_0_), channel_id=1, source_target_pairs={{0,32},{16,48},{32,0},{48,16},{64,96},{80,112},{96,64},{112,80},{1... | collective-permute-start | bytes 983048 | tf_op jit(solution)/shard_map/ppermute | solution.py:58
  80.0 13.1 %collective-permute-start.19 = (bf16[4,10,16,256]{3,2,1,0:T(8,128)(2,1)S(1)}, bf16[4,10,16,256]{3,2,1,0:T(8,128)(2,1)S(1)}, u32[]{:S(2)}, u32[]{:S(2)}) collective-permute-start(bf16[4,10,16,256]{3,2,1,0:T(8,128)(2,1)S(1)} %ahead.1.refs_7_.refs_0_), channel_id=1, source_target_pairs={{0,48},{16,0},{32,16},{48,32},{64,112},{80,64},{96,80},{112,96},{1... | collective-permute-start | bytes 983048 | tf_op jit(solution)/shard_map/ppermute | solution.py:58
  82.5 6.6 %collective-permute-start.16 = (f32[8,256]{1,0:T(8,128)S(1)}, f32[8,256]{1,0:T(8,128)S(1)}, u32[]{:S(2)}, u32[]{:S(2)}) collective-permute-start(f32[8,256]{1,0:T(8,128)S(1)} %style.7), channel_id=1, source_target_pairs={{0,1},{1,0},{2,3},{3,2},{4,5},{5,4},{6,7},{7,6},{8,9},{9,8},{10,11... | collective-permute-start | bytes 24584 | tf_op jit(solution)/shard_map/ppermute | solution.py:38

commit v5 on v4

--- a/solution.py
+++ b/solution.py
@@ -63,7 +63,7 @@
         body,
         out_shape=outs,
         in_specs=in_specs,
-        out_specs=jax.tree.map(lambda _: out, outs),
+        out_specs=out if isinstance(out, tuple) else jax.tree.map(lambda _: out, outs),
         scratch_shapes=list(scratch),
         compiler_params=pltpu.CompilerParams(vmem_limit_bytes=vmem),
         cost_estimate=pl.CostEstimate(flops=flops, bytes_accessed=nbytes, transcendentals=0),
@@ -281,7 +281,7 @@
 
 def style_body(*refs):
     out = refs[-1]
-    zero, one, two, three = [take_row(ref.at[ref.shape[0] - 1]) for ref in refs[:-1]]
+    zero, one, two, three = [take_row(ref.at[ref.shape[0] - 1]) for ref in refs[:NX]]
     out[...] = jnp.broadcast_to((zero + two) + (one + three), out.shape)
 
 
@@ -292,10 +292,11 @@
 
 
 def banks_body(*refs):
-    out, both, sems = refs[-3:]
+    out, style, both, sems = refs[-4:]
     banks, taps, outs, channels = out.shape
+    style[...] = refs[0][0:1] + refs[1][0:1]
     pieces = []
-    for ref in refs[:-3]:
+    for ref in refs[2:-4]:
         if len(ref.shape) == 3:
             pieces.append(ref)
         else:
@@ -322,8 +323,9 @@
 
 def input_body(place, *refs, step=2):
     finals = refs[:NX]
-    low, high, cot, after, out, final, done, sems = refs[NX:]
+    low, high, cot, after, out, token, final, done, sems = refs[NX:]
     del after
+    token[...] = jnp.zeros(token.shape, F32)
     rows, width, channels = cot.shape
     x, z, core = place[0], place[1], place[2]
     for k in range(NX):
@@ -377,10 +379,9 @@
         rows_body,
         (shape((width, channels), BF16),) * 2,
         [HBM],
-        [dma((2, 2))],
+        [dma((2, 1))],
         nbytes=10**6,
         vmem=60 << 20,
-        out=HBM,
         name="rows",
     )(cot)
     count = lax.axis_size("tile")
@@ -388,7 +389,7 @@
     high = lax.ppermute(first, "tile", [(i + 1, i) for i in range(count - 1)])
 
     kernel, final = call(
-        mix_body, (shape(piece, F32), shape(piece, BF16)), [SMEM, VMEM, VMEM], flops=10**6, nbytes=10**6, name="mix"
+        mix_body, (shape(piece, F32), shape(piece, BF16)), [SMEM, VMEM, VMEM], flops=5*10**9, nbytes=10**6, name="mix"
     )(selection, style, jnp.transpose(bank, (0, 2, 1, 3)))
     final_z = swap_z(final)
     final_c = swap_core(final)
@@ -451,16 +452,14 @@
         name="kernels",
     )(style_row, final, final_c, final_z, final_cz)
     finals = [kernels] + [shift_x(kernels, k) for k in range(1, NX)]
-    style_part = call(style_body, shape((8, channels), F32), [VMEM] * NX, name="style")(*finals)
-    style_sum = style_part + swap_core(style_part)
 
     over_l = [flip_l(message, k) for k in range(1, NL)]
     ahead = call(ahead_body, shape((NL,) + message_of, BF16), [VMEM] * NL, name="ahead")(message, *over_l)
     over_y = [shift_y(ahead, k) for k in range(1, NY)]
 
-    input_grad = call(
+    input_grad, token = call(
         input_body,
-        shape((rows, width, channels), BF16),
+        (shape((rows, width, channels), BF16), shape((8, 128), F32)),
         [SMEM] + [VMEM] * (NX + 4),
         [
             pltpu.VMEM((3, channels, 3 * channels), BF16),
@@ -470,24 +469,25 @@
         flops=2 * 9 * rows * width * channels * channels,
         nbytes=4 * rows * width * channels,
         vmem=24 << 20,
-        out=HBM,
+        out=(HBM, VMEM),
         name="input",
     )(place, *finals, low, high, cot, ahead)
 
-    bank_grad = pl.pallas_call(
+    style_part = call(style_body, shape((8, channels), F32), [VMEM] * (NX + 1), name="style")(*finals, token)
+    bank_grad, style_grad = pl.pallas_call(
         banks_body,
-        out_shape=shape((banks,) + piece, F32),
-        in_specs=[VMEM] * NY,
-        out_specs=HBM,
+        out_shape=(shape((banks,) + piece, F32), shape((1, channels), F32)),
+        in_specs=[VMEM] * (NY + 2),
+        out_specs=(HBM, VMEM),
         scratch_shapes=[pltpu.VMEM((banks,) + piece, F32), dma((taps,))],
         compiler_params=pltpu.CompilerParams(vmem_limit_bytes=16 << 20),
         cost_estimate=pl.CostEstimate(flops=10**7, bytes_accessed=3 * 10**6, transcendentals=0),
         name="banks",
-    )(ahead, *over_y)
+    )(style_part, swap_core(style_part), ahead, *over_y)
 
     return (
         input_grad.reshape(feature_map.shape),
-        style_sum[:1],
+        style_grad,
         jnp.transpose(bank_grad, (0, 2, 1, 3)),
     )
 

time: 94.7 us -> 86.5 us (0.913)
  Pallas kernels: 26.8 us -> 20.1 us
  waiting for transfers between devices: 23 us -> 25.2 us
  starting transfers between devices: 40.4 us -> 38.2 us
  local copies, waits for them, and re-layouts: 2.66 us -> 1.61 us
    pallas_call x4, Pallas kernels: 16.8 us -> 10.1 us  [the longest x1 6.47 us: local(): call(input_body, (shape((rows, width, channels), BF16), shape((8, 128), F...]
    ppermute x3, starting transfers between devices: 5.67 us -> 3.99 us  [flip_l(): return lax.ppermute(a, 'img', img_perm(lambda l, y: (l ^ k, y)))]
    ppermute x3, waiting for transfers between devices: 5.11 us -> 6.69 us  [flip_l(): return lax.ppermute(a, 'img', img_perm(lambda l, y: (l ^ k, y)))]
    ppermute x2, starting transfers between devices: 15.7 us -> 14.4 us  [swap_z(): return lax.ppermute(a, 'tile', tile_perm(lambda x, z, c: (x, 1 - z, c)))]
    ppermute x3, waiting for transfers between devices: 3.49 us -> 2.27 us  [shift_y(): return lax.ppermute(a, 'img', img_perm(lambda l, y: (l, (y + k) % NY)))]
    ppermute x4, waiting for transfers between devices: 2.91 us -> 4.06 us  [swap_core(): return lax.ppermute(a, 'tile', tile_perm(lambda x, z, c: (x, z, 1 - c)))]
    unnamed x10, local copies, waits for them, and re-layouts: 2.66 us -> 1.61 us
  transfers between devices with their start and end apart: 20 -> 20, of which waited for: 9 -> 10; matrix products, arithmetic and copies ran while one was open for 1% -> 0% of each run, Pallas kernels for 14% -> 16%
where the time goes in v5:
time: 86.5 us; the launch traced here: 86.1 us
  starting transfers between devices  38.2 us (44%)
  waiting for transfers between devices  25.2 us (29%)
  Pallas kernels  20.1 us (23%)
  local copies, waits for them, and re-layouts  1.61 us (2%)
  between operations  0.98 us (1%)
    ppermute x2, starting transfers between devices, swap_z(): return lax.ppermute(a, 'tile', tile_perm(lambda x, z, c: (x, 1 - z, c)))  14.4 us
    ppermute x6, starting transfers between devices, shift_x(): lax.ppermute(a, 'tile', tile_perm(lambda x, z, c: ((x + k) % NX, z, c)))  11 us
    ppermute x2, waiting for transfers between devices, swap_z(): return lax.ppermute(a, 'tile', tile_perm(lambda x, z, c: (x, 1 - z, c)))  7.98 us
    ppermute x3, waiting for transfers between devices, flip_l(): return lax.ppermute(a, 'img', img_perm(lambda l, y: (l ^ k, y)))  6.69 us
    pallas_call x1, Pallas kernels, local(): call(input_body, (shape((rows, width, channels), BF16), shape((8, 128), F...  6.47 us
    pallas_call x1, Pallas kernels, local(): call(grad_body, (shape((taps, NC, groups, 16, channels), F32), shape((2,...  6.12 us
    ppermute x3, starting transfers between devices, shift_y(): return lax.ppermute(a, 'img', img_perm(lambda l, y: (l, (y + k) % NY)))  5 us
    ppermute x6, waiting for transfers between devices, shift_x(): lax.ppermute(a, 'tile', tile_perm(lambda x, z, c: ((x + k) % NX, z, c)))  4.18 us
  transfers between devices with their start and end apart: 20, of which 10 were waited for; matrix products, arithmetic and copies ran while one was open for 0% of the time, Pallas kernels for 16%

profile of v5, /device:TPU:8, one launch (start us, length us, event | category | flops | bytes accessed | tf_op | source)
XLA Modules:
  0.0 86.1 jit_solution(8189445048290519016)
XLA Ops:
  0.7 1.7 %rows.1 = (bf16[256,256]{1,0:T(8,128)(2,1)}, bf16[256,256]{1,0:T(8,128)(2,1)}) custom-call(bf16[16,256,256]{2,1,0:T(8,128)(2,1)} %bitcast.8), custom_call_target="tpu_custom_call" | custom-call | bytes 1000000 | tf_op jit(solution)/shard_map/rows/pallas_call | solution.py:378
  2.4 1.7 %collective-permute-start = (bf16[256,256]{1,0:T(8,128)(2,1)}, bf16[256,256]{1,0:T(8,128)(2,1)S(1)}, u32[]{:S(2)}, u32[]{:S(2)}) collective-permute-start(bf16[256,256]{1,0:T(8,128)(2,1)} %get-tuple-element.26), channel_id=1, source_target_pairs={{0,1},{1,2},{2,3},{3,4},{4,5},{5,6},{6,7},{7,8},{8,9},{9,10},{10,1... | collective-permute-start | bytes 393224 | tf_op jit(solution)/shard_map/ppermute | solution.py:388
  4.2 1.3 %collective-permute-start.1 = (bf16[256,256]{1,0:T(8,128)(2,1)}, bf16[256,256]{1,0:T(8,128)(2,1)S(1)}, u32[]{:S(2)}, u32[]{:S(2)}) collective-permute-start(bf16[256,256]{1,0:T(8,128)(2,1)} %get-tuple-element.27), channel_id=1, source_target_pairs={{1,0},{2,1},{3,2},{4,3},{5,4},{6,5},{7,6},{8,7},{9,8},{10,9},{11,1... | collective-permute-start | bytes 393224 | tf_op jit(solution)/shard_map/ppermute | solution.py:389
  5.5 0.8 mix.1
  6.3 13.7 %collective-permute-start.2 = (bf16[9,16,256]{2,1,0:T(8,128)(2,1)S(1)}, bf16[9,16,256]{2,1,0:T(8,128)(2,1)S(1)}, u32[]{:S(2)}, u32[]{:S(2)}) collective-permute-start(bf16[9,16,256]{2,1,0:T(8,128)(2,1)S(1)} %get-tuple-element.28.near.refs_0_), channel_id=1, source_target_pairs={{0,2},{1,3},{2,0},{3,1},{4,6},{5,7},{6,4},{7,5},{8,10},{9,11},{10,... | collective-permute-start | bytes 221192 | tf_op jit(solution)/shard_map/ppermute | solution.py:42
  20.0 1.6 %copy-done.3 = bf16[1,16,256,256]{3,2,1,0:T(8,128)(2,1)S(1)} copy-done((bf16[1,16,256,256]{3,2,1,0:T(8,128)(2,1)S(1)}, bf16[1,16,256,256]{3,2,1,0:T(8,128)(2,1)}, u32[]{:S(2)}) %copy-start.3) | copy-done | bytes 2097176
  21.6 6.1 %grad.1 = (f32[9,2,8,16,256]{4,3,2,1,0:T(8,128)S(1)}, bf16[2,256,256]{2,1,0:T(8,128)(2,1)S(1)}) custom-call(s32[3]{0:T(128)S(1)} %pad_add_fusion.place, bf16[16,256,256]{2,1,0:T(8,128)(2,1)S(1)} %bitcast.9, bf16[16,256,256]{2,1,0:T(8,128)(2,1)S(1)} %bitcast.11), custom_call_target="tpu_custom_call" | custom-call | flops 4831838208 | bytes 4194304 | tf_op jit(solution)/shard_map/grad/pallas_call | solution.py:398
  27.8 1.0 %edge.1 = (f32[8,9,16,256]{3,2,1,0:T(8,128)S(1)}, bf16[8,9,16,256]{3,2,1,0:T(8,128)(2,1)S(1)}) custom-call(s32[3]{0:T(128)S(1)} %pad_add_fusion.place, f32[9,2,8,16,256]{4,3,2,1,0:T(8,128)S(1)} %get-tuple-element.24.grad, bf16[2,256,256]{2,1,0:T(8,128)(2,1)S(1)} %get-tuple-element.25.ends, bf16[256,256]{1,0:T(8,128)(2,1)S(1)} %collective-permute-done.low.refs_4_, ...), custom_call_target="tpu_custom_call" | custom-call | flops 201326592 | bytes 4000000 | tf_op jit(solution)/shard_map/edge/pallas_call | solution.py:411
  28.9 2.0 %collective-permute-done.3.got = bf16[8,9,16,256]{3,2,1,0:T(8,128)(2,1)S(1)} collective-permute-done((bf16[8,9,16,256]{3,2,1,0:T(8,128)(2,1)S(1)}, bf16[8,9,16,256]{3,2,1,0:T(8,128)(2,1)S(1)}, u32[]{:S(2)}, u32[]{:S(2)}) %collective-permute-start.3) | collective-permute-done | bytes 589856 | tf_op jit(solution)/shard_map/ppermute | solution.py:38
  31.5 1.6 %collective-permute-start.4 = (bf16[2,9,16,256]{3,2,1,0:T(8,128)(2,1)S(1)}, bf16[2,9,16,256]{3,2,1,0:T(8,128)(2,1)S(1)}, u32[]{:S(2)}, u32[]{:S(2)}) collective-permute-start(bf16[2,9,16,256]{3,2,1,0:T(8,128)(2,1)S(1)} %get-tuple-element.32), channel_id=1, source_target_pairs={{0,4},{1,5},{2,6},{3,7},{4,8},{5,9},{6,10},{7,11},{8,12},{9,13},{1... | collective-permute-start | bytes 442376 | tf_op jit(solution)/shard_map/ppermute | solution.py:46
  33.1 2.7 %collective-permute-start.5 = (bf16[2,9,16,256]{3,2,1,0:T(8,128)(2,1)S(1)}, bf16[2,9,16,256]{3,2,1,0:T(8,128)(2,1)S(1)}, u32[]{:S(2)}, u32[]{:S(2)}) collective-permute-start(bf16[2,9,16,256]{3,2,1,0:T(8,128)(2,1)S(1)} %get-tuple-element.33), channel_id=1, source_target_pairs={{0,8},{1,9},{2,10},{3,11},{4,12},{5,13},{6,14},{7,15},{8,0},{9,1},... | collective-permute-start | bytes 442376 | tf_op jit(solution)/shard_map/ppermute | solution.py:46
  35.8 1.4 %collective-permute-start.6 = (bf16[2,9,16,256]{3,2,1,0:T(8,128)(2,1)S(1)}, bf16[2,9,16,256]{3,2,1,0:T(8,128)(2,1)S(1)}, u32[]{:S(2)}, u32[]{:S(2)}) collective-permute-start(bf16[2,9,16,256]{3,2,1,0:T(8,128)(2,1)S(1)} %get-tuple-element.34), channel_id=1, source_target_pairs={{0,12},{1,13},{2,14},{3,15},{4,0},{5,1},{6,2},{7,3},{8,4},{9,5},{1... | collective-permute-start | bytes 442376 | tf_op jit(solution)/shard_map/ppermute | solution.py:46
  37.8 0.8 collective-permute-done.7.after.refs_1_
  38.7 4.1 %collective-permute-done.5.two = bf16[2,9,16,256]{3,2,1,0:T(8,128)(2,1)S(1)} collective-permute-done((bf16[2,9,16,256]{3,2,1,0:T(8,128)(2,1)S(1)}, bf16[2,9,16,256]{3,2,1,0:T(8,128)(2,1)S(1)}, u32[]{:S(2)}, u32[]{:S(2)}) %collective-permute-start.5) | collective-permute-done | bytes 147488 | tf_op jit(solution)/shard_map/ppermute | solution.py:46
  43.6 0.8 collective-permute-start.9
  44.4 8.0 %collective-permute-done.9.got = bf16[10,16,256]{2,1,0:T(8,128)(2,1)S(1)} collective-permute-done((bf16[10,16,256]{2,1,0:T(8,128)(2,1)S(1)}, bf16[10,16,256]{2,1,0:T(8,128)(2,1)S(1)}, u32[]{:S(2)}, u32[]{:S(2)}) %collective-permute-start.9) | collective-permute-done | bytes 81952 | tf_op jit(solution)/shard_map/ppermute | solution.py:42
  53.1 1.6 %collective-permute-start.10 = (bf16[37,16,256]{2,1,0:T(8,128)(2,1)S(1)}, bf16[37,16,256]{2,1,0:T(8,128)(2,1)S(1)}, u32[]{:S(2)}, u32[]{:S(2)}) collective-permute-start(bf16[37,16,256]{2,1,0:T(8,128)(2,1)S(1)} %kernels.1.refs_0_), channel_id=1, source_target_pairs={{0,4},{1,5},{2,6},{3,7},{4,8},{5,9},{6,10},{7,11},{8,12},{9,13},{1... | collective-permute-start | bytes 909320 | tf_op jit(solution)/shard_map/ppermute | solution.py:46
  54.7 2.3 %collective-permute-start.11 = (bf16[37,16,256]{2,1,0:T(8,128)(2,1)S(1)}, bf16[37,16,256]{2,1,0:T(8,128)(2,1)S(1)}, u32[]{:S(2)}, u32[]{:S(2)}) collective-permute-start(bf16[37,16,256]{2,1,0:T(8,128)(2,1)S(1)} %kernels.1.refs_0_), channel_id=1, source_target_pairs={{0,8},{1,9},{2,10},{3,11},{4,12},{5,13},{6,14},{7,15},{8,0},{9,1},... | collective-permute-start | bytes 909320 | tf_op jit(solution)/shard_map/ppermute | solution.py:46
  57.0 1.3 %collective-permute-start.12 = (bf16[37,16,256]{2,1,0:T(8,128)(2,1)S(1)}, bf16[37,16,256]{2,1,0:T(8,128)(2,1)S(1)}, u32[]{:S(2)}, u32[]{:S(2)}) collective-permute-start(bf16[37,16,256]{2,1,0:T(8,128)(2,1)S(1)} %kernels.1.refs_0_), channel_id=1, source_target_pairs={{0,12},{1,13},{2,14},{3,15},{4,0},{5,1},{6,2},{7,3},{8,4},{9,5},{1... | collective-permute-start | bytes 909320 | tf_op jit(solution)/shard_map/ppermute | solution.py:46
  58.3 0.8 collective-permute-start.13
  59.1 1.5 %collective-permute-start.14 = (bf16[10,16,256]{2,1,0:T(8,128)(2,1)S(1)}, bf16[10,16,256]{2,1,0:T(8,128)(2,1)S(1)}, u32[]{:S(2)}, u32[]{:S(2)}) collective-permute-start(bf16[10,16,256]{2,1,0:T(8,128)(2,1)S(1)} %get-tuple-element.38.refs_0_), channel_id=1, source_target_pairs={{0,128},{16,144},{32,160},{48,176},{64,192},{80,208},{96,224},{112... | collective-permute-start | bytes 245768 | tf_op jit(solution)/shard_map/ppermute | solution.py:54
  60.6 2.2 %collective-permute-done.13.refs_1_ = bf16[10,16,256]{2,1,0:T(8,128)(2,1)S(1)} collective-permute-done((bf16[10,16,256]{2,1,0:T(8,128)(2,1)S(1)}, bf16[10,16,256]{2,1,0:T(8,128)(2,1)S(1)}, u32[]{:S(2)}, u32[]{:S(2)}) %collective-permute-start.13) | collective-permute-done | bytes 81952 | tf_op jit(solution)/shard_map/ppermute | solution.py:54
  62.8 1.7 %collective-permute-start.15 = (bf16[10,16,256]{2,1,0:T(8,128)(2,1)S(1)}, bf16[10,16,256]{2,1,0:T(8,128)(2,1)S(1)}, u32[]{:S(2)}, u32[]{:S(2)}) collective-permute-start(bf16[10,16,256]{2,1,0:T(8,128)(2,1)S(1)} %get-tuple-element.38.refs_0_), channel_id=1, source_target_pairs={{0,192},{16,208},{32,224},{48,240},{64,128},{80,144},{96,160},{112... | collective-permute-start | bytes 245768 | tf_op jit(solution)/shard_map/ppermute | solution.py:54
  64.5 1.6 %collective-permute-done.14.refs_2_ = bf16[10,16,256]{2,1,0:T(8,128)(2,1)S(1)} collective-permute-done((bf16[10,16,256]{2,1,0:T(8,128)(2,1)S(1)}, bf16[10,16,256]{2,1,0:T(8,128)(2,1)S(1)}, u32[]{:S(2)}, u32[]{:S(2)}) %collective-permute-start.14) | collective-permute-done | bytes 81952 | tf_op jit(solution)/shard_map/ppermute | solution.py:54
  66.1 2.9 %collective-permute-done.15.refs_3_ = bf16[10,16,256]{2,1,0:T(8,128)(2,1)S(1)} collective-permute-done((bf16[10,16,256]{2,1,0:T(8,128)(2,1)S(1)}, bf16[10,16,256]{2,1,0:T(8,128)(2,1)S(1)}, u32[]{:S(2)}, u32[]{:S(2)}) %collective-permute-start.15) | collective-permute-done | bytes 81952 | tf_op jit(solution)/shard_map/ppermute | solution.py:54
  69.1 1.7 %collective-permute-start.17 = (bf16[4,10,16,256]{3,2,1,0:T(8,128)(2,1)S(1)}, bf16[4,10,16,256]{3,2,1,0:T(8,128)(2,1)S(1)}, u32[]{:S(2)}, u32[]{:S(2)}) collective-permute-start(bf16[4,10,16,256]{3,2,1,0:T(8,128)(2,1)S(1)} %ahead.1.refs_7_.refs_2_), channel_id=1, source_target_pairs={{0,16},{16,32},{32,48},{48,0},{64,80},{80,96},{96,112},{112,64},{1... | collective-permute-start | bytes 983048 | tf_op jit(solution)/shard_map/ppermute | solution.py:58
  70.7 0.9 %collective-permute-start.18 = (bf16[4,10,16,256]{3,2,1,0:T(8,128)(2,1)S(1)}, bf16[4,10,16,256]{3,2,1,0:T(8,128)(2,1)S(1)}, u32[]{:S(2)}, u32[]{:S(2)}) collective-permute-start(bf16[4,10,16,256]{3,2,1,0:T(8,128)(2,1)S(1)} %ahead.1.refs_7_.refs_2_), channel_id=1, source_target_pairs={{0,32},{16,48},{32,0},{48,16},{64,96},{80,112},{96,64},{112,80},{1... | collective-permute-start | bytes 983048 | tf_op jit(solution)/shard_map/ppermute | solution.py:58
  71.6 2.4 %collective-permute-start.19 = (bf16[4,10,16,256]{3,2,1,0:T(8,128)(2,1)S(1)}, bf16[4,10,16,256]{3,2,1,0:T(8,128)(2,1)S(1)}, u32[]{:S(2)}, u32[]{:S(2)}) collective-permute-start(bf16[4,10,16,256]{3,2,1,0:T(8,128)(2,1)S(1)} %ahead.1.refs_7_.refs_2_), channel_id=1, source_target_pairs={{0,48},{16,0},{32,16},{48,32},{64,112},{80,64},{96,80},{112,96},{1... | collective-permute-start | bytes 983048 | tf_op jit(solution)/shard_map/ppermute | solution.py:58
  74.1 6.5 %input.1 = (bf16[16,256,256]{2,1,0:T(8,128)(2,1)}, f32[8,128]{1,0:T(8,128)S(1)}) custom-call(s32[3]{0:T(128)S(1)} %pad_add_fusion.place, bf16[37,16,256]{2,1,0:T(8,128)(2,1)S(1)} %kernels.1.refs_0_, bf16[37,16,256]{2,1,0:T(8,128)(2,1)S(1)} %collective-permute-done.10.refs_1_, bf16[37,16,256]{2,1,0:T(8,128)(2,1)S(1)} %collective-permute-done.11.refs_2_, ...), custom_call_target="tpu_custom_call" | custom-call | flops 4831838208 | bytes 4194304 | tf_op jit(solution)/shard_map/input/pallas_call | solution.py:460
  80.7 1.2 %collective-permute-done.16.refs_1_ = f32[8,256]{1,0:T(8,128)S(1)} collective-permute-done((f32[8,256]{1,0:T(8,128)S(1)}, f32[8,256]{1,0:T(8,128)S(1)}, u32[]{:S(2)}, u32[]{:S(2)}) %collective-permute-start.16) | collective-permute-done | bytes 8224 | tf_op jit(solution)/shard_map/ppermute | solution.py:38
  81.8 2.3 %collective-permute-done.19.refs_5_ = bf16[4,10,16,256]{3,2,1,0:T(8,128)(2,1)S(1)} collective-permute-done((bf16[4,10,16,256]{3,2,1,0:T(8,128)(2,1)S(1)}, bf16[4,10,16,256]{3,2,1,0:T(8,128)(2,1)S(1)}, u32[]{:S(2)}, u32[]{:S(2)}) %collective-permute-start.19) | collective-permute-done | bytes 327712 | tf_op jit(solution)/shard_map/ppermute | solution.py:58
  84.1 1.8 %banks.1 = (f32[8,9,16,256]{3,2,1,0:T(8,128)}, f32[1,256]{1,0:T(1,128)}) custom-call(f32[8,256]{1,0:T(8,128)S(1)} %style.7.refs_0_, f32[8,256]{1,0:T(8,128)S(1)} %collective-permute-done.16.refs_1_, bf16[4,10,16,256]{3,2,1,0:T(8,128)(2,1)S(1)} %ahead.1.refs_7_.refs_2_, bf16[4,10,16,256]{3,2,1,0:T(8,128)(2,1)S(1)} %collective-permute-done.17.refs_3_, ...), custom_call_target="tpu_custom_call" | custom-call | flops 10000000 | bytes 3000000 | tf_op jit(solution)/shard_map/banks/pallas_call | solution.py:477
  (31 shorter events, 3.1 us)
Async XLA Ops:
  0.6 4.8 %copy-start.2 = (s32[1,3]{1,0:T(1,128)S(1)}, s32[1,3]{1,0:T(1,128)}, u32[]{:S(2)}) copy-start(s32[1,3]{1,0:T(1,128)} %sel.3) | copy-start | bytes 40
  0.6 4.8 %copy-start.1 = (f32[1,256]{1,0:T(1,128)S(1)}, f32[1,256]{1,0:T(1,128)}, u32[]{:S(2)}) copy-start(f32[1,256]{1,0:T(1,128)} %style.6) | copy-start | bytes 3076
  0.7 4.8 %copy-start.4 = (bf16[8,16,9,256]{3,1,2,0:T(8,128)(2,1)S(1)}, bf16[8,16,9,256]{3,1,2,0:T(8,128)(2,1)}, u32[]{:S(2)}) copy-start(bf16[8,16,9,256]{3,1,2,0:T(8,128)(2,1)} %param.8) | copy-start | bytes 1769476
  2.4 25.4 %collective-permute-start = (bf16[256,256]{1,0:T(8,128)(2,1)}, bf16[256,256]{1,0:T(8,128)(2,1)S(1)}, u32[]{:S(2)}, u32[]{:S(2)}) collective-permute-start(bf16[256,256]{1,0:T(8,128)(2,1)} %get-tuple-element.26), channel_id=1, source_target_pairs={{0,1},{1,2},{2,3},{3,4},{4,5},{5,6},{6,7},{7,8},{8,9},{9,10},{10,1... | collective-permute-start | bytes 393224 | tf_op jit(solution)/shard_map/ppermute | solution.py:388
  4.2 23.6 %collective-permute-start.1 = (bf16[256,256]{1,0:T(8,128)(2,1)}, bf16[256,256]{1,0:T(8,128)(2,1)S(1)}, u32[]{:S(2)}, u32[]{:S(2)}) collective-permute-start(bf16[256,256]{1,0:T(8,128)(2,1)} %get-tuple-element.27), channel_id=1, source_target_pairs={{1,0},{2,1},{3,2},{4,3},{5,4},{6,5},{7,6},{8,7},{9,8},{10,9},{11,1... | collective-permute-start | bytes 393224 | tf_op jit(solution)/shard_map/ppermute | solution.py:389
  5.5 14.5 %copy-start = (bf16[1,16,256,256]{3,2,1,0:T(8,128)(2,1)S(1)}, bf16[1,16,256,256]{3,2,1,0:T(8,128)(2,1)}, u32[]{:S(2)}) copy-start(bf16[1,16,256,256]{3,2,1,0:T(8,128)(2,1)} %param.6) | copy-start | bytes 6291460
  6.3 21.5 %collective-permute-start.2 = (bf16[9,16,256]{2,1,0:T(8,128)(2,1)S(1)}, bf16[9,16,256]{2,1,0:T(8,128)(2,1)S(1)}, u32[]{:S(2)}, u32[]{:S(2)}) collective-permute-start(bf16[9,16,256]{2,1,0:T(8,128)(2,1)S(1)} %get-tuple-element.28.near.refs_0_), channel_id=1, source_target_pairs={{0,2},{1,3},{2,0},{3,1},{4,6},{5,7},{6,4},{7,5},{8,10},{9,11},{10,... | collective-permute-start | bytes 221192 | tf_op jit(solution)/shard_map/ppermute | solution.py:42
  20.0 1.6 %copy-start.3 = (bf16[1,16,256,256]{3,2,1,0:T(8,128)(2,1)S(1)}, bf16[1,16,256,256]{3,2,1,0:T(8,128)(2,1)}, u32[]{:S(2)}) copy-start(bf16[1,16,256,256]{3,2,1,0:T(8,128)(2,1)} %param.5) | copy-start | bytes 6291460
  28.8 2.1 %collective-permute-start.3 = (bf16[8,9,16,256]{3,2,1,0:T(8,128)(2,1)S(1)}, bf16[8,9,16,256]{3,2,1,0:T(8,128)(2,1)S(1)}, u32[]{:S(2)}, u32[]{:S(2)}) collective-permute-start(bf16[8,9,16,256]{3,2,1,0:T(8,128)(2,1)S(1)} %get-tuple-element.30), channel_id=1, source_target_pairs={{0,1},{1,0},{2,3},{3,2},{4,5},{5,4},{6,7},{7,6},{8,9},{9,8},{10,11... | collective-permute-start | bytes 1769480 | tf_op jit(solution)/shard_map/ppermute | solution.py:38
  31.5 7.2 %collective-permute-start.4 = (bf16[2,9,16,256]{3,2,1,0:T(8,128)(2,1)S(1)}, bf16[2,9,16,256]{3,2,1,0:T(8,128)(2,1)S(1)}, u32[]{:S(2)}, u32[]{:S(2)}) collective-permute-start(bf16[2,9,16,256]{3,2,1,0:T(8,128)(2,1)S(1)} %get-tuple-element.32), channel_id=1, source_target_pairs={{0,4},{1,5},{2,6},{3,7},{4,8},{5,9},{6,10},{7,11},{8,12},{9,13},{1... | collective-permute-start | bytes 442376 | tf_op jit(solution)/shard_map/ppermute | solution.py:46
  33.1 9.8 %collective-permute-start.5 = (bf16[2,9,16,256]{3,2,1,0:T(8,128)(2,1)S(1)}, bf16[2,9,16,256]{3,2,1,0:T(8,128)(2,1)S(1)}, u32[]{:S(2)}, u32[]{:S(2)}) collective-permute-start(bf16[2,9,16,256]{3,2,1,0:T(8,128)(2,1)S(1)} %get-tuple-element.33), channel_id=1, source_target_pairs={{0,8},{1,9},{2,10},{3,11},{4,12},{5,13},{6,14},{7,15},{8,0},{9,1},... | collective-permute-start | bytes 442376 | tf_op jit(solution)/shard_map/ppermute | solution.py:46
  35.8 7.0 %collective-permute-start.6 = (bf16[2,9,16,256]{3,2,1,0:T(8,128)(2,1)S(1)}, bf16[2,9,16,256]{3,2,1,0:T(8,128)(2,1)S(1)}, u32[]{:S(2)}, u32[]{:S(2)}) collective-permute-start(bf16[2,9,16,256]{3,2,1,0:T(8,128)(2,1)S(1)} %get-tuple-element.34), channel_id=1, source_target_pairs={{0,12},{1,13},{2,14},{3,15},{4,0},{5,1},{6,2},{7,3},{8,4},{9,5},{1... | collective-permute-start | bytes 442376 | tf_op jit(solution)/shard_map/ppermute | solution.py:46
  37.3 1.3 %collective-permute-start.7 = (bf16[9,16,256]{2,1,0:T(8,128)(2,1)S(1)}, bf16[9,16,256]{2,1,0:T(8,128)(2,1)S(1)}, u32[]{:S(2)}, u32[]{:S(2)}) collective-permute-start(bf16[9,16,256]{2,1,0:T(8,128)(2,1)S(1)} %get-tuple-element.28.near.refs_0_), channel_id=1, source_target_pairs={{0,1},{1,0},{2,3},{3,2},{4,5},{5,4},{6,7},{7,6},{8,9},{9,8},{10,11... | collective-permute-start | bytes 221192 | tf_op jit(solution)/shard_map/ppermute | solution.py:38
  37.3 1.4 %collective-permute-start.8 = (bf16[9,16,256]{2,1,0:T(8,128)(2,1)S(1)}, bf16[9,16,256]{2,1,0:T(8,128)(2,1)S(1)}, u32[]{:S(2)}, u32[]{:S(2)}) collective-permute-start(bf16[9,16,256]{2,1,0:T(8,128)(2,1)S(1)} %collective-permute-done.2.after.got.refs_2_), channel_id=1, source_target_pairs={{0,1},{1,0},{2,3},{3,2},{4,5},{5,4},{6,7},{7,6},{8,9},{9,8},{10,11... | collective-permute-start | bytes 221192 | tf_op jit(solution)/shard_map/ppermute | solution.py:38
  43.6 8.7 %collective-permute-start.9 = (bf16[10,16,256]{2,1,0:T(8,128)(2,1)S(1)}, bf16[10,16,256]{2,1,0:T(8,128)(2,1)S(1)}, u32[]{:S(2)}, u32[]{:S(2)}) collective-permute-start(bf16[10,16,256]{2,1,0:T(8,128)(2,1)S(1)} %get-tuple-element.36.sent), channel_id=1, source_target_pairs={{0,2},{1,3},{2,0},{3,1},{4,6},{5,7},{6,4},{7,5},{8,10},{9,11},{10,... | collective-permute-start | bytes 245768 | tf_op jit(solution)/shard_map/ppermute | solution.py:42
  53.1 18.6 %collective-permute-start.10 = (bf16[37,16,256]{2,1,0:T(8,128)(2,1)S(1)}, bf16[37,16,256]{2,1,0:T(8,128)(2,1)S(1)}, u32[]{:S(2)}, u32[]{:S(2)}) collective-permute-start(bf16[37,16,256]{2,1,0:T(8,128)(2,1)S(1)} %kernels.1.refs_0_), channel_id=1, source_target_pairs={{0,4},{1,5},{2,6},{3,7},{4,8},{5,9},{6,10},{7,11},{8,12},{9,13},{1... | collective-permute-start | bytes 909320 | tf_op jit(solution)/shard_map/ppermute | solution.py:46
  54.7 19.3 %collective-permute-start.11 = (bf16[37,16,256]{2,1,0:T(8,128)(2,1)S(1)}, bf16[37,16,256]{2,1,0:T(8,128)(2,1)S(1)}, u32[]{:S(2)}, u32[]{:S(2)}) collective-permute-start(bf16[37,16,256]{2,1,0:T(8,128)(2,1)S(1)} %kernels.1.refs_0_), channel_id=1, source_target_pairs={{0,8},{1,9},{2,10},{3,11},{4,12},{5,13},{6,14},{7,15},{8,0},{9,1},... | collective-permute-start | bytes 909320 | tf_op jit(solution)/shard_map/ppermute | solution.py:46
  57.0 17.1 %collective-permute-start.12 = (bf16[37,16,256]{2,1,0:T(8,128)(2,1)S(1)}, bf16[37,16,256]{2,1,0:T(8,128)(2,1)S(1)}, u32[]{:S(2)}, u32[]{:S(2)}) collective-permute-start(bf16[37,16,256]{2,1,0:T(8,128)(2,1)S(1)} %kernels.1.refs_0_), channel_id=1, source_target_pairs={{0,12},{1,13},{2,14},{3,15},{4,0},{5,1},{6,2},{7,3},{8,4},{9,5},{1... | collective-permute-start | bytes 909320 | tf_op jit(solution)/shard_map/ppermute | solution.py:46
  58.3 4.4 %collective-permute-start.13 = (bf16[10,16,256]{2,1,0:T(8,128)(2,1)S(1)}, bf16[10,16,256]{2,1,0:T(8,128)(2,1)S(1)}, u32[]{:S(2)}, u32[]{:S(2)}) collective-permute-start(bf16[10,16,256]{2,1,0:T(8,128)(2,1)S(1)} %get-tuple-element.38.refs_0_), channel_id=1, source_target_pairs={{0,64},{16,80},{32,96},{48,112},{64,0},{80,16},{96,32},{112,48},{1... | collective-permute-start | bytes 245768 | tf_op jit(solution)/shard_map/ppermute | solution.py:54
  59.1 7.0 %collective-permute-start.14 = (bf16[10,16,256]{2,1,0:T(8,128)(2,1)S(1)}, bf16[10,16,256]{2,1,0:T(8,128)(2,1)S(1)}, u32[]{:S(2)}, u32[]{:S(2)}) collective-permute-start(bf16[10,16,256]{2,1,0:T(8,128)(2,1)S(1)} %get-tuple-element.38.refs_0_), channel_id=1, source_target_pairs={{0,128},{16,144},{32,160},{48,176},{64,192},{80,208},{96,224},{112... | collective-permute-start | bytes 245768 | tf_op jit(solution)/shard_map/ppermute | solution.py:54
  62.8 6.2 %collective-permute-start.15 = (bf16[10,16,256]{2,1,0:T(8,128)(2,1)S(1)}, bf16[10,16,256]{2,1,0:T(8,128)(2,1)S(1)}, u32[]{:S(2)}, u32[]{:S(2)}) collective-permute-start(bf16[10,16,256]{2,1,0:T(8,128)(2,1)S(1)} %get-tuple-element.38.refs_0_), channel_id=1, source_target_pairs={{0,192},{16,208},{32,224},{48,240},{64,128},{80,144},{96,160},{112... | collective-permute-start | bytes 245768 | tf_op jit(solution)/shard_map/ppermute | solution.py:54
  69.1 12.8 %collective-permute-start.17 = (bf16[4,10,16,256]{3,2,1,0:T(8,128)(2,1)S(1)}, bf16[4,10,16,256]{3,2,1,0:T(8,128)(2,1)S(1)}, u32[]{:S(2)}, u32[]{:S(2)}) collective-permute-start(bf16[4,10,16,256]{3,2,1,0:T(8,128)(2,1)S(1)} %ahead.1.refs_7_.refs_2_), channel_id=1, source_target_pairs={{0,16},{16,32},{32,48},{48,0},{64,80},{80,96},{96,112},{112,64},{1... | collective-permute-start | bytes 983048 | tf_op jit(solution)/shard_map/ppermute | solution.py:58
  70.7 11.1 %collective-permute-start.18 = (bf16[4,10,16,256]{3,2,1,0:T(8,128)(2,1)S(1)}, bf16[4,10,16,256]{3,2,1,0:T(8,128)(2,1)S(1)}, u32[]{:S(2)}, u32[]{:S(2)}) collective-permute-start(bf16[4,10,16,256]{3,2,1,0:T(8,128)(2,1)S(1)} %ahead.1.refs_7_.refs_2_), channel_id=1, source_target_pairs={{0,32},{16,48},{32,0},{48,16},{64,96},{80,112},{96,64},{112,80},{1... | collective-permute-start | bytes 983048 | tf_op jit(solution)/shard_map/ppermute | solution.py:58
  71.6 12.4 %collective-permute-start.19 = (bf16[4,10,16,256]{3,2,1,0:T(8,128)(2,1)S(1)}, bf16[4,10,16,256]{3,2,1,0:T(8,128)(2,1)S(1)}, u32[]{:S(2)}, u32[]{:S(2)}) collective-permute-start(bf16[4,10,16,256]{3,2,1,0:T(8,128)(2,1)S(1)} %ahead.1.refs_7_.refs_2_), channel_id=1, source_target_pairs={{0,48},{16,0},{32,16},{48,32},{64,112},{80,64},{96,80},{112,96},{1... | collective-permute-start | bytes 983048 | tf_op jit(solution)/shard_map/ppermute | solution.py:58
  80.6 1.3 %collective-permute-start.16 = (f32[8,256]{1,0:T(8,128)S(1)}, f32[8,256]{1,0:T(8,128)S(1)}, u32[]{:S(2)}, u32[]{:S(2)}) collective-permute-start(f32[8,256]{1,0:T(8,128)S(1)} %style.7.refs_0_), channel_id=1, source_target_pairs={{0,1},{1,0},{2,3},{3,2},{4,5},{5,4},{6,7},{7,6},{8,9},{9,8},{10,11... | collective-permute-start | bytes 24584 | tf_op jit(solution)/shard_map/ppermute | solution.py:38

commit v6 on v5

--- a/solution.py
+++ b/solution.py
@@ -56,6 +56,10 @@
 
 def shift_y(a, k):
     return lax.ppermute(a, "img", img_perm(lambda l, y: (l, (y + k) % NY)))
+
+
+def two_first(shift, one, two, three):
+    return [shift(two, 2), shift(one, 1), shift(three, 3)]
 
 
 def call(body, outs, in_specs, scratch=(), flops=0, nbytes=0, vmem=16 << 20, out=VMEM, name=None):
@@ -224,7 +228,7 @@
     return (rows[0:1] + rows[1:2]) + rows[2:3]
 
 
-def split_z_body(place, style, mine, one, two, three, near, got, after, after_too, total, other):
+def split_z_body(place, style, mine, two, one, three, near, got, after, after_too, total, other):
     del after, after_too
     taps, outs, channels = total.shape
     z = place[1]
@@ -281,7 +285,7 @@
 
 def style_body(*refs):
     out = refs[-1]
-    zero, one, two, three = [take_row(ref.at[ref.shape[0] - 1]) for ref in refs[:NX]]
+    zero, two, one, three = [take_row(ref.at[ref.shape[0] - 1]) for ref in refs[:NX]]
     out[...] = jnp.broadcast_to((zero + two) + (one + three), out.shape)
 
 
@@ -292,11 +296,10 @@
 
 
 def banks_body(*refs):
-    out, style, both, sems = refs[-4:]
+    out, both, sems = refs[-3:]
     banks, taps, outs, channels = out.shape
-    style[...] = refs[0][0:1] + refs[1][0:1]
     pieces = []
-    for ref in refs[2:-4]:
+    for ref in refs[:-3]:
         if len(ref.shape) == 3:
             pieces.append(ref)
         else:
@@ -331,7 +334,7 @@
     for k in range(NX):
         for n in range(NZ):
             for c in range(NC):
-                at = (lax.rem(x + NX - k, NX) * NZ + (z ^ n)) * NC + (core ^ c)
+                at = (lax.rem(x + NX - (0, 2, 1, 3)[k], NX) * NZ + (z ^ n)) * NC + (core ^ c)
                 here = pl.ds(pl.multiple_of(at * 16, 16), 16)
                 for t in range(9):
                     u, v = t // 3, t % 3
@@ -426,6 +429,7 @@
         nbytes=3 * 10**6,
         name="split_x",
     )(place, mine, swap_core(theirs))
+    x_got = two_first(shift_x, one, two, three)
     total, other = call(
         split_z_body,
         (shape(piece, F32), shape(message_of, BF16)),
@@ -433,7 +437,7 @@
         flops=10**6,
         nbytes=10**6,
         name="split_z",
-    )(place, style, own_x, shift_x(one, 1), shift_x(two, 2), shift_x(three, 3), final, final_z, final_c, final_cz)
+    )(place, style, own_x, *x_got, final, final_z, final_c, final_cz)
     message, style_row = call(
         owner_body,
         (shape(message_of, BF16), shape((8, channels), F32)),
@@ -451,11 +455,11 @@
         nbytes=10**7,
         name="kernels",
     )(style_row, final, final_c, final_z, final_cz)
-    finals = [kernels] + [shift_x(kernels, k) for k in range(1, NX)]
+    finals = [kernels] + two_first(shift_x, kernels, kernels, kernels)
 
     over_l = [flip_l(message, k) for k in range(1, NL)]
     ahead = call(ahead_body, shape((NL,) + message_of, BF16), [VMEM] * NL, name="ahead")(message, *over_l)
-    over_y = [shift_y(ahead, k) for k in range(1, NY)]
+    over_y = two_first(shift_y, ahead, ahead, ahead)
 
     input_grad, token = call(
         input_body,
@@ -474,16 +478,17 @@
     )(place, *finals, low, high, cot, ahead)
 
     style_part = call(style_body, shape((8, channels), F32), [VMEM] * (NX + 1), name="style")(*finals, token)
-    bank_grad, style_grad = pl.pallas_call(
+    style_grad = (style_part + swap_core(style_part))[:1]
+    bank_grad = pl.pallas_call(
         banks_body,
-        out_shape=(shape((banks,) + piece, F32), shape((1, channels), F32)),
-        in_specs=[VMEM] * (NY + 2),
-        out_specs=(HBM, VMEM),
+        out_shape=shape((banks,) + piece, F32),
+        in_specs=[VMEM] * NY,
+        out_specs=HBM,
         scratch_shapes=[pltpu.VMEM((banks,) + piece, F32), dma((taps,))],
         compiler_params=pltpu.CompilerParams(vmem_limit_bytes=16 << 20),
         cost_estimate=pl.CostEstimate(flops=10**7, bytes_accessed=3 * 10**6, transcendentals=0),
         name="banks",
-    )(style_part, swap_core(style_part), ahead, *over_y)
+    )(ahead, *over_y)
 
     return (
         input_grad.reshape(feature_map.shape),

time: 86.5 us -> 86.2 us (level); the launches traced: 86.1 us -> 84.6 us
  waiting for transfers between devices: 25.2 us -> 23.2 us
    ppermute x6, waiting for transfers between devices: 4.18 us -> 2.96 us  [shift_x(): lax.ppermute(a, 'tile', tile_perm(lambda x, z, c: ((x + k) % NX, z, c)))]
  transfers between devices with their start and end apart: 20 -> 20, of which waited for: 10 -> 11; matrix products, arithmetic and copies ran while one was open for 0% -> 1% of each run, Pallas kernels for 16% -> 16%
where the time goes in v6:
time: 86.2 us; the launch traced here: 84.6 us
  starting transfers between devices  38.7 us (45%)
  waiting for transfers between devices  23.2 us (27%)
  Pallas kernels  19.5 us (23%)
  local copies, waits for them, and re-layouts  1.61 us (2%)
  between operations  0.98 us (1%)
    ppermute x2, starting transfers between devices, swap_z(): return lax.ppermute(a, 'tile', tile_perm(lambda x, z, c: (x, 1 - z, c)))  14.7 us
    ppermute x6, starting transfers between devices, shift_x(): lax.ppermute(a, 'tile', tile_perm(lambda x, z, c: ((x + k) % NX, z, c)))  11.7 us
    ppermute x2, waiting for transfers between devices, swap_z(): return lax.ppermute(a, 'tile', tile_perm(lambda x, z, c: (x, 1 - z, c)))  7.79 us
    ppermute x3, waiting for transfers between devices, flip_l(): return lax.ppermute(a, 'img', img_perm(lambda l, y: (l ^ k, y)))  6.51 us
    pallas_call x1, Pallas kernels, local(): call(input_body, (shape((rows, width, channels), BF16), shape((8, 128), F...  6.47 us
    pallas_call x1, Pallas kernels, local(): call(grad_body, (shape((taps, NC, groups, 16, channels), F32), shape((2,...  6.12 us
    ppermute x3, starting transfers between devices, shift_y(): return lax.ppermute(a, 'img', img_perm(lambda l, y: (l, (y + k) % NY)))  4.41 us
    ppermute x3, starting transfers between devices, flip_l(): return lax.ppermute(a, 'img', img_perm(lambda l, y: (l ^ k, y)))  4.17 us
  transfers between devices with their start and end apart: 20, of which 11 were waited for; matrix products, arithmetic and copies ran while one was open for 1% of the time, Pallas kernels for 16%

profile of v6, /device:TPU:8, one launch (start us, length us, event | category | flops | bytes accessed | tf_op | source)
XLA Modules:
  0.0 84.6 jit_solution(3275785078949524527)
XLA Ops:
  0.7 1.7 %rows.1 = (bf16[256,256]{1,0:T(8,128)(2,1)}, bf16[256,256]{1,0:T(8,128)(2,1)}) custom-call(bf16[16,256,256]{2,1,0:T(8,128)(2,1)} %bitcast.8), custom_call_target="tpu_custom_call" | custom-call | bytes 1000000 | tf_op jit(solution)/shard_map/rows/pallas_call | solution.py:381
  2.4 1.7 %collective-permute-start = (bf16[256,256]{1,0:T(8,128)(2,1)}, bf16[256,256]{1,0:T(8,128)(2,1)S(1)}, u32[]{:S(2)}, u32[]{:S(2)}) collective-permute-start(bf16[256,256]{1,0:T(8,128)(2,1)} %get-tuple-element.24), channel_id=1, source_target_pairs={{0,1},{1,2},{2,3},{3,4},{4,5},{5,6},{6,7},{7,8},{8,9},{9,10},{10,1... | collective-permute-start | bytes 393224 | tf_op jit(solution)/shard_map/ppermute | solution.py:391
  4.2 1.3 %collective-permute-start.1 = (bf16[256,256]{1,0:T(8,128)(2,1)}, bf16[256,256]{1,0:T(8,128)(2,1)S(1)}, u32[]{:S(2)}, u32[]{:S(2)}) collective-permute-start(bf16[256,256]{1,0:T(8,128)(2,1)} %get-tuple-element.25), channel_id=1, source_target_pairs={{1,0},{2,1},{3,2},{4,3},{5,4},{6,5},{7,6},{8,7},{9,8},{10,9},{11,1... | collective-permute-start | bytes 393224 | tf_op jit(solution)/shard_map/ppermute | solution.py:392
  5.5 0.8 mix.1
  6.3 13.7 %collective-permute-start.2 = (bf16[9,16,256]{2,1,0:T(8,128)(2,1)S(1)}, bf16[9,16,256]{2,1,0:T(8,128)(2,1)S(1)}, u32[]{:S(2)}, u32[]{:S(2)}) collective-permute-start(bf16[9,16,256]{2,1,0:T(8,128)(2,1)S(1)} %get-tuple-element.26.near.refs_0_), channel_id=1, source_target_pairs={{0,2},{1,3},{2,0},{3,1},{4,6},{5,7},{6,4},{7,5},{8,10},{9,11},{10,... | collective-permute-start | bytes 221192 | tf_op jit(solution)/shard_map/ppermute | solution.py:42
  20.0 1.6 %copy-done.3 = bf16[1,16,256,256]{3,2,1,0:T(8,128)(2,1)S(1)} copy-done((bf16[1,16,256,256]{3,2,1,0:T(8,128)(2,1)S(1)}, bf16[1,16,256,256]{3,2,1,0:T(8,128)(2,1)}, u32[]{:S(2)}) %copy-start.3) | copy-done | bytes 2097176
  21.6 6.1 %grad.1 = (f32[9,2,8,16,256]{4,3,2,1,0:T(8,128)S(1)}, bf16[2,256,256]{2,1,0:T(8,128)(2,1)S(1)}) custom-call(s32[3]{0:T(128)S(1)} %pad_add_fusion.place, bf16[16,256,256]{2,1,0:T(8,128)(2,1)S(1)} %bitcast.9, bf16[16,256,256]{2,1,0:T(8,128)(2,1)S(1)} %bitcast.11), custom_call_target="tpu_custom_call" | custom-call | flops 4831838208 | bytes 4194304 | tf_op jit(solution)/shard_map/grad/pallas_call | solution.py:401
  27.8 1.0 %edge.1 = (f32[8,9,16,256]{3,2,1,0:T(8,128)S(1)}, bf16[8,9,16,256]{3,2,1,0:T(8,128)(2,1)S(1)}) custom-call(s32[3]{0:T(128)S(1)} %pad_add_fusion.place, f32[9,2,8,16,256]{4,3,2,1,0:T(8,128)S(1)} %get-tuple-element.22.grad, bf16[2,256,256]{2,1,0:T(8,128)(2,1)S(1)} %get-tuple-element.23.ends, bf16[256,256]{1,0:T(8,128)(2,1)S(1)} %collective-permute-done.low.refs_4_, ...), custom_call_target="tpu_custom_call" | custom-call | flops 201326592 | bytes 4000000 | tf_op jit(solution)/shard_map/edge/pallas_call | solution.py:414
  28.9 2.0 %collective-permute-done.3.got = bf16[8,9,16,256]{3,2,1,0:T(8,128)(2,1)S(1)} collective-permute-done((bf16[8,9,16,256]{3,2,1,0:T(8,128)(2,1)S(1)}, bf16[8,9,16,256]{3,2,1,0:T(8,128)(2,1)S(1)}, u32[]{:S(2)}, u32[]{:S(2)}) %collective-permute-start.3) | collective-permute-done | bytes 589856 | tf_op jit(solution)/shard_map/ppermute | solution.py:38
  31.5 3.1 %collective-permute-start.4 = (bf16[2,9,16,256]{3,2,1,0:T(8,128)(2,1)S(1)}, bf16[2,9,16,256]{3,2,1,0:T(8,128)(2,1)S(1)}, u32[]{:S(2)}, u32[]{:S(2)}) collective-permute-start(bf16[2,9,16,256]{3,2,1,0:T(8,128)(2,1)S(1)} %get-tuple-element.30), channel_id=1, source_target_pairs={{0,8},{1,9},{2,10},{3,11},{4,12},{5,13},{6,14},{7,15},{8,0},{9,1},... | collective-permute-start | bytes 442376 | tf_op jit(solution)/shard_map/ppermute | solution.py:46
  35.2 2.6 %collective-permute-start.6 = (bf16[2,9,16,256]{3,2,1,0:T(8,128)(2,1)S(1)}, bf16[2,9,16,256]{3,2,1,0:T(8,128)(2,1)S(1)}, u32[]{:S(2)}, u32[]{:S(2)}) collective-permute-start(bf16[2,9,16,256]{3,2,1,0:T(8,128)(2,1)S(1)} %get-tuple-element.32), channel_id=1, source_target_pairs={{0,12},{1,13},{2,14},{3,15},{4,0},{5,1},{6,2},{7,3},{8,4},{9,5},{1... | collective-permute-start | bytes 442376 | tf_op jit(solution)/shard_map/ppermute | solution.py:46
  38.4 0.8 collective-permute-done.7.after.refs_1_
  39.8 2.4 %collective-permute-done.5.one = bf16[2,9,16,256]{3,2,1,0:T(8,128)(2,1)S(1)} collective-permute-done((bf16[2,9,16,256]{3,2,1,0:T(8,128)(2,1)S(1)}, bf16[2,9,16,256]{3,2,1,0:T(8,128)(2,1)S(1)}, u32[]{:S(2)}, u32[]{:S(2)}) %collective-permute-start.5) | collective-permute-done | bytes 147488 | tf_op jit(solution)/shard_map/ppermute | solution.py:46
  42.3 0.7 split_z.1
  43.0 1.0 %collective-permute-start.9 = (bf16[10,16,256]{2,1,0:T(8,128)(2,1)S(1)}, bf16[10,16,256]{2,1,0:T(8,128)(2,1)S(1)}, u32[]{:S(2)}, u32[]{:S(2)}) collective-permute-start(bf16[10,16,256]{2,1,0:T(8,128)(2,1)S(1)} %get-tuple-element.34.sent), channel_id=1, source_target_pairs={{0,2},{1,3},{2,0},{3,1},{4,6},{5,7},{6,4},{7,5},{8,10},{9,11},{10,... | collective-permute-start | bytes 245768 | tf_op jit(solution)/shard_map/ppermute | solution.py:42
  44.0 7.8 %collective-permute-done.9.got = bf16[10,16,256]{2,1,0:T(8,128)(2,1)S(1)} collective-permute-done((bf16[10,16,256]{2,1,0:T(8,128)(2,1)S(1)}, bf16[10,16,256]{2,1,0:T(8,128)(2,1)S(1)}, u32[]{:S(2)}, u32[]{:S(2)}) %collective-permute-start.9) | collective-permute-done | bytes 81952 | tf_op jit(solution)/shard_map/ppermute | solution.py:42
  51.8 0.7 owner.1
  52.5 2.1 %collective-permute-start.10 = (bf16[37,16,256]{2,1,0:T(8,128)(2,1)S(1)}, bf16[37,16,256]{2,1,0:T(8,128)(2,1)S(1)}, u32[]{:S(2)}, u32[]{:S(2)}) collective-permute-start(bf16[37,16,256]{2,1,0:T(8,128)(2,1)S(1)} %kernels.1.refs_0_), channel_id=1, source_target_pairs={{0,8},{1,9},{2,10},{3,11},{4,12},{5,13},{6,14},{7,15},{8,0},{9,1},... | collective-permute-start | bytes 909320 | tf_op jit(solution)/shard_map/ppermute | solution.py:46
  54.6 1.6 %collective-permute-start.11 = (bf16[37,16,256]{2,1,0:T(8,128)(2,1)S(1)}, bf16[37,16,256]{2,1,0:T(8,128)(2,1)S(1)}, u32[]{:S(2)}, u32[]{:S(2)}) collective-permute-start(bf16[37,16,256]{2,1,0:T(8,128)(2,1)S(1)} %kernels.1.refs_0_), channel_id=1, source_target_pairs={{0,4},{1,5},{2,6},{3,7},{4,8},{5,9},{6,10},{7,11},{8,12},{9,13},{1... | collective-permute-start | bytes 909320 | tf_op jit(solution)/shard_map/ppermute | solution.py:46
  56.2 1.6 %collective-permute-start.12 = (bf16[37,16,256]{2,1,0:T(8,128)(2,1)S(1)}, bf16[37,16,256]{2,1,0:T(8,128)(2,1)S(1)}, u32[]{:S(2)}, u32[]{:S(2)}) collective-permute-start(bf16[37,16,256]{2,1,0:T(8,128)(2,1)S(1)} %kernels.1.refs_0_), channel_id=1, source_target_pairs={{0,12},{1,13},{2,14},{3,15},{4,0},{5,1},{6,2},{7,3},{8,4},{9,5},{1... | collective-permute-start | bytes 909320 | tf_op jit(solution)/shard_map/ppermute | solution.py:46
  57.9 0.9 %collective-permute-start.13 = (bf16[10,16,256]{2,1,0:T(8,128)(2,1)S(1)}, bf16[10,16,256]{2,1,0:T(8,128)(2,1)S(1)}, u32[]{:S(2)}, u32[]{:S(2)}) collective-permute-start(bf16[10,16,256]{2,1,0:T(8,128)(2,1)S(1)} %get-tuple-element.36.refs_0_), channel_id=1, source_target_pairs={{0,64},{16,80},{32,96},{48,112},{64,0},{80,16},{96,32},{112,48},{1... | collective-permute-start | bytes 245768 | tf_op jit(solution)/shard_map/ppermute | solution.py:54
  58.8 1.4 %collective-permute-start.14 = (bf16[10,16,256]{2,1,0:T(8,128)(2,1)S(1)}, bf16[10,16,256]{2,1,0:T(8,128)(2,1)S(1)}, u32[]{:S(2)}, u32[]{:S(2)}) collective-permute-start(bf16[10,16,256]{2,1,0:T(8,128)(2,1)S(1)} %get-tuple-element.36.refs_0_), channel_id=1, source_target_pairs={{0,128},{16,144},{32,160},{48,176},{64,192},{80,208},{96,224},{112... | collective-permute-start | bytes 245768 | tf_op jit(solution)/shard_map/ppermute | solution.py:54
  60.2 2.1 %collective-permute-done.13.refs_1_ = bf16[10,16,256]{2,1,0:T(8,128)(2,1)S(1)} collective-permute-done((bf16[10,16,256]{2,1,0:T(8,128)(2,1)S(1)}, bf16[10,16,256]{2,1,0:T(8,128)(2,1)S(1)}, u32[]{:S(2)}, u32[]{:S(2)}) %collective-permute-start.13) | collective-permute-done | bytes 81952 | tf_op jit(solution)/shard_map/ppermute | solution.py:54
  62.3 1.8 %collective-permute-start.15 = (bf16[10,16,256]{2,1,0:T(8,128)(2,1)S(1)}, bf16[10,16,256]{2,1,0:T(8,128)(2,1)S(1)}, u32[]{:S(2)}, u32[]{:S(2)}) collective-permute-start(bf16[10,16,256]{2,1,0:T(8,128)(2,1)S(1)} %get-tuple-element.36.refs_0_), channel_id=1, source_target_pairs={{0,192},{16,208},{32,224},{48,240},{64,128},{80,144},{96,160},{112... | collective-permute-start | bytes 245768 | tf_op jit(solution)/shard_map/ppermute | solution.py:54
  64.1 1.7 %collective-permute-done.14.refs_2_ = bf16[10,16,256]{2,1,0:T(8,128)(2,1)S(1)} collective-permute-done((bf16[10,16,256]{2,1,0:T(8,128)(2,1)S(1)}, bf16[10,16,256]{2,1,0:T(8,128)(2,1)S(1)}, u32[]{:S(2)}, u32[]{:S(2)}) %collective-permute-start.14) | collective-permute-done | bytes 81952 | tf_op jit(solution)/shard_map/ppermute | solution.py:54
  65.8 2.7 %collective-permute-done.15.refs_3_ = bf16[10,16,256]{2,1,0:T(8,128)(2,1)S(1)} collective-permute-done((bf16[10,16,256]{2,1,0:T(8,128)(2,1)S(1)}, bf16[10,16,256]{2,1,0:T(8,128)(2,1)S(1)}, u32[]{:S(2)}, u32[]{:S(2)}) %collective-permute-start.15) | collective-permute-done | bytes 81952 | tf_op jit(solution)/shard_map/ppermute | solution.py:54
  68.6 2.4 %collective-permute-start.17 = (bf16[4,10,16,256]{3,2,1,0:T(8,128)(2,1)S(1)}, bf16[4,10,16,256]{3,2,1,0:T(8,128)(2,1)S(1)}, u32[]{:S(2)}, u32[]{:S(2)}) collective-permute-start(bf16[4,10,16,256]{3,2,1,0:T(8,128)(2,1)S(1)} %ahead.1.refs_7_.refs_0_), channel_id=1, source_target_pairs={{0,32},{16,48},{32,0},{48,16},{64,96},{80,112},{96,64},{112,80},{1... | collective-permute-start | bytes 983048 | tf_op jit(solution)/shard_map/ppermute | solution.py:58
  71.0 2.0 %collective-permute-start.19 = (bf16[4,10,16,256]{3,2,1,0:T(8,128)(2,1)S(1)}, bf16[4,10,16,256]{3,2,1,0:T(8,128)(2,1)S(1)}, u32[]{:S(2)}, u32[]{:S(2)}) collective-permute-start(bf16[4,10,16,256]{3,2,1,0:T(8,128)(2,1)S(1)} %ahead.1.refs_7_.refs_0_), channel_id=1, source_target_pairs={{0,48},{16,0},{32,16},{48,32},{64,112},{80,64},{96,80},{112,96},{1... | collective-permute-start | bytes 983048 | tf_op jit(solution)/shard_map/ppermute | solution.py:58
  73.0 6.5 %input.1 = (bf16[16,256,256]{2,1,0:T(8,128)(2,1)}, f32[8,128]{1,0:T(8,128)S(1)}) custom-call(s32[3]{0:T(128)S(1)} %pad_add_fusion.place, bf16[37,16,256]{2,1,0:T(8,128)(2,1)S(1)} %kernels.1.refs_0_, bf16[37,16,256]{2,1,0:T(8,128)(2,1)S(1)} %collective-permute-done.10.refs_1_, bf16[37,16,256]{2,1,0:T(8,128)(2,1)S(1)} %collective-permute-done.11.refs_2_, ...), custom_call_target="tpu_custom_call" | custom-call | flops 4831838208 | bytes 4194304 | tf_op jit(solution)/shard_map/input/pallas_call | solution.py:464
  79.6 1.2 %collective-permute-done.16 = f32[8,256]{1,0:T(8,128)S(1)} collective-permute-done((f32[8,256]{1,0:T(8,128)S(1)}, f32[8,256]{1,0:T(8,128)S(1)}, u32[]{:S(2)}, u32[]{:S(2)}) %collective-permute-start.16) | collective-permute-done | bytes 8224 | tf_op jit(solution)/shard_map/ppermute | solution.py:38
  81.3 1.9 %collective-permute-done.18.refs_2_ = bf16[4,10,16,256]{3,2,1,0:T(8,128)(2,1)S(1)} collective-permute-done((bf16[4,10,16,256]{3,2,1,0:T(8,128)(2,1)S(1)}, bf16[4,10,16,256]{3,2,1,0:T(8,128)(2,1)S(1)}, u32[]{:S(2)}, u32[]{:S(2)}) %collective-permute-start.18) | collective-permute-done | bytes 327712 | tf_op jit(solution)/shard_map/ppermute | solution.py:58
  83.2 1.3 %banks.1 = f32[8,9,16,256]{3,2,1,0:T(8,128)} custom-call(bf16[4,10,16,256]{3,2,1,0:T(8,128)(2,1)S(1)} %ahead.1.refs_7_.refs_0_, bf16[4,10,16,256]{3,2,1,0:T(8,128)(2,1)S(1)} %collective-permute-done.17.refs_1_, bf16[4,10,16,256]{3,2,1,0:T(8,128)(2,1)S(1)} %collective-permute-done.18.refs_2_, bf16[4,10,16,256]{3,2,1,0:T(8,128)(2,1)S(1)} %collective-permute-done.19.refs_3_), custom_call_target="tpu_custom_call" | custom-call | flops 10000000 | bytes 3000000 | tf_op jit(solution)/shard_map/banks/pallas_call | solution.py:482
  (32 shorter events, 3.4 us)
Async XLA Ops:
  0.6 4.8 %copy-start.2 = (s32[1,3]{1,0:T(1,128)S(1)}, s32[1,3]{1,0:T(1,128)}, u32[]{:S(2)}) copy-start(s32[1,3]{1,0:T(1,128)} %sel.3) | copy-start | bytes 40
  0.6 4.8 %copy-start.1 = (f32[1,256]{1,0:T(1,128)S(1)}, f32[1,256]{1,0:T(1,128)}, u32[]{:S(2)}) copy-start(f32[1,256]{1,0:T(1,128)} %style.6) | copy-start | bytes 3076
  0.7 4.8 %copy-start.4 = (bf16[8,16,9,256]{3,1,2,0:T(8,128)(2,1)S(1)}, bf16[8,16,9,256]{3,1,2,0:T(8,128)(2,1)}, u32[]{:S(2)}) copy-start(bf16[8,16,9,256]{3,1,2,0:T(8,128)(2,1)} %param.8) | copy-start | bytes 1769476
  2.4 25.4 %collective-permute-start = (bf16[256,256]{1,0:T(8,128)(2,1)}, bf16[256,256]{1,0:T(8,128)(2,1)S(1)}, u32[]{:S(2)}, u32[]{:S(2)}) collective-permute-start(bf16[256,256]{1,0:T(8,128)(2,1)} %get-tuple-element.24), channel_id=1, source_target_pairs={{0,1},{1,2},{2,3},{3,4},{4,5},{5,6},{6,7},{7,8},{8,9},{9,10},{10,1... | collective-permute-start | bytes 393224 | tf_op jit(solution)/shard_map/ppermute | solution.py:391
  4.2 23.6 %collective-permute-start.1 = (bf16[256,256]{1,0:T(8,128)(2,1)}, bf16[256,256]{1,0:T(8,128)(2,1)S(1)}, u32[]{:S(2)}, u32[]{:S(2)}) collective-permute-start(bf16[256,256]{1,0:T(8,128)(2,1)} %get-tuple-element.25), channel_id=1, source_target_pairs={{1,0},{2,1},{3,2},{4,3},{5,4},{6,5},{7,6},{8,7},{9,8},{10,9},{11,1... | collective-permute-start | bytes 393224 | tf_op jit(solution)/shard_map/ppermute | solution.py:392
  5.5 14.5 %copy-start = (bf16[1,16,256,256]{3,2,1,0:T(8,128)(2,1)S(1)}, bf16[1,16,256,256]{3,2,1,0:T(8,128)(2,1)}, u32[]{:S(2)}) copy-start(bf16[1,16,256,256]{3,2,1,0:T(8,128)(2,1)} %param.6) | copy-start | bytes 6291460
  6.3 21.5 %collective-permute-start.2 = (bf16[9,16,256]{2,1,0:T(8,128)(2,1)S(1)}, bf16[9,16,256]{2,1,0:T(8,128)(2,1)S(1)}, u32[]{:S(2)}, u32[]{:S(2)}) collective-permute-start(bf16[9,16,256]{2,1,0:T(8,128)(2,1)S(1)} %get-tuple-element.26.near.refs_0_), channel_id=1, source_target_pairs={{0,2},{1,3},{2,0},{3,1},{4,6},{5,7},{6,4},{7,5},{8,10},{9,11},{10,... | collective-permute-start | bytes 221192 | tf_op jit(solution)/shard_map/ppermute | solution.py:42
  20.0 1.6 %copy-start.3 = (bf16[1,16,256,256]{3,2,1,0:T(8,128)(2,1)S(1)}, bf16[1,16,256,256]{3,2,1,0:T(8,128)(2,1)}, u32[]{:S(2)}) copy-start(bf16[1,16,256,256]{3,2,1,0:T(8,128)(2,1)} %param.5) | copy-start | bytes 6291460
  28.8 2.1 %collective-permute-start.3 = (bf16[8,9,16,256]{3,2,1,0:T(8,128)(2,1)S(1)}, bf16[8,9,16,256]{3,2,1,0:T(8,128)(2,1)S(1)}, u32[]{:S(2)}, u32[]{:S(2)}) collective-permute-start(bf16[8,9,16,256]{3,2,1,0:T(8,128)(2,1)S(1)} %get-tuple-element.28), channel_id=1, source_target_pairs={{0,1},{1,0},{2,3},{3,2},{4,5},{5,4},{6,7},{7,6},{8,9},{9,8},{10,11... | collective-permute-start | bytes 1769480 | tf_op jit(solution)/shard_map/ppermute | solution.py:38
  31.5 8.3 %collective-permute-start.4 = (bf16[2,9,16,256]{3,2,1,0:T(8,128)(2,1)S(1)}, bf16[2,9,16,256]{3,2,1,0:T(8,128)(2,1)S(1)}, u32[]{:S(2)}, u32[]{:S(2)}) collective-permute-start(bf16[2,9,16,256]{3,2,1,0:T(8,128)(2,1)S(1)} %get-tuple-element.30), channel_id=1, source_target_pairs={{0,8},{1,9},{2,10},{3,11},{4,12},{5,13},{6,14},{7,15},{8,0},{9,1},... | collective-permute-start | bytes 442376 | tf_op jit(solution)/shard_map/ppermute | solution.py:46
  34.7 7.6 %collective-permute-start.5 = (bf16[2,9,16,256]{3,2,1,0:T(8,128)(2,1)S(1)}, bf16[2,9,16,256]{3,2,1,0:T(8,128)(2,1)S(1)}, u32[]{:S(2)}, u32[]{:S(2)}) collective-permute-start(bf16[2,9,16,256]{3,2,1,0:T(8,128)(2,1)S(1)} %get-tuple-element.31), channel_id=1, source_target_pairs={{0,4},{1,5},{2,6},{3,7},{4,8},{5,9},{6,10},{7,11},{8,12},{9,13},{1... | collective-permute-start | bytes 442376 | tf_op jit(solution)/shard_map/ppermute | solution.py:46
  35.2 7.0 %collective-permute-start.6 = (bf16[2,9,16,256]{3,2,1,0:T(8,128)(2,1)S(1)}, bf16[2,9,16,256]{3,2,1,0:T(8,128)(2,1)S(1)}, u32[]{:S(2)}, u32[]{:S(2)}) collective-permute-start(bf16[2,9,16,256]{3,2,1,0:T(8,128)(2,1)S(1)} %get-tuple-element.32), channel_id=1, source_target_pairs={{0,12},{1,13},{2,14},{3,15},{4,0},{5,1},{6,2},{7,3},{8,4},{9,5},{1... | collective-permute-start | bytes 442376 | tf_op jit(solution)/shard_map/ppermute | solution.py:46
  37.9 1.3 %collective-permute-start.7 = (bf16[9,16,256]{2,1,0:T(8,128)(2,1)S(1)}, bf16[9,16,256]{2,1,0:T(8,128)(2,1)S(1)}, u32[]{:S(2)}, u32[]{:S(2)}) collective-permute-start(bf16[9,16,256]{2,1,0:T(8,128)(2,1)S(1)} %get-tuple-element.26.near.refs_0_), channel_id=1, source_target_pairs={{0,1},{1,0},{2,3},{3,2},{4,5},{5,4},{6,7},{7,6},{8,9},{9,8},{10,11... | collective-permute-start | bytes 221192 | tf_op jit(solution)/shard_map/ppermute | solution.py:38
  37.9 1.4 %collective-permute-start.8 = (bf16[9,16,256]{2,1,0:T(8,128)(2,1)S(1)}, bf16[9,16,256]{2,1,0:T(8,128)(2,1)S(1)}, u32[]{:S(2)}, u32[]{:S(2)}) collective-permute-start(bf16[9,16,256]{2,1,0:T(8,128)(2,1)S(1)} %collective-permute-done.2.after.got.refs_2_), channel_id=1, source_target_pairs={{0,1},{1,0},{2,3},{3,2},{4,5},{5,4},{6,7},{7,6},{8,9},{9,8},{10,11... | collective-permute-start | bytes 221192 | tf_op jit(solution)/shard_map/ppermute | solution.py:38
  43.0 8.8 %collective-permute-start.9 = (bf16[10,16,256]{2,1,0:T(8,128)(2,1)S(1)}, bf16[10,16,256]{2,1,0:T(8,128)(2,1)S(1)}, u32[]{:S(2)}, u32[]{:S(2)}) collective-permute-start(bf16[10,16,256]{2,1,0:T(8,128)(2,1)S(1)} %get-tuple-element.34.sent), channel_id=1, source_target_pairs={{0,2},{1,3},{2,0},{3,1},{4,6},{5,7},{6,4},{7,5},{8,10},{9,11},{10,... | collective-permute-start | bytes 245768 | tf_op jit(solution)/shard_map/ppermute | solution.py:42
  52.5 18.4 %collective-permute-start.10 = (bf16[37,16,256]{2,1,0:T(8,128)(2,1)S(1)}, bf16[37,16,256]{2,1,0:T(8,128)(2,1)S(1)}, u32[]{:S(2)}, u32[]{:S(2)}) collective-permute-start(bf16[37,16,256]{2,1,0:T(8,128)(2,1)S(1)} %kernels.1.refs_0_), channel_id=1, source_target_pairs={{0,8},{1,9},{2,10},{3,11},{4,12},{5,13},{6,14},{7,15},{8,0},{9,1},... | collective-permute-start | bytes 909320 | tf_op jit(solution)/shard_map/ppermute | solution.py:46
  54.6 18.4 %collective-permute-start.11 = (bf16[37,16,256]{2,1,0:T(8,128)(2,1)S(1)}, bf16[37,16,256]{2,1,0:T(8,128)(2,1)S(1)}, u32[]{:S(2)}, u32[]{:S(2)}) collective-permute-start(bf16[37,16,256]{2,1,0:T(8,128)(2,1)S(1)} %kernels.1.refs_0_), channel_id=1, source_target_pairs={{0,4},{1,5},{2,6},{3,7},{4,8},{5,9},{6,10},{7,11},{8,12},{9,13},{1... | collective-permute-start | bytes 909320 | tf_op jit(solution)/shard_map/ppermute | solution.py:46
  56.2 16.8 %collective-permute-start.12 = (bf16[37,16,256]{2,1,0:T(8,128)(2,1)S(1)}, bf16[37,16,256]{2,1,0:T(8,128)(2,1)S(1)}, u32[]{:S(2)}, u32[]{:S(2)}) collective-permute-start(bf16[37,16,256]{2,1,0:T(8,128)(2,1)S(1)} %kernels.1.refs_0_), channel_id=1, source_target_pairs={{0,12},{1,13},{2,14},{3,15},{4,0},{5,1},{6,2},{7,3},{8,4},{9,5},{1... | collective-permute-start | bytes 909320 | tf_op jit(solution)/shard_map/ppermute | solution.py:46
  57.9 4.5 %collective-permute-start.13 = (bf16[10,16,256]{2,1,0:T(8,128)(2,1)S(1)}, bf16[10,16,256]{2,1,0:T(8,128)(2,1)S(1)}, u32[]{:S(2)}, u32[]{:S(2)}) collective-permute-start(bf16[10,16,256]{2,1,0:T(8,128)(2,1)S(1)} %get-tuple-element.36.refs_0_), channel_id=1, source_target_pairs={{0,64},{16,80},{32,96},{48,112},{64,0},{80,16},{96,32},{112,48},{1... | collective-permute-start | bytes 245768 | tf_op jit(solution)/shard_map/ppermute | solution.py:54
  58.8 7.0 %collective-permute-start.14 = (bf16[10,16,256]{2,1,0:T(8,128)(2,1)S(1)}, bf16[10,16,256]{2,1,0:T(8,128)(2,1)S(1)}, u32[]{:S(2)}, u32[]{:S(2)}) collective-permute-start(bf16[10,16,256]{2,1,0:T(8,128)(2,1)S(1)} %get-tuple-element.36.refs_0_), channel_id=1, source_target_pairs={{0,128},{16,144},{32,160},{48,176},{64,192},{80,208},{96,224},{112... | collective-permute-start | bytes 245768 | tf_op jit(solution)/shard_map/ppermute | solution.py:54
  62.3 6.2 %collective-permute-start.15 = (bf16[10,16,256]{2,1,0:T(8,128)(2,1)S(1)}, bf16[10,16,256]{2,1,0:T(8,128)(2,1)S(1)}, u32[]{:S(2)}, u32[]{:S(2)}) collective-permute-start(bf16[10,16,256]{2,1,0:T(8,128)(2,1)S(1)} %get-tuple-element.36.refs_0_), channel_id=1, source_target_pairs={{0,192},{16,208},{32,224},{48,240},{64,128},{80,144},{96,160},{112... | collective-permute-start | bytes 245768 | tf_op jit(solution)/shard_map/ppermute | solution.py:54
  68.6 12.7 %collective-permute-start.17 = (bf16[4,10,16,256]{3,2,1,0:T(8,128)(2,1)S(1)}, bf16[4,10,16,256]{3,2,1,0:T(8,128)(2,1)S(1)}, u32[]{:S(2)}, u32[]{:S(2)}) collective-permute-start(bf16[4,10,16,256]{3,2,1,0:T(8,128)(2,1)S(1)} %ahead.1.refs_7_.refs_0_), channel_id=1, source_target_pairs={{0,32},{16,48},{32,0},{48,16},{64,96},{80,112},{96,64},{112,80},{1... | collective-permute-start | bytes 983048 | tf_op jit(solution)/shard_map/ppermute | solution.py:58
  71.0 12.2 %collective-permute-start.18 = (bf16[4,10,16,256]{3,2,1,0:T(8,128)(2,1)S(1)}, bf16[4,10,16,256]{3,2,1,0:T(8,128)(2,1)S(1)}, u32[]{:S(2)}, u32[]{:S(2)}) collective-permute-start(bf16[4,10,16,256]{3,2,1,0:T(8,128)(2,1)S(1)} %ahead.1.refs_7_.refs_0_), channel_id=1, source_target_pairs={{0,16},{16,32},{32,48},{48,0},{64,80},{80,96},{96,112},{112,64},{1... | collective-permute-start | bytes 983048 | tf_op jit(solution)/shard_map/ppermute | solution.py:58
  71.0 12.2 %collective-permute-start.19 = (bf16[4,10,16,256]{3,2,1,0:T(8,128)(2,1)S(1)}, bf16[4,10,16,256]{3,2,1,0:T(8,128)(2,1)S(1)}, u32[]{:S(2)}, u32[]{:S(2)}) collective-permute-start(bf16[4,10,16,256]{3,2,1,0:T(8,128)(2,1)S(1)} %ahead.1.refs_7_.refs_0_), channel_id=1, source_target_pairs={{0,48},{16,0},{32,16},{48,32},{64,112},{80,64},{96,80},{112,96},{1... | collective-permute-start | bytes 983048 | tf_op jit(solution)/shard_map/ppermute | solution.py:58
  79.5 1.3 %collective-permute-start.16 = (f32[8,256]{1,0:T(8,128)S(1)}, f32[8,256]{1,0:T(8,128)S(1)}, u32[]{:S(2)}, u32[]{:S(2)}) collective-permute-start(f32[8,256]{1,0:T(8,128)S(1)} %style.7), channel_id=1, source_target_pairs={{0,1},{1,0},{2,3},{3,2},{4,5},{5,4},{6,7},{7,6},{8,9},{9,8},{10,11... | collective-permute-start | bytes 24584 | tf_op jit(solution)/shard_map/ppermute | solution.py:38

commit v7 on v6

--- a/solution.py
+++ b/solution.py
@@ -289,6 +289,11 @@
     out[...] = jnp.broadcast_to((zero + two) + (one + three), out.shape)
 
 
+def add_body(one, two, token, out):
+    del token
+    out[...] = one[0:1] + two[0:1]
+
+
 def ahead_body(*refs):
     out = refs[-1]
     for k, piece in enumerate(refs[:-1]):
@@ -296,10 +301,11 @@
 
 
 def banks_body(*refs):
-    out, both, sems = refs[-3:]
+    out, token, both, sems = refs[-4:]
     banks, taps, outs, channels = out.shape
+    token[...] = jnp.zeros(token.shape, F32)
     pieces = []
-    for ref in refs[:-3]:
+    for ref in refs[:-4]:
         if len(ref.shape) == 3:
             pieces.append(ref)
         else:
@@ -478,17 +484,19 @@
     )(place, *finals, low, high, cot, ahead)
 
     style_part = call(style_body, shape((8, channels), F32), [VMEM] * (NX + 1), name="style")(*finals, token)
-    style_grad = (style_part + swap_core(style_part))[:1]
-    bank_grad = pl.pallas_call(
+    bank_grad, token = pl.pallas_call(
         banks_body,
-        out_shape=shape((banks,) + piece, F32),
+        out_shape=(shape((banks,) + piece, F32), shape((8, 128), F32)),
         in_specs=[VMEM] * NY,
-        out_specs=HBM,
+        out_specs=(HBM, VMEM),
         scratch_shapes=[pltpu.VMEM((banks,) + piece, F32), dma((taps,))],
         compiler_params=pltpu.CompilerParams(vmem_limit_bytes=16 << 20),
         cost_estimate=pl.CostEstimate(flops=10**7, bytes_accessed=3 * 10**6, transcendentals=0),
         name="banks",
     )(ahead, *over_y)
+    style_grad = call(add_body, shape((1, channels), F32), [VMEM] * 3, name="add")(
+        style_part, swap_core(style_part), token
+    )
 
     return (
         input_grad.reshape(feature_map.shape),

time: 86.2 us -> 85.3 us (0.990); the launches traced: 84.6 us -> 85 us
    ppermute x3, waiting for transfers between devices: 1.87 us -> 3.59 us  [shift_y(): return lax.ppermute(a, 'img', img_perm(lambda l, y: (l, (y + k) % NY)))]
    ppermute x4, waiting for transfers between devices: 4.06 us -> 2.91 us  [swap_core(): return lax.ppermute(a, 'tile', tile_perm(lambda x, z, c: (x, z, 1 - c)))]
    pallas_call x1 -> x2, Pallas kernels: 1.28 us -> 1.85 us  [the longest x1 1.28 us: local(): pl.pallas_call(banks_body, out_shape=(shape((banks,) + piece, F32), shape...]
  transfers between devices with their start and end apart: 20 -> 20, of which waited for: 11 -> 10; matrix products, arithmetic and copies ran while one was open for 1% -> 0% of each run, Pallas kernels for 16% -> 17%
where the time goes in v7:
time: 85.3 us; the launch traced here: 85 us
  starting transfers between devices  38.7 us (45%)
  waiting for transfers between devices  23.8 us (28%)
  Pallas kernels  20.1 us (24%)
  local copies, waits for them, and re-layouts  1.61 us (2%)
    ppermute x2, starting transfers between devices, swap_z(): return lax.ppermute(a, 'tile', tile_perm(lambda x, z, c: (x, 1 - z, c)))  14.7 us
    ppermute x6, starting transfers between devices, shift_x(): lax.ppermute(a, 'tile', tile_perm(lambda x, z, c: ((x + k) % NX, z, c)))  11.7 us
    ppermute x2, waiting for transfers between devices, swap_z(): return lax.ppermute(a, 'tile', tile_perm(lambda x, z, c: (x, 1 - z, c)))  7.79 us
    ppermute x3, waiting for transfers between devices, flip_l(): return lax.ppermute(a, 'img', img_perm(lambda l, y: (l ^ k, y)))  6.51 us
    pallas_call x1, Pallas kernels, local(): call(input_body, (shape((rows, width, channels), BF16), shape((8, 128), F...  6.47 us
    pallas_call x1, Pallas kernels, local(): call(grad_body, (shape((taps, NC, groups, 16, channels), F32), shape((2,...  6.12 us
    ppermute x3, starting transfers between devices, shift_y(): return lax.ppermute(a, 'img', img_perm(lambda l, y: (l, (y + k) % NY)))  4.41 us
    ppermute x3, starting transfers between devices, flip_l(): return lax.ppermute(a, 'img', img_perm(lambda l, y: (l ^ k, y)))  4.17 us
  transfers between devices with their start and end apart: 20, of which 10 were waited for; matrix products, arithmetic and copies ran while one was open for 0% of the time, Pallas kernels for 17%

profile of v7, /device:TPU:8, one launch (start us, length us, event | category | flops | bytes accessed | tf_op | source)
XLA Modules:
  0.0 85.0 jit_solution(10411954503683728428)
XLA Ops:
  0.7 1.7 %rows.1 = (bf16[256,256]{1,0:T(8,128)(2,1)}, bf16[256,256]{1,0:T(8,128)(2,1)}) custom-call(bf16[16,256,256]{2,1,0:T(8,128)(2,1)} %bitcast.8), custom_call_target="tpu_custom_call" | custom-call | bytes 1000000 | tf_op jit(solution)/shard_map/rows/pallas_call | solution.py:387
  2.4 1.7 %collective-permute-start = (bf16[256,256]{1,0:T(8,128)(2,1)}, bf16[256,256]{1,0:T(8,128)(2,1)S(1)}, u32[]{:S(2)}, u32[]{:S(2)}) collective-permute-start(bf16[256,256]{1,0:T(8,128)(2,1)} %get-tuple-element.26), channel_id=1, source_target_pairs={{0,1},{1,2},{2,3},{3,4},{4,5},{5,6},{6,7},{7,8},{8,9},{9,10},{10,1... | collective-permute-start | bytes 393224 | tf_op jit(solution)/shard_map/ppermute | solution.py:397
  4.2 1.3 %collective-permute-start.1 = (bf16[256,256]{1,0:T(8,128)(2,1)}, bf16[256,256]{1,0:T(8,128)(2,1)S(1)}, u32[]{:S(2)}, u32[]{:S(2)}) collective-permute-start(bf16[256,256]{1,0:T(8,128)(2,1)} %get-tuple-element.27), channel_id=1, source_target_pairs={{1,0},{2,1},{3,2},{4,3},{5,4},{6,5},{7,6},{8,7},{9,8},{10,9},{11,1... | collective-permute-start | bytes 393224 | tf_op jit(solution)/shard_map/ppermute | solution.py:398
  5.5 0.8 mix.1
  6.3 13.7 %collective-permute-start.2 = (bf16[9,16,256]{2,1,0:T(8,128)(2,1)S(1)}, bf16[9,16,256]{2,1,0:T(8,128)(2,1)S(1)}, u32[]{:S(2)}, u32[]{:S(2)}) collective-permute-start(bf16[9,16,256]{2,1,0:T(8,128)(2,1)S(1)} %get-tuple-element.28.near.refs_0_), channel_id=1, source_target_pairs={{0,2},{1,3},{2,0},{3,1},{4,6},{5,7},{6,4},{7,5},{8,10},{9,11},{10,... | collective-permute-start | bytes 221192 | tf_op jit(solution)/shard_map/ppermute | solution.py:42
  20.0 1.6 %copy-done.3 = bf16[1,16,256,256]{3,2,1,0:T(8,128)(2,1)S(1)} copy-done((bf16[1,16,256,256]{3,2,1,0:T(8,128)(2,1)S(1)}, bf16[1,16,256,256]{3,2,1,0:T(8,128)(2,1)}, u32[]{:S(2)}) %copy-start.3) | copy-done | bytes 2097176
  21.6 6.1 %grad.1 = (f32[9,2,8,16,256]{4,3,2,1,0:T(8,128)S(1)}, bf16[2,256,256]{2,1,0:T(8,128)(2,1)S(1)}) custom-call(s32[3]{0:T(128)S(1)} %pad_add_fusion.place, bf16[16,256,256]{2,1,0:T(8,128)(2,1)S(1)} %bitcast.9, bf16[16,256,256]{2,1,0:T(8,128)(2,1)S(1)} %bitcast.11), custom_call_target="tpu_custom_call" | custom-call | flops 4831838208 | bytes 4194304 | tf_op jit(solution)/shard_map/grad/pallas_call | solution.py:407
  27.8 1.0 %edge.1 = (f32[8,9,16,256]{3,2,1,0:T(8,128)S(1)}, bf16[8,9,16,256]{3,2,1,0:T(8,128)(2,1)S(1)}) custom-call(s32[3]{0:T(128)S(1)} %pad_add_fusion.place, f32[9,2,8,16,256]{4,3,2,1,0:T(8,128)S(1)} %get-tuple-element.24.grad, bf16[2,256,256]{2,1,0:T(8,128)(2,1)S(1)} %get-tuple-element.25.ends, bf16[256,256]{1,0:T(8,128)(2,1)S(1)} %collective-permute-done.low.refs_4_, ...), custom_call_target="tpu_custom_call" | custom-call | flops 201326592 | bytes 4000000 | tf_op jit(solution)/shard_map/edge/pallas_call | solution.py:420
  28.9 2.0 %collective-permute-done.3.got = bf16[8,9,16,256]{3,2,1,0:T(8,128)(2,1)S(1)} collective-permute-done((bf16[8,9,16,256]{3,2,1,0:T(8,128)(2,1)S(1)}, bf16[8,9,16,256]{3,2,1,0:T(8,128)(2,1)S(1)}, u32[]{:S(2)}, u32[]{:S(2)}) %collective-permute-start.3) | collective-permute-done | bytes 589856 | tf_op jit(solution)/shard_map/ppermute | solution.py:38
  30.9 0.6 split_x.1
  31.5 3.1 %collective-permute-start.4 = (bf16[2,9,16,256]{3,2,1,0:T(8,128)(2,1)S(1)}, bf16[2,9,16,256]{3,2,1,0:T(8,128)(2,1)S(1)}, u32[]{:S(2)}, u32[]{:S(2)}) collective-permute-start(bf16[2,9,16,256]{3,2,1,0:T(8,128)(2,1)S(1)} %get-tuple-element.32), channel_id=1, source_target_pairs={{0,8},{1,9},{2,10},{3,11},{4,12},{5,13},{6,14},{7,15},{8,0},{9,1},... | collective-permute-start | bytes 442376 | tf_op jit(solution)/shard_map/ppermute | solution.py:46
  35.2 2.6 %collective-permute-start.6 = (bf16[2,9,16,256]{3,2,1,0:T(8,128)(2,1)S(1)}, bf16[2,9,16,256]{3,2,1,0:T(8,128)(2,1)S(1)}, u32[]{:S(2)}, u32[]{:S(2)}) collective-permute-start(bf16[2,9,16,256]{3,2,1,0:T(8,128)(2,1)S(1)} %get-tuple-element.34), channel_id=1, source_target_pairs={{0,12},{1,13},{2,14},{3,15},{4,0},{5,1},{6,2},{7,3},{8,4},{9,5},{1... | collective-permute-start | bytes 442376 | tf_op jit(solution)/shard_map/ppermute | solution.py:46
  38.4 0.8 collective-permute-done.7.after.refs_1_
  39.8 2.4 %collective-permute-done.5.one = bf16[2,9,16,256]{3,2,1,0:T(8,128)(2,1)S(1)} collective-permute-done((bf16[2,9,16,256]{3,2,1,0:T(8,128)(2,1)S(1)}, bf16[2,9,16,256]{3,2,1,0:T(8,128)(2,1)S(1)}, u32[]{:S(2)}, u32[]{:S(2)}) %collective-permute-start.5) | collective-permute-done | bytes 147488 | tf_op jit(solution)/shard_map/ppermute | solution.py:46
  42.3 0.7 split_z.1
  43.0 1.0 %collective-permute-start.9 = (bf16[10,16,256]{2,1,0:T(8,128)(2,1)S(1)}, bf16[10,16,256]{2,1,0:T(8,128)(2,1)S(1)}, u32[]{:S(2)}, u32[]{:S(2)}) collective-permute-start(bf16[10,16,256]{2,1,0:T(8,128)(2,1)S(1)} %get-tuple-element.36.sent), channel_id=1, source_target_pairs={{0,2},{1,3},{2,0},{3,1},{4,6},{5,7},{6,4},{7,5},{8,10},{9,11},{10,... | collective-permute-start | bytes 245768 | tf_op jit(solution)/shard_map/ppermute | solution.py:42
  44.0 7.8 %collective-permute-done.9.got = bf16[10,16,256]{2,1,0:T(8,128)(2,1)S(1)} collective-permute-done((bf16[10,16,256]{2,1,0:T(8,128)(2,1)S(1)}, bf16[10,16,256]{2,1,0:T(8,128)(2,1)S(1)}, u32[]{:S(2)}, u32[]{:S(2)}) %collective-permute-start.9) | collective-permute-done | bytes 81952 | tf_op jit(solution)/shard_map/ppermute | solution.py:42
  51.8 0.7 owner.1
  52.5 2.1 %collective-permute-start.10 = (bf16[37,16,256]{2,1,0:T(8,128)(2,1)S(1)}, bf16[37,16,256]{2,1,0:T(8,128)(2,1)S(1)}, u32[]{:S(2)}, u32[]{:S(2)}) collective-permute-start(bf16[37,16,256]{2,1,0:T(8,128)(2,1)S(1)} %kernels.1.refs_0_), channel_id=1, source_target_pairs={{0,8},{1,9},{2,10},{3,11},{4,12},{5,13},{6,14},{7,15},{8,0},{9,1},... | collective-permute-start | bytes 909320 | tf_op jit(solution)/shard_map/ppermute | solution.py:46
  54.6 1.6 %collective-permute-start.11 = (bf16[37,16,256]{2,1,0:T(8,128)(2,1)S(1)}, bf16[37,16,256]{2,1,0:T(8,128)(2,1)S(1)}, u32[]{:S(2)}, u32[]{:S(2)}) collective-permute-start(bf16[37,16,256]{2,1,0:T(8,128)(2,1)S(1)} %kernels.1.refs_0_), channel_id=1, source_target_pairs={{0,4},{1,5},{2,6},{3,7},{4,8},{5,9},{6,10},{7,11},{8,12},{9,13},{1... | collective-permute-start | bytes 909320 | tf_op jit(solution)/shard_map/ppermute | solution.py:46
  56.2 1.6 %collective-permute-start.12 = (bf16[37,16,256]{2,1,0:T(8,128)(2,1)S(1)}, bf16[37,16,256]{2,1,0:T(8,128)(2,1)S(1)}, u32[]{:S(2)}, u32[]{:S(2)}) collective-permute-start(bf16[37,16,256]{2,1,0:T(8,128)(2,1)S(1)} %kernels.1.refs_0_), channel_id=1, source_target_pairs={{0,12},{1,13},{2,14},{3,15},{4,0},{5,1},{6,2},{7,3},{8,4},{9,5},{1... | collective-permute-start | bytes 909320 | tf_op jit(solution)/shard_map/ppermute | solution.py:46
  57.9 0.9 %collective-permute-start.13 = (bf16[10,16,256]{2,1,0:T(8,128)(2,1)S(1)}, bf16[10,16,256]{2,1,0:T(8,128)(2,1)S(1)}, u32[]{:S(2)}, u32[]{:S(2)}) collective-permute-start(bf16[10,16,256]{2,1,0:T(8,128)(2,1)S(1)} %get-tuple-element.38.refs_0_), channel_id=1, source_target_pairs={{0,64},{16,80},{32,96},{48,112},{64,0},{80,16},{96,32},{112,48},{1... | collective-permute-start | bytes 245768 | tf_op jit(solution)/shard_map/ppermute | solution.py:54
  58.8 1.4 %collective-permute-start.14 = (bf16[10,16,256]{2,1,0:T(8,128)(2,1)S(1)}, bf16[10,16,256]{2,1,0:T(8,128)(2,1)S(1)}, u32[]{:S(2)}, u32[]{:S(2)}) collective-permute-start(bf16[10,16,256]{2,1,0:T(8,128)(2,1)S(1)} %get-tuple-element.38.refs_0_), channel_id=1, source_target_pairs={{0,128},{16,144},{32,160},{48,176},{64,192},{80,208},{96,224},{112... | collective-permute-start | bytes 245768 | tf_op jit(solution)/shard_map/ppermute | solution.py:54
  60.2 2.1 %collective-permute-done.13.refs_1_ = bf16[10,16,256]{2,1,0:T(8,128)(2,1)S(1)} collective-permute-done((bf16[10,16,256]{2,1,0:T(8,128)(2,1)S(1)}, bf16[10,16,256]{2,1,0:T(8,128)(2,1)S(1)}, u32[]{:S(2)}, u32[]{:S(2)}) %collective-permute-start.13) | collective-permute-done | bytes 81952 | tf_op jit(solution)/shard_map/ppermute | solution.py:54
  62.3 1.8 %collective-permute-start.15 = (bf16[10,16,256]{2,1,0:T(8,128)(2,1)S(1)}, bf16[10,16,256]{2,1,0:T(8,128)(2,1)S(1)}, u32[]{:S(2)}, u32[]{:S(2)}) collective-permute-start(bf16[10,16,256]{2,1,0:T(8,128)(2,1)S(1)} %get-tuple-element.38.refs_0_), channel_id=1, source_target_pairs={{0,192},{16,208},{32,224},{48,240},{64,128},{80,144},{96,160},{112... | collective-permute-start | bytes 245768 | tf_op jit(solution)/shard_map/ppermute | solution.py:54
  64.1 1.7 %collective-permute-done.14.refs_2_ = bf16[10,16,256]{2,1,0:T(8,128)(2,1)S(1)} collective-permute-done((bf16[10,16,256]{2,1,0:T(8,128)(2,1)S(1)}, bf16[10,16,256]{2,1,0:T(8,128)(2,1)S(1)}, u32[]{:S(2)}, u32[]{:S(2)}) %collective-permute-start.14) | collective-permute-done | bytes 81952 | tf_op jit(solution)/shard_map/ppermute | solution.py:54
  65.8 2.7 %collective-permute-done.15.refs_3_ = bf16[10,16,256]{2,1,0:T(8,128)(2,1)S(1)} collective-permute-done((bf16[10,16,256]{2,1,0:T(8,128)(2,1)S(1)}, bf16[10,16,256]{2,1,0:T(8,128)(2,1)S(1)}, u32[]{:S(2)}, u32[]{:S(2)}) %collective-permute-start.15) | collective-permute-done | bytes 81952 | tf_op jit(solution)/shard_map/ppermute | solution.py:54
  68.6 2.4 %collective-permute-start.17 = (bf16[4,10,16,256]{3,2,1,0:T(8,128)(2,1)S(1)}, bf16[4,10,16,256]{3,2,1,0:T(8,128)(2,1)S(1)}, u32[]{:S(2)}, u32[]{:S(2)}) collective-permute-start(bf16[4,10,16,256]{3,2,1,0:T(8,128)(2,1)S(1)} %ahead.1.refs_7_.refs_0_), channel_id=1, source_target_pairs={{0,32},{16,48},{32,0},{48,16},{64,96},{80,112},{96,64},{112,80},{1... | collective-permute-start | bytes 983048 | tf_op jit(solution)/shard_map/ppermute | solution.py:58
  71.0 2.0 %collective-permute-start.19 = (bf16[4,10,16,256]{3,2,1,0:T(8,128)(2,1)S(1)}, bf16[4,10,16,256]{3,2,1,0:T(8,128)(2,1)S(1)}, u32[]{:S(2)}, u32[]{:S(2)}) collective-permute-start(bf16[4,10,16,256]{3,2,1,0:T(8,128)(2,1)S(1)} %ahead.1.refs_7_.refs_0_), channel_id=1, source_target_pairs={{0,48},{16,0},{32,16},{48,32},{64,112},{80,64},{96,80},{112,96},{1... | collective-permute-start | bytes 983048 | tf_op jit(solution)/shard_map/ppermute | solution.py:58
  73.0 6.5 %input.1 = (bf16[16,256,256]{2,1,0:T(8,128)(2,1)}, f32[8,128]{1,0:T(8,128)S(1)}) custom-call(s32[3]{0:T(128)S(1)} %pad_add_fusion.place, bf16[37,16,256]{2,1,0:T(8,128)(2,1)S(1)} %kernels.1.refs_0_, bf16[37,16,256]{2,1,0:T(8,128)(2,1)S(1)} %collective-permute-done.10.refs_1_, bf16[37,16,256]{2,1,0:T(8,128)(2,1)S(1)} %collective-permute-done.11.refs_2_, ...), custom_call_target="tpu_custom_call" | custom-call | flops 4831838208 | bytes 4194304 | tf_op jit(solution)/shard_map/input/pallas_call | solution.py:470
  79.6 3.6 %collective-permute-done.18.refs_2_ = bf16[4,10,16,256]{3,2,1,0:T(8,128)(2,1)S(1)} collective-permute-done((bf16[4,10,16,256]{3,2,1,0:T(8,128)(2,1)S(1)}, bf16[4,10,16,256]{3,2,1,0:T(8,128)(2,1)S(1)}, u32[]{:S(2)}, u32[]{:S(2)}) %collective-permute-start.18) | collective-permute-done | bytes 327712 | tf_op jit(solution)/shard_map/ppermute | solution.py:58
  83.2 1.3 %banks.1 = (f32[8,9,16,256]{3,2,1,0:T(8,128)}, f32[8,128]{1,0:T(8,128)S(1)}) custom-call(bf16[4,10,16,256]{3,2,1,0:T(8,128)(2,1)S(1)} %ahead.1.refs_7_.refs_0_, bf16[4,10,16,256]{3,2,1,0:T(8,128)(2,1)S(1)} %collective-permute-done.17.refs_1_, bf16[4,10,16,256]{3,2,1,0:T(8,128)(2,1)S(1)} %collective-permute-done.18.refs_2_, ...), custom_call_target="tpu_custom_call" | custom-call | flops 10000000 | bytes 3000000 | tf_op jit(solution)/shard_map/banks/pallas_call | solution.py:487
  (32 shorter events, 2.8 us)
Async XLA Ops:
  0.6 4.8 %copy-start.2 = (s32[1,3]{1,0:T(1,128)S(1)}, s32[1,3]{1,0:T(1,128)}, u32[]{:S(2)}) copy-start(s32[1,3]{1,0:T(1,128)} %sel.3) | copy-start | bytes 40
  0.6 4.8 %copy-start.1 = (f32[1,256]{1,0:T(1,128)S(1)}, f32[1,256]{1,0:T(1,128)}, u32[]{:S(2)}) copy-start(f32[1,256]{1,0:T(1,128)} %style.6) | copy-start | bytes 3076
  0.7 4.8 %copy-start.4 = (bf16[8,16,9,256]{3,1,2,0:T(8,128)(2,1)S(1)}, bf16[8,16,9,256]{3,1,2,0:T(8,128)(2,1)}, u32[]{:S(2)}) copy-start(bf16[8,16,9,256]{3,1,2,0:T(8,128)(2,1)} %param.8) | copy-start | bytes 1769476
  2.4 25.4 %collective-permute-start = (bf16[256,256]{1,0:T(8,128)(2,1)}, bf16[256,256]{1,0:T(8,128)(2,1)S(1)}, u32[]{:S(2)}, u32[]{:S(2)}) collective-permute-start(bf16[256,256]{1,0:T(8,128)(2,1)} %get-tuple-element.26), channel_id=1, source_target_pairs={{0,1},{1,2},{2,3},{3,4},{4,5},{5,6},{6,7},{7,8},{8,9},{9,10},{10,1... | collective-permute-start | bytes 393224 | tf_op jit(solution)/shard_map/ppermute | solution.py:397
  4.2 23.6 %collective-permute-start.1 = (bf16[256,256]{1,0:T(8,128)(2,1)}, bf16[256,256]{1,0:T(8,128)(2,1)S(1)}, u32[]{:S(2)}, u32[]{:S(2)}) collective-permute-start(bf16[256,256]{1,0:T(8,128)(2,1)} %get-tuple-element.27), channel_id=1, source_target_pairs={{1,0},{2,1},{3,2},{4,3},{5,4},{6,5},{7,6},{8,7},{9,8},{10,9},{11,1... | collective-permute-start | bytes 393224 | tf_op jit(solution)/shard_map/ppermute | solution.py:398
  5.5 14.5 %copy-start = (bf16[1,16,256,256]{3,2,1,0:T(8,128)(2,1)S(1)}, bf16[1,16,256,256]{3,2,1,0:T(8,128)(2,1)}, u32[]{:S(2)}) copy-start(bf16[1,16,256,256]{3,2,1,0:T(8,128)(2,1)} %param.6) | copy-start | bytes 6291460
  6.3 21.5 %collective-permute-start.2 = (bf16[9,16,256]{2,1,0:T(8,128)(2,1)S(1)}, bf16[9,16,256]{2,1,0:T(8,128)(2,1)S(1)}, u32[]{:S(2)}, u32[]{:S(2)}) collective-permute-start(bf16[9,16,256]{2,1,0:T(8,128)(2,1)S(1)} %get-tuple-element.28.near.refs_0_), channel_id=1, source_target_pairs={{0,2},{1,3},{2,0},{3,1},{4,6},{5,7},{6,4},{7,5},{8,10},{9,11},{10,... | collective-permute-start | bytes 221192 | tf_op jit(solution)/shard_map/ppermute | solution.py:42
  20.0 1.6 %copy-start.3 = (bf16[1,16,256,256]{3,2,1,0:T(8,128)(2,1)S(1)}, bf16[1,16,256,256]{3,2,1,0:T(8,128)(2,1)}, u32[]{:S(2)}) copy-start(bf16[1,16,256,256]{3,2,1,0:T(8,128)(2,1)} %param.5) | copy-start | bytes 6291460
  28.8 2.1 %collective-permute-start.3 = (bf16[8,9,16,256]{3,2,1,0:T(8,128)(2,1)S(1)}, bf16[8,9,16,256]{3,2,1,0:T(8,128)(2,1)S(1)}, u32[]{:S(2)}, u32[]{:S(2)}) collective-permute-start(bf16[8,9,16,256]{3,2,1,0:T(8,128)(2,1)S(1)} %get-tuple-element.30), channel_id=1, source_target_pairs={{0,1},{1,0},{2,3},{3,2},{4,5},{5,4},{6,7},{7,6},{8,9},{9,8},{10,11... | collective-permute-start | bytes 1769480 | tf_op jit(solution)/shard_map/ppermute | solution.py:38
  31.5 8.3 %collective-permute-start.4 = (bf16[2,9,16,256]{3,2,1,0:T(8,128)(2,1)S(1)}, bf16[2,9,16,256]{3,2,1,0:T(8,128)(2,1)S(1)}, u32[]{:S(2)}, u32[]{:S(2)}) collective-permute-start(bf16[2,9,16,256]{3,2,1,0:T(8,128)(2,1)S(1)} %get-tuple-element.32), channel_id=1, source_target_pairs={{0,8},{1,9},{2,10},{3,11},{4,12},{5,13},{6,14},{7,15},{8,0},{9,1},... | collective-permute-start | bytes 442376 | tf_op jit(solution)/shard_map/ppermute | solution.py:46
  34.7 7.6 %collective-permute-start.5 = (bf16[2,9,16,256]{3,2,1,0:T(8,128)(2,1)S(1)}, bf16[2,9,16,256]{3,2,1,0:T(8,128)(2,1)S(1)}, u32[]{:S(2)}, u32[]{:S(2)}) collective-permute-start(bf16[2,9,16,256]{3,2,1,0:T(8,128)(2,1)S(1)} %get-tuple-element.33), channel_id=1, source_target_pairs={{0,4},{1,5},{2,6},{3,7},{4,8},{5,9},{6,10},{7,11},{8,12},{9,13},{1... | collective-permute-start | bytes 442376 | tf_op jit(solution)/shard_map/ppermute | solution.py:46
  35.2 7.0 %collective-permute-start.6 = (bf16[2,9,16,256]{3,2,1,0:T(8,128)(2,1)S(1)}, bf16[2,9,16,256]{3,2,1,0:T(8,128)(2,1)S(1)}, u32[]{:S(2)}, u32[]{:S(2)}) collective-permute-start(bf16[2,9,16,256]{3,2,1,0:T(8,128)(2,1)S(1)} %get-tuple-element.34), channel_id=1, source_target_pairs={{0,12},{1,13},{2,14},{3,15},{4,0},{5,1},{6,2},{7,3},{8,4},{9,5},{1... | collective-permute-start | bytes 442376 | tf_op jit(solution)/shard_map/ppermute | solution.py:46
  37.9 1.3 %collective-permute-start.7 = (bf16[9,16,256]{2,1,0:T(8,128)(2,1)S(1)}, bf16[9,16,256]{2,1,0:T(8,128)(2,1)S(1)}, u32[]{:S(2)}, u32[]{:S(2)}) collective-permute-start(bf16[9,16,256]{2,1,0:T(8,128)(2,1)S(1)} %get-tuple-element.28.near.refs_0_), channel_id=1, source_target_pairs={{0,1},{1,0},{2,3},{3,2},{4,5},{5,4},{6,7},{7,6},{8,9},{9,8},{10,11... | collective-permute-start | bytes 221192 | tf_op jit(solution)/shard_map/ppermute | solution.py:38
  37.9 1.4 %collective-permute-start.8 = (bf16[9,16,256]{2,1,0:T(8,128)(2,1)S(1)}, bf16[9,16,256]{2,1,0:T(8,128)(2,1)S(1)}, u32[]{:S(2)}, u32[]{:S(2)}) collective-permute-start(bf16[9,16,256]{2,1,0:T(8,128)(2,1)S(1)} %collective-permute-done.2.after.got.refs_2_), channel_id=1, source_target_pairs={{0,1},{1,0},{2,3},{3,2},{4,5},{5,4},{6,7},{7,6},{8,9},{9,8},{10,11... | collective-permute-start | bytes 221192 | tf_op jit(solution)/shard_map/ppermute | solution.py:38
  43.0 8.8 %collective-permute-start.9 = (bf16[10,16,256]{2,1,0:T(8,128)(2,1)S(1)}, bf16[10,16,256]{2,1,0:T(8,128)(2,1)S(1)}, u32[]{:S(2)}, u32[]{:S(2)}) collective-permute-start(bf16[10,16,256]{2,1,0:T(8,128)(2,1)S(1)} %get-tuple-element.36.sent), channel_id=1, source_target_pairs={{0,2},{1,3},{2,0},{3,1},{4,6},{5,7},{6,4},{7,5},{8,10},{9,11},{10,... | collective-permute-start | bytes 245768 | tf_op jit(solution)/shard_map/ppermute | solution.py:42
  52.5 18.4 %collective-permute-start.10 = (bf16[37,16,256]{2,1,0:T(8,128)(2,1)S(1)}, bf16[37,16,256]{2,1,0:T(8,128)(2,1)S(1)}, u32[]{:S(2)}, u32[]{:S(2)}) collective-permute-start(bf16[37,16,256]{2,1,0:T(8,128)(2,1)S(1)} %kernels.1.refs_0_), channel_id=1, source_target_pairs={{0,8},{1,9},{2,10},{3,11},{4,12},{5,13},{6,14},{7,15},{8,0},{9,1},... | collective-permute-start | bytes 909320 | tf_op jit(solution)/shard_map/ppermute | solution.py:46
  54.6 18.4 %collective-permute-start.11 = (bf16[37,16,256]{2,1,0:T(8,128)(2,1)S(1)}, bf16[37,16,256]{2,1,0:T(8,128)(2,1)S(1)}, u32[]{:S(2)}, u32[]{:S(2)}) collective-permute-start(bf16[37,16,256]{2,1,0:T(8,128)(2,1)S(1)} %kernels.1.refs_0_), channel_id=1, source_target_pairs={{0,4},{1,5},{2,6},{3,7},{4,8},{5,9},{6,10},{7,11},{8,12},{9,13},{1... | collective-permute-start | bytes 909320 | tf_op jit(solution)/shard_map/ppermute | solution.py:46
  56.2 16.8 %collective-permute-start.12 = (bf16[37,16,256]{2,1,0:T(8,128)(2,1)S(1)}, bf16[37,16,256]{2,1,0:T(8,128)(2,1)S(1)}, u32[]{:S(2)}, u32[]{:S(2)}) collective-permute-start(bf16[37,16,256]{2,1,0:T(8,128)(2,1)S(1)} %kernels.1.refs_0_), channel_id=1, source_target_pairs={{0,12},{1,13},{2,14},{3,15},{4,0},{5,1},{6,2},{7,3},{8,4},{9,5},{1... | collective-permute-start | bytes 909320 | tf_op jit(solution)/shard_map/ppermute | solution.py:46
  57.9 4.5 %collective-permute-start.13 = (bf16[10,16,256]{2,1,0:T(8,128)(2,1)S(1)}, bf16[10,16,256]{2,1,0:T(8,128)(2,1)S(1)}, u32[]{:S(2)}, u32[]{:S(2)}) collective-permute-start(bf16[10,16,256]{2,1,0:T(8,128)(2,1)S(1)} %get-tuple-element.38.refs_0_), channel_id=1, source_target_pairs={{0,64},{16,80},{32,96},{48,112},{64,0},{80,16},{96,32},{112,48},{1... | collective-permute-start | bytes 245768 | tf_op jit(solution)/shard_map/ppermute | solution.py:54
  58.8 7.0 %collective-permute-start.14 = (bf16[10,16,256]{2,1,0:T(8,128)(2,1)S(1)}, bf16[10,16,256]{2,1,0:T(8,128)(2,1)S(1)}, u32[]{:S(2)}, u32[]{:S(2)}) collective-permute-start(bf16[10,16,256]{2,1,0:T(8,128)(2,1)S(1)} %get-tuple-element.38.refs_0_), channel_id=1, source_target_pairs={{0,128},{16,144},{32,160},{48,176},{64,192},{80,208},{96,224},{112... | collective-permute-start | bytes 245768 | tf_op jit(solution)/shard_map/ppermute | solution.py:54
  62.3 6.2 %collective-permute-start.15 = (bf16[10,16,256]{2,1,0:T(8,128)(2,1)S(1)}, bf16[10,16,256]{2,1,0:T(8,128)(2,1)S(1)}, u32[]{:S(2)}, u32[]{:S(2)}) collective-permute-start(bf16[10,16,256]{2,1,0:T(8,128)(2,1)S(1)} %get-tuple-element.38.refs_0_), channel_id=1, source_target_pairs={{0,192},{16,208},{32,224},{48,240},{64,128},{80,144},{96,160},{112... | collective-permute-start | bytes 245768 | tf_op jit(solution)/shard_map/ppermute | solution.py:54
  68.6 11.0 %collective-permute-start.17 = (bf16[4,10,16,256]{3,2,1,0:T(8,128)(2,1)S(1)}, bf16[4,10,16,256]{3,2,1,0:T(8,128)(2,1)S(1)}, u32[]{:S(2)}, u32[]{:S(2)}) collective-permute-start(bf16[4,10,16,256]{3,2,1,0:T(8,128)(2,1)S(1)} %ahead.1.refs_7_.refs_0_), channel_id=1, source_target_pairs={{0,32},{16,48},{32,0},{48,16},{64,96},{80,112},{96,64},{112,80},{1... | collective-permute-start | bytes 983048 | tf_op jit(solution)/shard_map/ppermute | solution.py:58
  71.0 12.2 %collective-permute-start.18 = (bf16[4,10,16,256]{3,2,1,0:T(8,128)(2,1)S(1)}, bf16[4,10,16,256]{3,2,1,0:T(8,128)(2,1)S(1)}, u32[]{:S(2)}, u32[]{:S(2)}) collective-permute-start(bf16[4,10,16,256]{3,2,1,0:T(8,128)(2,1)S(1)} %ahead.1.refs_7_.refs_0_), channel_id=1, source_target_pairs={{0,16},{16,32},{32,48},{48,0},{64,80},{80,96},{96,112},{112,64},{1... | collective-permute-start | bytes 983048 | tf_op jit(solution)/shard_map/ppermute | solution.py:58
  71.0 12.2 %collective-permute-start.19 = (bf16[4,10,16,256]{3,2,1,0:T(8,128)(2,1)S(1)}, bf16[4,10,16,256]{3,2,1,0:T(8,128)(2,1)S(1)}, u32[]{:S(2)}, u32[]{:S(2)}) collective-permute-start(bf16[4,10,16,256]{3,2,1,0:T(8,128)(2,1)S(1)} %ahead.1.refs_7_.refs_0_), channel_id=1, source_target_pairs={{0,48},{16,0},{32,16},{48,32},{64,112},{80,64},{96,80},{112,96},{1... | collective-permute-start | bytes 983048 | tf_op jit(solution)/shard_map/ppermute | solution.py:58
  79.5 5.0 %collective-permute-start.16 = (f32[8,256]{1,0:T(8,128)S(1)}, f32[8,256]{1,0:T(8,128)S(1)}, u32[]{:S(2)}, u32[]{:S(2)}) collective-permute-start(f32[8,256]{1,0:T(8,128)S(1)} %style.7.one), channel_id=1, source_target_pairs={{0,1},{1,0},{2,3},{3,2},{4,5},{5,4},{6,7},{7,6},{8,9},{9,8},{10,11... | collective-permute-start | bytes 24584 | tf_op jit(solution)/shard_map/ppermute | solution.py:38

commit v8 on v7

--- a/solution.py
+++ b/solution.py
@@ -463,7 +463,7 @@
     )(style_row, final, final_c, final_z, final_cz)
     finals = [kernels] + two_first(shift_x, kernels, kernels, kernels)
 
-    over_l = [flip_l(message, k) for k in range(1, NL)]
+    over_l = [flip_l(message, k) for k in (1, 3, 2)]
     ahead = call(ahead_body, shape((NL,) + message_of, BF16), [VMEM] * NL, name="ahead")(message, *over_l)
     over_y = two_first(shift_y, ahead, ahead, ahead)
 

time: 85.3 us -> 85.9 us (level)
  starting transfers between devices: 38.7 us -> 40.1 us
    ppermute x3, waiting for transfers between devices: 6.51 us -> 5.03 us  [flip_l(): return lax.ppermute(a, 'img', img_perm(lambda l, y: (l ^ k, y)))]
    ppermute x3, starting transfers between devices: 4.17 us -> 5.63 us  [flip_l(): return lax.ppermute(a, 'img', img_perm(lambda l, y: (l ^ k, y)))]
  transfers between devices with their start and end apart: 20 -> 20, of which waited for: 10 -> 11; matrix products, arithmetic and copies ran while one was open for 0% -> 0% of each run, Pallas kernels for 17% -> 17%
where the time goes in v8:
time: 85.9 us; the launch traced here: 85.7 us
  starting transfers between devices  40.1 us (47%)
  waiting for transfers between devices  23 us (27%)
  Pallas kernels  20.1 us (23%)
  local copies, waits for them, and re-layouts  1.61 us (2%)
    ppermute x2, starting transfers between devices, swap_z(): return lax.ppermute(a, 'tile', tile_perm(lambda x, z, c: (x, 1 - z, c)))  14.7 us
    ppermute x6, starting transfers between devices, shift_x(): lax.ppermute(a, 'tile', tile_perm(lambda x, z, c: ((x + k) % NX, z, c)))  11.7 us
    ppermute x2, waiting for transfers between devices, swap_z(): return lax.ppermute(a, 'tile', tile_perm(lambda x, z, c: (x, 1 - z, c)))  7.79 us
    pallas_call x1, Pallas kernels, local(): call(input_body, (shape((rows, width, channels), BF16), shape((8, 128), F...  6.47 us
    pallas_call x1, Pallas kernels, local(): call(grad_body, (shape((taps, NC, groups, 16, channels), F32), shape((2,...  6.12 us
    ppermute x3, starting transfers between devices, flip_l(): return lax.ppermute(a, 'img', img_perm(lambda l, y: (l ^ k, y)))  5.63 us
    ppermute x3, waiting for transfers between devices, flip_l(): return lax.ppermute(a, 'img', img_perm(lambda l, y: (l ^ k, y)))  5.03 us
    ppermute x3, starting transfers between devices, shift_y(): return lax.ppermute(a, 'img', img_perm(lambda l, y: (l, (y + k) % NY)))  4.4 us
  transfers between devices with their start and end apart: 20, of which 11 were waited for; matrix products, arithmetic and copies ran while one was open for 0% of the time, Pallas kernels for 17%

profile of v8, /device:TPU:8, one launch (start us, length us, event | category | flops | bytes accessed | tf_op | source)
XLA Modules:
  0.0 85.7 jit_solution(9222446505813172368)
XLA Ops:
  0.7 1.7 %rows.1 = (bf16[256,256]{1,0:T(8,128)(2,1)}, bf16[256,256]{1,0:T(8,128)(2,1)}) custom-call(bf16[16,256,256]{2,1,0:T(8,128)(2,1)} %bitcast.8), custom_call_target="tpu_custom_call" | custom-call | bytes 1000000 | tf_op jit(solution)/shard_map/rows/pallas_call | solution.py:387
  2.4 1.7 %collective-permute-start = (bf16[256,256]{1,0:T(8,128)(2,1)}, bf16[256,256]{1,0:T(8,128)(2,1)S(1)}, u32[]{:S(2)}, u32[]{:S(2)}) collective-permute-start(bf16[256,256]{1,0:T(8,128)(2,1)} %get-tuple-element.26), channel_id=1, source_target_pairs={{0,1},{1,2},{2,3},{3,4},{4,5},{5,6},{6,7},{7,8},{8,9},{9,10},{10,1... | collective-permute-start | bytes 393224 | tf_op jit(solution)/shard_map/ppermute | solution.py:397
  4.2 1.3 %collective-permute-start.1 = (bf16[256,256]{1,0:T(8,128)(2,1)}, bf16[256,256]{1,0:T(8,128)(2,1)S(1)}, u32[]{:S(2)}, u32[]{:S(2)}) collective-permute-start(bf16[256,256]{1,0:T(8,128)(2,1)} %get-tuple-element.27), channel_id=1, source_target_pairs={{1,0},{2,1},{3,2},{4,3},{5,4},{6,5},{7,6},{8,7},{9,8},{10,9},{11,1... | collective-permute-start | bytes 393224 | tf_op jit(solution)/shard_map/ppermute | solution.py:398
  5.5 0.8 mix.1
  6.3 13.7 %collective-permute-start.2 = (bf16[9,16,256]{2,1,0:T(8,128)(2,1)S(1)}, bf16[9,16,256]{2,1,0:T(8,128)(2,1)S(1)}, u32[]{:S(2)}, u32[]{:S(2)}) collective-permute-start(bf16[9,16,256]{2,1,0:T(8,128)(2,1)S(1)} %get-tuple-element.28.near.refs_0_), channel_id=1, source_target_pairs={{0,2},{1,3},{2,0},{3,1},{4,6},{5,7},{6,4},{7,5},{8,10},{9,11},{10,... | collective-permute-start | bytes 221192 | tf_op jit(solution)/shard_map/ppermute | solution.py:42
  20.0 1.6 %copy-done.3 = bf16[1,16,256,256]{3,2,1,0:T(8,128)(2,1)S(1)} copy-done((bf16[1,16,256,256]{3,2,1,0:T(8,128)(2,1)S(1)}, bf16[1,16,256,256]{3,2,1,0:T(8,128)(2,1)}, u32[]{:S(2)}) %copy-start.3) | copy-done | bytes 2097176
  21.6 6.1 %grad.1 = (f32[9,2,8,16,256]{4,3,2,1,0:T(8,128)S(1)}, bf16[2,256,256]{2,1,0:T(8,128)(2,1)S(1)}) custom-call(s32[3]{0:T(128)S(1)} %pad_add_fusion.place, bf16[16,256,256]{2,1,0:T(8,128)(2,1)S(1)} %bitcast.9, bf16[16,256,256]{2,1,0:T(8,128)(2,1)S(1)} %bitcast.11), custom_call_target="tpu_custom_call" | custom-call | flops 4831838208 | bytes 4194304 | tf_op jit(solution)/shard_map/grad/pallas_call | solution.py:407
  27.8 1.0 %edge.1 = (f32[8,9,16,256]{3,2,1,0:T(8,128)S(1)}, bf16[8,9,16,256]{3,2,1,0:T(8,128)(2,1)S(1)}) custom-call(s32[3]{0:T(128)S(1)} %pad_add_fusion.place, f32[9,2,8,16,256]{4,3,2,1,0:T(8,128)S(1)} %get-tuple-element.24.grad, bf16[2,256,256]{2,1,0:T(8,128)(2,1)S(1)} %get-tuple-element.25.ends, bf16[256,256]{1,0:T(8,128)(2,1)S(1)} %collective-permute-done.low.refs_4_, ...), custom_call_target="tpu_custom_call" | custom-call | flops 201326592 | bytes 4000000 | tf_op jit(solution)/shard_map/edge/pallas_call | solution.py:420
  28.9 2.0 %collective-permute-done.3.got = bf16[8,9,16,256]{3,2,1,0:T(8,128)(2,1)S(1)} collective-permute-done((bf16[8,9,16,256]{3,2,1,0:T(8,128)(2,1)S(1)}, bf16[8,9,16,256]{3,2,1,0:T(8,128)(2,1)S(1)}, u32[]{:S(2)}, u32[]{:S(2)}) %collective-permute-start.3) | collective-permute-done | bytes 589856 | tf_op jit(solution)/shard_map/ppermute | solution.py:38
  30.9 0.6 split_x.1
  31.5 3.1 %collective-permute-start.4 = (bf16[2,9,16,256]{3,2,1,0:T(8,128)(2,1)S(1)}, bf16[2,9,16,256]{3,2,1,0:T(8,128)(2,1)S(1)}, u32[]{:S(2)}, u32[]{:S(2)}) collective-permute-start(bf16[2,9,16,256]{3,2,1,0:T(8,128)(2,1)S(1)} %get-tuple-element.32), channel_id=1, source_target_pairs={{0,8},{1,9},{2,10},{3,11},{4,12},{5,13},{6,14},{7,15},{8,0},{9,1},... | collective-permute-start | bytes 442376 | tf_op jit(solution)/shard_map/ppermute | solution.py:46
  35.2 2.6 %collective-permute-start.6 = (bf16[2,9,16,256]{3,2,1,0:T(8,128)(2,1)S(1)}, bf16[2,9,16,256]{3,2,1,0:T(8,128)(2,1)S(1)}, u32[]{:S(2)}, u32[]{:S(2)}) collective-permute-start(bf16[2,9,16,256]{3,2,1,0:T(8,128)(2,1)S(1)} %get-tuple-element.34), channel_id=1, source_target_pairs={{0,12},{1,13},{2,14},{3,15},{4,0},{5,1},{6,2},{7,3},{8,4},{9,5},{1... | collective-permute-start | bytes 442376 | tf_op jit(solution)/shard_map/ppermute | solution.py:46
  38.4 0.8 collective-permute-done.7.after.refs_1_
  39.8 2.4 %collective-permute-done.5.one = bf16[2,9,16,256]{3,2,1,0:T(8,128)(2,1)S(1)} collective-permute-done((bf16[2,9,16,256]{3,2,1,0:T(8,128)(2,1)S(1)}, bf16[2,9,16,256]{3,2,1,0:T(8,128)(2,1)S(1)}, u32[]{:S(2)}, u32[]{:S(2)}) %collective-permute-start.5) | collective-permute-done | bytes 147488 | tf_op jit(solution)/shard_map/ppermute | solution.py:46
  42.3 0.7 split_z.1
  43.0 1.0 %collective-permute-start.9 = (bf16[10,16,256]{2,1,0:T(8,128)(2,1)S(1)}, bf16[10,16,256]{2,1,0:T(8,128)(2,1)S(1)}, u32[]{:S(2)}, u32[]{:S(2)}) collective-permute-start(bf16[10,16,256]{2,1,0:T(8,128)(2,1)S(1)} %get-tuple-element.36.sent), channel_id=1, source_target_pairs={{0,2},{1,3},{2,0},{3,1},{4,6},{5,7},{6,4},{7,5},{8,10},{9,11},{10,... | collective-permute-start | bytes 245768 | tf_op jit(solution)/shard_map/ppermute | solution.py:42
  44.0 7.8 %collective-permute-done.9.got = bf16[10,16,256]{2,1,0:T(8,128)(2,1)S(1)} collective-permute-done((bf16[10,16,256]{2,1,0:T(8,128)(2,1)S(1)}, bf16[10,16,256]{2,1,0:T(8,128)(2,1)S(1)}, u32[]{:S(2)}, u32[]{:S(2)}) %collective-permute-start.9) | collective-permute-done | bytes 81952 | tf_op jit(solution)/shard_map/ppermute | solution.py:42
  51.8 0.7 owner.1
  52.5 2.1 %collective-permute-start.10 = (bf16[37,16,256]{2,1,0:T(8,128)(2,1)S(1)}, bf16[37,16,256]{2,1,0:T(8,128)(2,1)S(1)}, u32[]{:S(2)}, u32[]{:S(2)}) collective-permute-start(bf16[37,16,256]{2,1,0:T(8,128)(2,1)S(1)} %kernels.1.refs_0_), channel_id=1, source_target_pairs={{0,8},{1,9},{2,10},{3,11},{4,12},{5,13},{6,14},{7,15},{8,0},{9,1},... | collective-permute-start | bytes 909320 | tf_op jit(solution)/shard_map/ppermute | solution.py:46
  54.6 1.6 %collective-permute-start.11 = (bf16[37,16,256]{2,1,0:T(8,128)(2,1)S(1)}, bf16[37,16,256]{2,1,0:T(8,128)(2,1)S(1)}, u32[]{:S(2)}, u32[]{:S(2)}) collective-permute-start(bf16[37,16,256]{2,1,0:T(8,128)(2,1)S(1)} %kernels.1.refs_0_), channel_id=1, source_target_pairs={{0,4},{1,5},{2,6},{3,7},{4,8},{5,9},{6,10},{7,11},{8,12},{9,13},{1... | collective-permute-start | bytes 909320 | tf_op jit(solution)/shard_map/ppermute | solution.py:46
  56.2 1.6 %collective-permute-start.12 = (bf16[37,16,256]{2,1,0:T(8,128)(2,1)S(1)}, bf16[37,16,256]{2,1,0:T(8,128)(2,1)S(1)}, u32[]{:S(2)}, u32[]{:S(2)}) collective-permute-start(bf16[37,16,256]{2,1,0:T(8,128)(2,1)S(1)} %kernels.1.refs_0_), channel_id=1, source_target_pairs={{0,12},{1,13},{2,14},{3,15},{4,0},{5,1},{6,2},{7,3},{8,4},{9,5},{1... | collective-permute-start | bytes 909320 | tf_op jit(solution)/shard_map/ppermute | solution.py:46
  57.9 0.9 %collective-permute-start.13 = (bf16[10,16,256]{2,1,0:T(8,128)(2,1)S(1)}, bf16[10,16,256]{2,1,0:T(8,128)(2,1)S(1)}, u32[]{:S(2)}, u32[]{:S(2)}) collective-permute-start(bf16[10,16,256]{2,1,0:T(8,128)(2,1)S(1)} %get-tuple-element.38.refs_0_), channel_id=1, source_target_pairs={{0,64},{16,80},{32,96},{48,112},{64,0},{80,16},{96,32},{112,48},{1... | collective-permute-start | bytes 245768 | tf_op jit(solution)/shard_map/ppermute | solution.py:54
  58.8 2.3 %collective-permute-start.14 = (bf16[10,16,256]{2,1,0:T(8,128)(2,1)S(1)}, bf16[10,16,256]{2,1,0:T(8,128)(2,1)S(1)}, u32[]{:S(2)}, u32[]{:S(2)}) collective-permute-start(bf16[10,16,256]{2,1,0:T(8,128)(2,1)S(1)} %get-tuple-element.38.refs_0_), channel_id=1, source_target_pairs={{0,192},{16,208},{32,224},{48,240},{64,128},{80,144},{96,160},{112... | collective-permute-start | bytes 245768 | tf_op jit(solution)/shard_map/ppermute | solution.py:54
  61.1 1.2 %collective-permute-done.13.refs_1_ = bf16[10,16,256]{2,1,0:T(8,128)(2,1)S(1)} collective-permute-done((bf16[10,16,256]{2,1,0:T(8,128)(2,1)S(1)}, bf16[10,16,256]{2,1,0:T(8,128)(2,1)S(1)}, u32[]{:S(2)}, u32[]{:S(2)}) %collective-permute-start.13) | collective-permute-done | bytes 81952 | tf_op jit(solution)/shard_map/ppermute | solution.py:54
  62.3 2.4 %collective-permute-start.15 = (bf16[10,16,256]{2,1,0:T(8,128)(2,1)S(1)}, bf16[10,16,256]{2,1,0:T(8,128)(2,1)S(1)}, u32[]{:S(2)}, u32[]{:S(2)}) collective-permute-start(bf16[10,16,256]{2,1,0:T(8,128)(2,1)S(1)} %get-tuple-element.38.refs_0_), channel_id=1, source_target_pairs={{0,128},{16,144},{32,160},{48,176},{64,192},{80,208},{96,224},{112... | collective-permute-start | bytes 245768 | tf_op jit(solution)/shard_map/ppermute | solution.py:54
  65.3 3.2 %collective-permute-done.15.refs_3_ = bf16[10,16,256]{2,1,0:T(8,128)(2,1)S(1)} collective-permute-done((bf16[10,16,256]{2,1,0:T(8,128)(2,1)S(1)}, bf16[10,16,256]{2,1,0:T(8,128)(2,1)S(1)}, u32[]{:S(2)}, u32[]{:S(2)}) %collective-permute-start.15) | collective-permute-done | bytes 81952 | tf_op jit(solution)/shard_map/ppermute | solution.py:54
  68.5 2.4 %collective-permute-start.17 = (bf16[4,10,16,256]{3,2,1,0:T(8,128)(2,1)S(1)}, bf16[4,10,16,256]{3,2,1,0:T(8,128)(2,1)S(1)}, u32[]{:S(2)}, u32[]{:S(2)}) collective-permute-start(bf16[4,10,16,256]{3,2,1,0:T(8,128)(2,1)S(1)} %ahead.1.refs_7_.refs_0_), channel_id=1, source_target_pairs={{0,32},{16,48},{32,0},{48,16},{64,96},{80,112},{96,64},{112,80},{1... | collective-permute-start | bytes 983048 | tf_op jit(solution)/shard_map/ppermute | solution.py:58
  70.9 2.0 %collective-permute-start.19 = (bf16[4,10,16,256]{3,2,1,0:T(8,128)(2,1)S(1)}, bf16[4,10,16,256]{3,2,1,0:T(8,128)(2,1)S(1)}, u32[]{:S(2)}, u32[]{:S(2)}) collective-permute-start(bf16[4,10,16,256]{3,2,1,0:T(8,128)(2,1)S(1)} %ahead.1.refs_7_.refs_0_), channel_id=1, source_target_pairs={{0,48},{16,0},{32,16},{48,32},{64,112},{80,64},{96,80},{112,96},{1... | collective-permute-start | bytes 983048 | tf_op jit(solution)/shard_map/ppermute | solution.py:58
  73.0 6.5 %input.1 = (bf16[16,256,256]{2,1,0:T(8,128)(2,1)}, f32[8,128]{1,0:T(8,128)S(1)}) custom-call(s32[3]{0:T(128)S(1)} %pad_add_fusion.place, bf16[37,16,256]{2,1,0:T(8,128)(2,1)S(1)} %kernels.1.refs_0_, bf16[37,16,256]{2,1,0:T(8,128)(2,1)S(1)} %collective-permute-done.10.refs_1_, bf16[37,16,256]{2,1,0:T(8,128)(2,1)S(1)} %collective-permute-done.11.refs_2_, ...), custom_call_target="tpu_custom_call" | custom-call | flops 4831838208 | bytes 4194304 | tf_op jit(solution)/shard_map/input/pallas_call | solution.py:470
  79.6 0.8 collective-permute-done.17.refs_1_
  80.3 3.5 %collective-permute-done.18.refs_2_ = bf16[4,10,16,256]{3,2,1,0:T(8,128)(2,1)S(1)} collective-permute-done((bf16[4,10,16,256]{3,2,1,0:T(8,128)(2,1)S(1)}, bf16[4,10,16,256]{3,2,1,0:T(8,128)(2,1)S(1)}, u32[]{:S(2)}, u32[]{:S(2)}) %collective-permute-start.18) | collective-permute-done | bytes 327712 | tf_op jit(solution)/shard_map/ppermute | solution.py:58
  83.8 1.3 %banks.1 = (f32[8,9,16,256]{3,2,1,0:T(8,128)}, f32[8,128]{1,0:T(8,128)S(1)}) custom-call(bf16[4,10,16,256]{3,2,1,0:T(8,128)(2,1)S(1)} %ahead.1.refs_7_.refs_0_, bf16[4,10,16,256]{3,2,1,0:T(8,128)(2,1)S(1)} %collective-permute-done.17.refs_1_, bf16[4,10,16,256]{3,2,1,0:T(8,128)(2,1)S(1)} %collective-permute-done.18.refs_2_, ...), custom_call_target="tpu_custom_call" | custom-call | flops 10000000 | bytes 3000000 | tf_op jit(solution)/shard_map/banks/pallas_call | solution.py:487
  (32 shorter events, 3.3 us)
Async XLA Ops:
  0.6 4.8 %copy-start.2 = (s32[1,3]{1,0:T(1,128)S(1)}, s32[1,3]{1,0:T(1,128)}, u32[]{:S(2)}) copy-start(s32[1,3]{1,0:T(1,128)} %sel.3) | copy-start | bytes 40
  0.6 4.8 %copy-start.1 = (f32[1,256]{1,0:T(1,128)S(1)}, f32[1,256]{1,0:T(1,128)}, u32[]{:S(2)}) copy-start(f32[1,256]{1,0:T(1,128)} %style.6) | copy-start | bytes 3076
  0.7 4.8 %copy-start.4 = (bf16[8,16,9,256]{3,1,2,0:T(8,128)(2,1)S(1)}, bf16[8,16,9,256]{3,1,2,0:T(8,128)(2,1)}, u32[]{:S(2)}) copy-start(bf16[8,16,9,256]{3,1,2,0:T(8,128)(2,1)} %param.8) | copy-start | bytes 1769476
  2.4 25.4 %collective-permute-start = (bf16[256,256]{1,0:T(8,128)(2,1)}, bf16[256,256]{1,0:T(8,128)(2,1)S(1)}, u32[]{:S(2)}, u32[]{:S(2)}) collective-permute-start(bf16[256,256]{1,0:T(8,128)(2,1)} %get-tuple-element.26), channel_id=1, source_target_pairs={{0,1},{1,2},{2,3},{3,4},{4,5},{5,6},{6,7},{7,8},{8,9},{9,10},{10,1... | collective-permute-start | bytes 393224 | tf_op jit(solution)/shard_map/ppermute | solution.py:397
  4.2 23.6 %collective-permute-start.1 = (bf16[256,256]{1,0:T(8,128)(2,1)}, bf16[256,256]{1,0:T(8,128)(2,1)S(1)}, u32[]{:S(2)}, u32[]{:S(2)}) collective-permute-start(bf16[256,256]{1,0:T(8,128)(2,1)} %get-tuple-element.27), channel_id=1, source_target_pairs={{1,0},{2,1},{3,2},{4,3},{5,4},{6,5},{7,6},{8,7},{9,8},{10,9},{11,1... | collective-permute-start | bytes 393224 | tf_op jit(solution)/shard_map/ppermute | solution.py:398
  5.5 14.5 %copy-start = (bf16[1,16,256,256]{3,2,1,0:T(8,128)(2,1)S(1)}, bf16[1,16,256,256]{3,2,1,0:T(8,128)(2,1)}, u32[]{:S(2)}) copy-start(bf16[1,16,256,256]{3,2,1,0:T(8,128)(2,1)} %param.6) | copy-start | bytes 6291460
  6.3 21.5 %collective-permute-start.2 = (bf16[9,16,256]{2,1,0:T(8,128)(2,1)S(1)}, bf16[9,16,256]{2,1,0:T(8,128)(2,1)S(1)}, u32[]{:S(2)}, u32[]{:S(2)}) collective-permute-start(bf16[9,16,256]{2,1,0:T(8,128)(2,1)S(1)} %get-tuple-element.28.near.refs_0_), channel_id=1, source_target_pairs={{0,2},{1,3},{2,0},{3,1},{4,6},{5,7},{6,4},{7,5},{8,10},{9,11},{10,... | collective-permute-start | bytes 221192 | tf_op jit(solution)/shard_map/ppermute | solution.py:42
  20.0 1.6 %copy-start.3 = (bf16[1,16,256,256]{3,2,1,0:T(8,128)(2,1)S(1)}, bf16[1,16,256,256]{3,2,1,0:T(8,128)(2,1)}, u32[]{:S(2)}) copy-start(bf16[1,16,256,256]{3,2,1,0:T(8,128)(2,1)} %param.5) | copy-start | bytes 6291460
  28.8 2.1 %collective-permute-start.3 = (bf16[8,9,16,256]{3,2,1,0:T(8,128)(2,1)S(1)}, bf16[8,9,16,256]{3,2,1,0:T(8,128)(2,1)S(1)}, u32[]{:S(2)}, u32[]{:S(2)}) collective-permute-start(bf16[8,9,16,256]{3,2,1,0:T(8,128)(2,1)S(1)} %get-tuple-element.30), channel_id=1, source_target_pairs={{0,1},{1,0},{2,3},{3,2},{4,5},{5,4},{6,7},{7,6},{8,9},{9,8},{10,11... | collective-permute-start | bytes 1769480 | tf_op jit(solution)/shard_map/ppermute | solution.py:38
  31.5 8.3 %collective-permute-start.4 = (bf16[2,9,16,256]{3,2,1,0:T(8,128)(2,1)S(1)}, bf16[2,9,16,256]{3,2,1,0:T(8,128)(2,1)S(1)}, u32[]{:S(2)}, u32[]{:S(2)}) collective-permute-start(bf16[2,9,16,256]{3,2,1,0:T(8,128)(2,1)S(1)} %get-tuple-element.32), channel_id=1, source_target_pairs={{0,8},{1,9},{2,10},{3,11},{4,12},{5,13},{6,14},{7,15},{8,0},{9,1},... | collective-permute-start | bytes 442376 | tf_op jit(solution)/shard_map/ppermute | solution.py:46
  34.7 7.6 %collective-permute-start.5 = (bf16[2,9,16,256]{3,2,1,0:T(8,128)(2,1)S(1)}, bf16[2,9,16,256]{3,2,1,0:T(8,128)(2,1)S(1)}, u32[]{:S(2)}, u32[]{:S(2)}) collective-permute-start(bf16[2,9,16,256]{3,2,1,0:T(8,128)(2,1)S(1)} %get-tuple-element.33), channel_id=1, source_target_pairs={{0,4},{1,5},{2,6},{3,7},{4,8},{5,9},{6,10},{7,11},{8,12},{9,13},{1... | collective-permute-start | bytes 442376 | tf_op jit(solution)/shard_map/ppermute | solution.py:46
  35.2 7.0 %collective-permute-start.6 = (bf16[2,9,16,256]{3,2,1,0:T(8,128)(2,1)S(1)}, bf16[2,9,16,256]{3,2,1,0:T(8,128)(2,1)S(1)}, u32[]{:S(2)}, u32[]{:S(2)}) collective-permute-start(bf16[2,9,16,256]{3,2,1,0:T(8,128)(2,1)S(1)} %get-tuple-element.34), channel_id=1, source_target_pairs={{0,12},{1,13},{2,14},{3,15},{4,0},{5,1},{6,2},{7,3},{8,4},{9,5},{1... | collective-permute-start | bytes 442376 | tf_op jit(solution)/shard_map/ppermute | solution.py:46
  37.9 1.3 %collective-permute-start.7 = (bf16[9,16,256]{2,1,0:T(8,128)(2,1)S(1)}, bf16[9,16,256]{2,1,0:T(8,128)(2,1)S(1)}, u32[]{:S(2)}, u32[]{:S(2)}) collective-permute-start(bf16[9,16,256]{2,1,0:T(8,128)(2,1)S(1)} %get-tuple-element.28.near.refs_0_), channel_id=1, source_target_pairs={{0,1},{1,0},{2,3},{3,2},{4,5},{5,4},{6,7},{7,6},{8,9},{9,8},{10,11... | collective-permute-start | bytes 221192 | tf_op jit(solution)/shard_map/ppermute | solution.py:38
  37.9 1.4 %collective-permute-start.8 = (bf16[9,16,256]{2,1,0:T(8,128)(2,1)S(1)}, bf16[9,16,256]{2,1,0:T(8,128)(2,1)S(1)}, u32[]{:S(2)}, u32[]{:S(2)}) collective-permute-start(bf16[9,16,256]{2,1,0:T(8,128)(2,1)S(1)} %collective-permute-done.2.after.got.refs_2_), channel_id=1, source_target_pairs={{0,1},{1,0},{2,3},{3,2},{4,5},{5,4},{6,7},{7,6},{8,9},{9,8},{10,11... | collective-permute-start | bytes 221192 | tf_op jit(solution)/shard_map/ppermute | solution.py:38
  43.0 8.8 %collective-permute-start.9 = (bf16[10,16,256]{2,1,0:T(8,128)(2,1)S(1)}, bf16[10,16,256]{2,1,0:T(8,128)(2,1)S(1)}, u32[]{:S(2)}, u32[]{:S(2)}) collective-permute-start(bf16[10,16,256]{2,1,0:T(8,128)(2,1)S(1)} %get-tuple-element.36.sent), channel_id=1, source_target_pairs={{0,2},{1,3},{2,0},{3,1},{4,6},{5,7},{6,4},{7,5},{8,10},{9,11},{10,... | collective-permute-start | bytes 245768 | tf_op jit(solution)/shard_map/ppermute | solution.py:42
  52.5 18.4 %collective-permute-start.10 = (bf16[37,16,256]{2,1,0:T(8,128)(2,1)S(1)}, bf16[37,16,256]{2,1,0:T(8,128)(2,1)S(1)}, u32[]{:S(2)}, u32[]{:S(2)}) collective-permute-start(bf16[37,16,256]{2,1,0:T(8,128)(2,1)S(1)} %kernels.1.refs_0_), channel_id=1, source_target_pairs={{0,8},{1,9},{2,10},{3,11},{4,12},{5,13},{6,14},{7,15},{8,0},{9,1},... | collective-permute-start | bytes 909320 | tf_op jit(solution)/shard_map/ppermute | solution.py:46
  54.6 18.3 %collective-permute-start.11 = (bf16[37,16,256]{2,1,0:T(8,128)(2,1)S(1)}, bf16[37,16,256]{2,1,0:T(8,128)(2,1)S(1)}, u32[]{:S(2)}, u32[]{:S(2)}) collective-permute-start(bf16[37,16,256]{2,1,0:T(8,128)(2,1)S(1)} %kernels.1.refs_0_), channel_id=1, source_target_pairs={{0,4},{1,5},{2,6},{3,7},{4,8},{5,9},{6,10},{7,11},{8,12},{9,13},{1... | collective-permute-start | bytes 909320 | tf_op jit(solution)/shard_map/ppermute | solution.py:46
  56.2 16.7 %collective-permute-start.12 = (bf16[37,16,256]{2,1,0:T(8,128)(2,1)S(1)}, bf16[37,16,256]{2,1,0:T(8,128)(2,1)S(1)}, u32[]{:S(2)}, u32[]{:S(2)}) collective-permute-start(bf16[37,16,256]{2,1,0:T(8,128)(2,1)S(1)} %kernels.1.refs_0_), channel_id=1, source_target_pairs={{0,12},{1,13},{2,14},{3,15},{4,0},{5,1},{6,2},{7,3},{8,4},{9,5},{1... | collective-permute-start | bytes 909320 | tf_op jit(solution)/shard_map/ppermute | solution.py:46
  57.9 4.4 %collective-permute-start.13 = (bf16[10,16,256]{2,1,0:T(8,128)(2,1)S(1)}, bf16[10,16,256]{2,1,0:T(8,128)(2,1)S(1)}, u32[]{:S(2)}, u32[]{:S(2)}) collective-permute-start(bf16[10,16,256]{2,1,0:T(8,128)(2,1)S(1)} %get-tuple-element.38.refs_0_), channel_id=1, source_target_pairs={{0,64},{16,80},{32,96},{48,112},{64,0},{80,16},{96,32},{112,48},{1... | collective-permute-start | bytes 245768 | tf_op jit(solution)/shard_map/ppermute | solution.py:54
  58.8 6.5 %collective-permute-start.14 = (bf16[10,16,256]{2,1,0:T(8,128)(2,1)S(1)}, bf16[10,16,256]{2,1,0:T(8,128)(2,1)S(1)}, u32[]{:S(2)}, u32[]{:S(2)}) collective-permute-start(bf16[10,16,256]{2,1,0:T(8,128)(2,1)S(1)} %get-tuple-element.38.refs_0_), channel_id=1, source_target_pairs={{0,192},{16,208},{32,224},{48,240},{64,128},{80,144},{96,160},{112... | collective-permute-start | bytes 245768 | tf_op jit(solution)/shard_map/ppermute | solution.py:54
  62.3 6.2 %collective-permute-start.15 = (bf16[10,16,256]{2,1,0:T(8,128)(2,1)S(1)}, bf16[10,16,256]{2,1,0:T(8,128)(2,1)S(1)}, u32[]{:S(2)}, u32[]{:S(2)}) collective-permute-start(bf16[10,16,256]{2,1,0:T(8,128)(2,1)S(1)} %get-tuple-element.38.refs_0_), channel_id=1, source_target_pairs={{0,128},{16,144},{32,160},{48,176},{64,192},{80,208},{96,224},{112... | collective-permute-start | bytes 245768 | tf_op jit(solution)/shard_map/ppermute | solution.py:54
  68.5 11.8 %collective-permute-start.17 = (bf16[4,10,16,256]{3,2,1,0:T(8,128)(2,1)S(1)}, bf16[4,10,16,256]{3,2,1,0:T(8,128)(2,1)S(1)}, u32[]{:S(2)}, u32[]{:S(2)}) collective-permute-start(bf16[4,10,16,256]{3,2,1,0:T(8,128)(2,1)S(1)} %ahead.1.refs_7_.refs_0_), channel_id=1, source_target_pairs={{0,32},{16,48},{32,0},{48,16},{64,96},{80,112},{96,64},{112,80},{1... | collective-permute-start | bytes 983048 | tf_op jit(solution)/shard_map/ppermute | solution.py:58
  70.9 12.9 %collective-permute-start.18 = (bf16[4,10,16,256]{3,2,1,0:T(8,128)(2,1)S(1)}, bf16[4,10,16,256]{3,2,1,0:T(8,128)(2,1)S(1)}, u32[]{:S(2)}, u32[]{:S(2)}) collective-permute-start(bf16[4,10,16,256]{3,2,1,0:T(8,128)(2,1)S(1)} %ahead.1.refs_7_.refs_0_), channel_id=1, source_target_pairs={{0,16},{16,32},{32,48},{48,0},{64,80},{80,96},{96,112},{112,64},{1... | collective-permute-start | bytes 983048 | tf_op jit(solution)/shard_map/ppermute | solution.py:58
  70.9 12.9 %collective-permute-start.19 = (bf16[4,10,16,256]{3,2,1,0:T(8,128)(2,1)S(1)}, bf16[4,10,16,256]{3,2,1,0:T(8,128)(2,1)S(1)}, u32[]{:S(2)}, u32[]{:S(2)}) collective-permute-start(bf16[4,10,16,256]{3,2,1,0:T(8,128)(2,1)S(1)} %ahead.1.refs_7_.refs_0_), channel_id=1, source_target_pairs={{0,48},{16,0},{32,16},{48,32},{64,112},{80,64},{96,80},{112,96},{1... | collective-permute-start | bytes 983048 | tf_op jit(solution)/shard_map/ppermute | solution.py:58
  79.5 5.7 %collective-permute-start.16 = (f32[8,256]{1,0:T(8,128)S(1)}, f32[8,256]{1,0:T(8,128)S(1)}, u32[]{:S(2)}, u32[]{:S(2)}) collective-permute-start(f32[8,256]{1,0:T(8,128)S(1)} %style.7.one), channel_id=1, source_target_pairs={{0,1},{1,0},{2,3},{3,2},{4,5},{5,4},{6,7},{7,6},{8,9},{9,8},{10,11... | collective-permute-start | bytes 24584 | tf_op jit(solution)/shard_map/ppermute | solution.py:38
